TPU v7x, 32 devices: a whole 2x2x4 slice. The times are simulated.
32 devices in a mesh: groups: 2 (over x), row: 8 (over z, y), col: 2 (over core).
Axes of the slice: x: 2, y: 2, z: 4, core: 2. Of those that a mesh axis runs over, the one named last changes fastest.
Arguments:
- queries: bfloat16 [16384, 512], P(('groups', 'row'), 'col'), parts along dimension 0, may hold values from -6 to 6
- keys: bfloat16 [16384, 512], P(('groups', 'row'), 'col'), parts along dimension 0, may hold values from -6 to 6
- values: bfloat16 [16384, 512], P(('groups', 'row'), 'col'), parts along dimension 0, may hold values from -6 to 6
- attended: bfloat16 [16384, 512], P(('groups', 'row'), 'col'), parts along dimension 0, may hold values from -6 to 6
- grad_out: bfloat16 [16384, 512], P(('groups', 'row'), 'col'), parts along dimension 0, may hold values from -2 to 2
- log_norms: bfloat16 [16384, 8], P(('groups', 'row'), 'col'), parts along dimension 0, may hold values from 2 to 4
- block_slot: int32 [64], P('groups'), parts along dimension 0, may hold values from 0 to 31, as said below
- neighbours: int32 [64, 8], P('groups'), parts along dimension 0, may hold values from 0 to 31, as said below
- live_count: int32 [64], P('groups'), parts along dimension 0, may hold values from 3 to 8
Outputs:
- query_grad: bfloat16 [16384, 512], P(('groups', 'row'), 'col'), parts along dimension 0
- key_grad: bfloat16 [16384, 512], P(('groups', 'row'), 'col'), parts along dimension 0
- value_grad: bfloat16 [16384, 512], P(('groups', 'row'), 'col'), parts along dimension 0
There are 2 independent parts, one for each index of `groups`. A program takes and returns all parts, laid end to end along the dimension named above; each array names one. Nothing has to cross between parts.
Inputs may be any that keep to these rules, and one draw needn't show every extreme that they name: `block_slot`: a permutation: every slot holds exactly one block. `neighbours`: over the 32 list entries of the blocks held by one row index, at most 4 name blocks held by any one row index, and for every row index some row index is named by exactly 4 of them; entries at or beyond live_count carry no weight but name blocks too.
All inputs are finite; a program needn't handle non-finite values.
Results may differ from a plain program's by a relative error of at most 0.0093.
Values may be sent and summed in bfloat16 or wider, within the bound.
A program may use at most 128 MiB of HBM per device.

v0:
```python
import jax
import jax.numpy as jnp
from jax import lax
from jax.sharding import PartitionSpec as P

BLOCK = 256
NEIGH = 8


SCALE = 0.125


def entry_terms(query_blk, grad_blk, norm_blk, delta_blk, key_blk, value_blk, weight):
    count, rows, width = query_blk.shape
    heads = norm_blk.shape[2]

    def shaped(array):
        return array.reshape(count, rows, heads, width // heads)

    query_h = shaped(query_blk)
    grad_h = shaped(grad_blk)
    key_h = shaped(key_blk)
    value_h = shaped(value_blk)
    shift = jnp.transpose(norm_blk.astype(jnp.float32), (0, 2, 1))[..., None]
    offset = jnp.transpose(delta_blk.astype(jnp.float32), (0, 2, 1))[..., None]
    scores = (
        jnp.einsum("mqhe,mkhe->mhqk", query_h, key_h, preferred_element_type=jnp.float32) * SCALE
    )
    prob = jnp.exp(scores - shift) * weight[:, None, None, None]
    prob_low = prob.astype(jnp.bfloat16)
    dprob = jnp.einsum("mqhe,mkhe->mhqk", grad_h, value_h, preferred_element_type=jnp.float32)
    dscore = (prob * (dprob - offset)).astype(jnp.bfloat16)
    query_part = (
        jnp.einsum("mhqk,mkhe->mqhe", dscore, key_h, preferred_element_type=jnp.float32) * SCALE
    ).astype(jnp.bfloat16)
    key_part = (
        jnp.einsum("mhqk,mqhe->mkhe", dscore, query_h, preferred_element_type=jnp.float32) * SCALE
    ).astype(jnp.bfloat16)
    value_part = jnp.einsum(
        "mhqk,mqhe->mkhe", prob_low, grad_h, preferred_element_type=jnp.float32
    ).astype(jnp.bfloat16)
    return (
        query_part.reshape(count, rows, width),
        key_part.reshape(count, rows, width),
        value_part.reshape(count, rows, width),
    )


def in_pairs(operands):
    count = operands[0].shape[0]
    paired = tuple((array.reshape((count // 2, 2) + array.shape[1:]) for array in operands))
    results = lax.map(lambda items: entry_terms(*items), paired)
    return tuple((array.reshape((count,) + array.shape[2:]) for array in results))


def entry_tables(block_slot, neighbours, live_count, per_row, n_row):
    blocks = block_slot.shape[0]
    slots = jnp.arange(blocks, dtype=jnp.int32)
    one_hot = (block_slot[None, :] == slots[:, None]).astype(jnp.int32)
    held = jnp.sum(one_hot * slots[None, :], axis=1)
    target = jnp.take(block_slot, jnp.take(neighbours, held, axis=0), axis=0)
    weights = (
        jnp.arange(NEIGH, dtype=jnp.int32)[None, :] < jnp.take(live_count, held)[:, None]
    ).astype(jnp.float32)
    entries = NEIGH * per_row
    target = target.reshape(n_row, entries)
    weights = weights.reshape(n_row, entries)
    target_row = target // per_row
    target_local = target % per_row
    earlier = jnp.tril(jnp.ones((entries, entries), jnp.int32), -1)
    same_row = (target_row[:, :, None] == target_row[:, None, :]).astype(jnp.int32)
    slot_rank = jnp.sum(same_row * earlier[None], axis=2)
    return (target_row, target_local, slot_rank, weights)


def body(queries, keys, values, attended, grad_out, log_norms, block_slot, neighbours, live_count):
    n_row = lax.axis_size("row")
    here = lax.axis_index("row")
    per_row = queries.shape[0] // BLOCK
    width = queries.shape[1]
    heads = log_norms.shape[1]
    entries = NEIGH * per_row
    capacity = (entries + n_row - 1) // n_row
    target_row, target_local, slot_rank, weights = entry_tables(
        block_slot, neighbours, live_count, per_row, n_row
    )

    def as_blocks(array):
        return array.reshape(per_row, BLOCK, array.shape[1])

    delta = jnp.sum(
        (grad_out.astype(jnp.float32) * attended.astype(jnp.float32)).reshape(
            -1, heads, width // heads
        ),
        axis=2,
    ).astype(jnp.bfloat16)
    query_loc = as_blocks(queries)
    key_loc = as_blocks(keys)
    value_loc = as_blocks(values)
    grad_loc = as_blocks(grad_out)
    norm_loc = as_blocks(log_norms)
    delta_loc = as_blocks(delta)
    my_row = jnp.take(target_row, here, axis=0)
    my_rank = jnp.take(slot_rank, here, axis=0)
    my_weight = jnp.take(weights, here, axis=0)
    position = my_row * capacity + my_rank
    owner_of = jnp.arange(entries, dtype=jnp.int32) // NEIGH
    matched = (
        (target_row == here)[:, :, None]
        & (slot_rank[:, :, None] == jnp.arange(capacity, dtype=jnp.int32)[None, None, :])
    ).astype(jnp.int32)
    local_slot = jnp.sum(matched * target_local[:, :, None], axis=1).reshape(-1)
    used = jnp.sum(matched, axis=1).reshape(-1)
    collect = (
        (local_slot[:, None] == jnp.arange(per_row, dtype=jnp.int32)[None, :]) & (used[:, None] > 0)
    ).astype(jnp.bfloat16)
    query_rep = jnp.take(query_loc, owner_of, axis=0)
    grad_rep = jnp.take(grad_loc, owner_of, axis=0)
    norm_rep = jnp.take(norm_loc, owner_of, axis=0)
    delta_rep = jnp.take(delta_loc, owner_of, axis=0)
    send_keys = jnp.take(key_loc, local_slot, axis=0).reshape(n_row, capacity, BLOCK, width)
    send_values = jnp.take(value_loc, local_slot, axis=0).reshape(n_row, capacity, BLOCK, width)
    got_keys, got_values = (
        lax.all_to_all(send_keys, "row", split_axis=0, concat_axis=0, tiled=True),
        lax.all_to_all(send_values, "row", split_axis=0, concat_axis=0, tiled=True),
    )
    entry_keys = jnp.take(got_keys.reshape(n_row * capacity, BLOCK, width), position, axis=0)
    entry_values = jnp.take(got_values.reshape(n_row * capacity, BLOCK, width), position, axis=0)
    query_terms, key_part, value_part = in_pairs(
        (query_rep, grad_rep, norm_rep, delta_rep, entry_keys, entry_values, my_weight)
    )
    empty = jnp.zeros((n_row * capacity, BLOCK, width), jnp.bfloat16)
    key_out = empty.at[position].set(key_part).reshape(n_row, capacity, BLOCK, width)
    value_out = empty.at[position].set(value_part).reshape(n_row, capacity, BLOCK, width)
    key_ret, value_ret = (
        lax.all_to_all(key_out, "row", split_axis=0, concat_axis=0, tiled=True),
        lax.all_to_all(value_out, "row", split_axis=0, concat_axis=0, tiled=True),
    )
    key_back = key_ret.reshape(n_row * capacity, BLOCK, width)
    value_back = value_ret.reshape(n_row * capacity, BLOCK, width)
    query_grad = jnp.sum(
        query_terms.astype(jnp.float32).reshape(per_row, NEIGH, BLOCK, width), axis=1
    )
    key_grad = jnp.einsum("pi,pbd->ibd", collect, key_back, preferred_element_type=jnp.float32)
    value_grad = jnp.einsum("pi,pbd->ibd", collect, value_back, preferred_element_type=jnp.float32)
    return (
        query_grad.reshape(-1, width).astype(jnp.bfloat16),
        key_grad.reshape(-1, width).astype(jnp.bfloat16),
        value_grad.reshape(-1, width).astype(jnp.bfloat16),
    )


def solution(mesh):
    placed = (
        P(("groups", "row"), "col"),
        P(("groups", "row"), "col"),
        P(("groups", "row"), "col"),
        P(("groups", "row"), "col"),
        P(("groups", "row"), "col"),
        P(("groups", "row"), "col"),
        P("groups"),
        P("groups", None),
        P("groups"),
    )
    return jax.shard_map(
        body,
        mesh=mesh,
        in_specs=placed,
        out_specs=(
            P(("groups", "row"), "col"),
            P(("groups", "row"), "col"),
            P(("groups", "row"), "col"),
        ),
        check_vma=False,
    )
```

profile of v0, /device:TPU:10, one launch (start us, length us, event | category | flops | bytes accessed | tf_op | source)
XLA Modules:
  0.0 590.5 jit_solution(7606626698562229995)
XLA Ops:
  3.2 1.9 gather_fusion.1
  7.8 2.8 gather_fusion.3
  10.6 2.8 gather_fusion.8
  13.3 5.2 broadcast_select_fusion.4
  18.5 98.4 %all_to_all.20 = bf16[8,4,256,256]{3,2,1,0:T(8,128)(2,1)} all-to-all(bf16[8,4,256,256]{3,2,1,0:T(8,128)(2,1)S(1)} %bitcast.154), channel_id=1, replica_groups=mesh['groups'=2,'row'=8,'col'=2] {'row'}, dimensions={0} | all-to-all | bytes 8388608 | tf_op jit(solution)/shard_map/all_to_all | solution.py:124
  117.0 5.5 all-to-all-start.1
  122.7 2.8 gather_fusion.5
  125.5 2.9 gather_fusion.7
  131.3 6.0 %broadcast_select_fusion = (bf16[32,256,256]{2,1,0:T(8,128)(2,1)}, bf16[32,256,256]{2,1,0:T(8,128)(2,1)}) fusion(bf16[32,256,256]{2,1,0:T(8,128)(2,1)} %gather_fusion.7, pred[32]{0:T(512)(128)(4,1)S(1)} %get-tuple-element.203, bf16[32,256,256]{2,1,0:T(8,128)(2,1)} %gather_fusion.5), kind=kLoop, calls=%fused_computation.34 | loop fusion | flops 4194304 | bytes 16777248 | tf_op jit(solution)/shard_map/jit(_take)/select_n | solution.py:118
  137.3 5.0 gather_fusion.4
  142.2 70.2 %all-to-all-done.1 = bf16[8,4,256,256]{3,2,1,0:T(8,128)(2,1)} async-done(((bf16[8,4,256,256]{3,2,1,0:T(8,128)(2,1)}), bf16[8,4,256,256]{3,2,1,0:T(8,128)(2,1)}, u32[]{:S(2)}, u32[]{:S(2)}) %all-to-all-start.1) | async-done | bytes 4194336 | tf_op jit(solution)/shard_map/all_to_all | solution.py:125
  212.4 4.9 gather_fusion.9
  217.3 5.9 broadcast_select_fusion.2
  223.2 128.3 %while.16 = (s32[]{:T(128)}, bf16[16,2,256,256]{2,3,1,0:T(8,128)(2,1)}, bf16[16,2,256,256]{2,3,1,0:T(8,128)(2,1)}, bf16[16,2,256,256]{2,3,1,0:T(8,128)(2,1)}, bf...) while((s32[]{:T(128)}, ...), condition=%wide.region_5.10_spmd, body=%wide.region_4.9_spmd.sunk | while | flops 339873792 | bytes 17868444 | solution.py:52
  226.1 1.1 constant_dynamic-slice_fusion.11
  234.1 1.1 constant_dynamic-slice_fusion.11
  242.2 1.1 constant_dynamic-slice_fusion.11
  250.2 1.1 constant_dynamic-slice_fusion.11
  258.2 1.1 constant_dynamic-slice_fusion.11
  266.2 1.1 constant_dynamic-slice_fusion.11
  274.3 1.1 constant_dynamic-slice_fusion.11
  282.3 1.1 constant_dynamic-slice_fusion.11
  290.3 1.1 constant_dynamic-slice_fusion.11
  298.3 1.1 constant_dynamic-slice_fusion.11
  306.3 1.1 constant_dynamic-slice_fusion.11
  322.4 1.1 constant_dynamic-slice_fusion.11
  330.4 1.1 constant_dynamic-slice_fusion.11
  338.4 1.1 constant_dynamic-slice_fusion.11
  346.4 1.1 constant_dynamic-slice_fusion.11
  351.6 6.5 %copy.101 = bf16[32,256,256]{2,1,0:T(8,128)(2,1)} copy(bf16[32,256,256]{1,2,0:T(8,128)(2,1)} %bitcast.160) | data formatting | bytes 8388608 | tf_op jit(solution)/shard_map/reshape | solution.py:53
  358.0 2.4 broadcast_in_dim.122.clone
  360.5 11.4 %scatter_fusion = bf16[32,256,256]{2,1,0:T(8,128)(2,1)} fusion(bf16[32,256,256]{2,1,0:T(8,128)(2,1)} %broadcast_in_dim.122.clone, s32[32]{0:T(128)S(1)} %get-tuple-element.184, bf16[32,256,256]{2,1,0:T(8,128)(2,1)} %copy.101), kind=kCustom, calls=%fused_computation.11 | custom fusion | bytes 12583040 | tf_op jit(solution)/shard_map/scatter | solution.py:133
  371.8 7.4 %copy.102 = bf16[8,4,256,256]{3,1,2,0:T(4,128)(2,1)} copy(bf16[8,4,256,256]{3,2,1,0:T(8,128)(2,1)} %bitcast.146) | data formatting | bytes 8388608 | tf_op jit(solution)/shard_map/reshape | solution.py:133
  379.2 7.0 %all-to-all-start.2 = ((bf16[8,4,256,256]{3,1,2,0:T(4,128)(2,1)}), bf16[8,4,256,256]{3,1,2,0:T(4,128)(2,1)}, u32[]{:S(2)}, u32[]{:S(2)}) async-start(bf16[8,4,256,256]{3,1,2,0:T(4,128)(2,1)} %copy.102), calls=%async_computation.2 | async-start | bytes 8388608 | tf_op jit(solution)/shard_map/all_to_all | solution.py:136
  386.1 6.4 %copy.105 = bf16[32,256,256]{2,1,0:T(8,128)(2,1)} copy(bf16[32,256,256]{1,2,0:T(8,128)(2,1)} %bitcast.43) | data formatting | bytes 8388608 | tf_op jit(solution)/shard_map/reshape | solution.py:53
  392.6 2.4 broadcast_in_dim.122.clone.1
  395.0 11.4 %scatter_fusion.1 = bf16[32,256,256]{2,1,0:T(8,128)(2,1)} fusion(bf16[32,256,256]{2,1,0:T(8,128)(2,1)} %broadcast_in_dim.122.clone.1, s32[32]{0:T(128)S(1)} %get-tuple-element.184, bf16[32,256,256]{2,1,0:T(8,128)(2,1)} %copy.105), kind=kCustom, calls=%fused_computation.12 | custom fusion | bytes 12583040 | tf_op jit(solution)/shard_map/scatter | solution.py:134
  406.4 7.4 %copy.106 = bf16[8,4,256,256]{3,1,2,0:T(4,128)(2,1)} copy(bf16[8,4,256,256]{3,2,1,0:T(8,128)(2,1)} %bitcast.145) | data formatting | bytes 8388608 | tf_op jit(solution)/shard_map/reshape | solution.py:134
  413.8 62.5 %all-to-all-done.2 = bf16[8,4,256,256]{3,1,2,0:T(4,128)(2,1)} async-done(((bf16[8,4,256,256]{3,1,2,0:T(4,128)(2,1)}), bf16[8,4,256,256]{3,1,2,0:T(4,128)(2,1)}, u32[]{:S(2)}, u32[]{:S(2)}) %all-to-all-start.2) | async-done | bytes 4194336 | tf_op jit(solution)/shard_map/all_to_all | solution.py:136
  476.3 7.1 %all-to-all-start.3 = ((bf16[8,4,256,256]{3,1,2,0:T(4,128)(2,1)}), bf16[8,4,256,256]{3,1,2,0:T(4,128)(2,1)}, u32[]{:S(2)}, u32[]{:S(2)}) async-start(bf16[8,4,256,256]{3,1,2,0:T(4,128)(2,1)} %copy.106), calls=%async_computation.3 | async-start | bytes 8388608 | tf_op jit(solution)/shard_map/all_to_all | solution.py:137
  483.5 3.5 convert_reduce_fusion
  488.3 6.5 %copy.103 = bf16[8,4,256,256]{3,1,0,2:T(4,128)(2,1)} copy(bf16[8,4,256,256]{3,1,2,0:T(4,128)(2,1)} %all-to-all-done.2) | data formatting | bytes 8388608 | tf_op jit(solution)/shard_map/all_to_all | solution.py:136
  494.8 7.0 %reshape.389 = bf16[32,256,256]{2,0,1:T(8,128)(2,1)} reshape(bf16[8,4,256,256]{3,1,0,2:T(4,128)(2,1)} %copy.103) | data formatting | bytes 8388608 | tf_op jit(solution)/shard_map/reshape | solution.py:139
  501.8 2.8 convolution_convert_fusion.2
  505.5 67.8 %all-to-all-done.3 = bf16[8,4,256,256]{3,1,2,0:T(4,128)(2,1)} async-done(((bf16[8,4,256,256]{3,1,2,0:T(4,128)(2,1)}), bf16[8,4,256,256]{3,1,2,0:T(4,128)(2,1)}, u32[]{:S(2)}, u32[]{:S(2)}) %all-to-all-start.3) | async-done | bytes 4194336 | tf_op jit(solution)/shard_map/all_to_all | solution.py:137
  573.3 6.5 %copy.107 = bf16[8,4,256,256]{3,1,0,2:T(4,128)(2,1)} copy(bf16[8,4,256,256]{3,1,2,0:T(4,128)(2,1)} %all-to-all-done.3) | data formatting | bytes 8388608 | tf_op jit(solution)/shard_map/all_to_all | solution.py:137
  579.8 7.0 %reshape.392 = bf16[32,256,256]{2,0,1:T(8,128)(2,1)} reshape(bf16[8,4,256,256]{3,1,0,2:T(4,128)(2,1)} %copy.107) | data formatting | bytes 8388608 | tf_op jit(solution)/shard_map/reshape | solution.py:140
  586.8 2.8 convolution_convert_fusion.1
  (321 shorter events, 122.6 us)
Async XLA Ops:
  0.6 7.2 %copy-start = (bf16[1024,256]{1,0:T(8,128)(2,1)S(1)}, bf16[1024,256]{1,0:T(8,128)(2,1)}, u32[]{:S(2)}) copy-start(bf16[1024,256]{1,0:T(8,128)(2,1)} %param.20) | copy-start | bytes 1572868
  0.6 2.5 copy-start.2
  3.2 2.0 copy-start.4
  7.2 0.6 copy-start.9
  7.8 2.8 copy-start.6
  117.0 5.5 copy-start.5
  117.0 5.7 copy-start.7
  117.0 95.4 %all-to-all-start.1 = ((bf16[8,4,256,256]{3,2,1,0:T(8,128)(2,1)}), bf16[8,4,256,256]{3,2,1,0:T(8,128)(2,1)}, u32[]{:S(2)}, u32[]{:S(2)}) async-start(bf16[8,4,256,256]{3,2,1,0:T(8,128)(2,1)} %bitcast.153), calls=%async_computation.1 | async-start | bytes 8388608 | tf_op jit(solution)/shard_map/all_to_all | solution.py:125
  125.5 2.9 copy-start.8
  128.4 1.0 copy-start.3
  379.2 97.1 %all-to-all-start.2 = ((bf16[8,4,256,256]{3,1,2,0:T(4,128)(2,1)}), bf16[8,4,256,256]{3,1,2,0:T(4,128)(2,1)}, u32[]{:S(2)}, u32[]{:S(2)}) async-start(bf16[8,4,256,256]{3,1,2,0:T(4,128)(2,1)} %copy.102), calls=%async_computation.2 | async-start | bytes 8388608 | tf_op jit(solution)/shard_map/all_to_all | solution.py:136
  476.3 97.0 %all-to-all-start.3 = ((bf16[8,4,256,256]{3,1,2,0:T(4,128)(2,1)}), bf16[8,4,256,256]{3,1,2,0:T(4,128)(2,1)}, u32[]{:S(2)}, u32[]{:S(2)}) async-start(bf16[8,4,256,256]{3,1,2,0:T(4,128)(2,1)} %copy.106), calls=%async_computation.3 | async-start | bytes 8388608 | tf_op jit(solution)/shard_map/all_to_all | solution.py:137
  494.8 7.0 %copy-start.10 = (s32[32]{0:T(128)S(1)}, s32[32]{0:T(128)}, u32[]{:S(2)}) copy-start(s32[32]{0:T(128)} %copy-done.9) | copy-start | bytes 388
  579.8 10.7 %copy-start.1 = (bf16[1024,256]{1,0:T(8,128)(2,1)S(1)}, bf16[1024,256]{1,0:T(8,128)(2,1)}, u32[]{:S(2)}) copy-start(bf16[1024,256]{1,0:T(8,128)(2,1)} %param.20) | copy-start | bytes 1572868
where the time goes:
time: 597 us; the launch traced here: 591 us
  local copies, waits for them, and re-layouts  203 us (34%)
  waiting for transfers between devices  200 us (34%)
  blocking collectives  98.4 us (16%)
  matrix products  44 us (7%)
  other arithmetic  23 us (4%)
  starting transfers between devices  19.5 us (3%)
    all_to_all x1, blocking collectives, body(): lax.all_to_all(send_keys, 'row', split_axis=0, concat_axis=0, tiled=True)  98.4 us
    all_to_all x1, waiting for transfers between devices, body(): lax.all_to_all(send_values, 'row', split_axis=0, concat_axis=0, tiled=True)  70.2 us
    all_to_all x1, waiting for transfers between devices, body(): lax.all_to_all(value_out, 'row', split_axis=0, concat_axis=0, tiled=True)  67.8 us
    all_to_all x1, waiting for transfers between devices, body(): lax.all_to_all(key_out, 'row', split_axis=0, concat_axis=0, tiled=True)  62.5 us
    dynamic_slice x96, local copies, waits for them, and re-layouts, in_pairs(): results = lax.map(lambda items: entry_terms(*items), paired)  42.6 us
    dynamic_update_slice x48, local copies, waits for them, and re-layouts, in_pairs(): results = lax.map(lambda items: entry_terms(*items), paired)  34.9 us
    dot_general x16, matrix products, entry_terms(): jnp.einsum('mqhe,mkhe->mhqk', query_h, key_h, preferred_element_type=jnp....  13.3 us
    reshape x2, local copies, waits for them, and re-layouts, in_pairs(): array.reshape((count,) + array.shape[2:])  12.9 us
  transfers between devices with their start and end apart: 3, of which 3 were waited for; matrix products, arithmetic and copies ran while one was open for 12% of the time, Pallas kernels for 0%

commit v1 on v0

v1 whole, which is shorter than its diff:
```python
import functools

import jax
import jax.numpy as jnp
from jax import lax
from jax.experimental import pallas as pl
from jax.experimental.pallas import tpu as pltpu
from jax.sharding import PartitionSpec as P

BLOCK = 256
NEIGH = 8
SCALE = 0.125
HEAD = 64
PAIR = 2 * HEAD
STATS = 16


def nt(a, b):
    return lax.dot_general(a, b, (((1,), (1,)), ((), ())), preferred_element_type=jnp.float32)


def nn(a, b):
    return lax.dot_general(a, b, (((1,), (0,)), ((), ())), preferred_element_type=jnp.float32)


def grads_kernel(
    here_ref, slot_ref, near_ref, live_ref, load_ref, key_ref, value_ref,
    dq_ref, dk_ref, dv_ref,
    src_list, dst_list, dq_acc, dk_acc, dv_acc, key_m, value_m, key_t,
):
    blocks = slot_ref.shape[0]
    per_row = key_ref.shape[0]
    first = here_ref[0] * per_row

    def scan_block(b, count):
        source = slot_ref[b]
        live = live_ref[b]

        def scan_entry(j, count):
            target = slot_ref[near_ref[b * NEIGH + j]] - first
            mine = (target >= 0) & (target < per_row) & (j < live)

            @pl.when(mine)
            def _():
                src_list[count] = source
                dst_list[count] = target

            return count + mine.astype(jnp.int32)

        return lax.fori_loop(0, NEIGH, scan_entry, count, unroll=True)

    count = lax.fori_loop(0, blocks, scan_block, jnp.int32(0))

    dk_acc[...] = jnp.zeros_like(dk_acc)
    dv_acc[...] = jnp.zeros_like(dv_acc)

    @pl.loop(0, blocks)
    def _(s):
        dq_acc[s] = jnp.zeros(dq_acc.shape[1:], jnp.float32)

    low = lax.broadcasted_iota(jnp.int32, (BLOCK, PAIR), 1) < HEAD
    for t in range(per_row):
        key = key_ref[t].astype(jnp.float32) * SCALE
        value = value_ref[t].astype(jnp.float32)
        for h in range(2):
            mask = low if h == 0 else ~low
            masked = jnp.where(mask, key, 0.0)
            key_m[t, h * BLOCK:(h + 1) * BLOCK] = masked.astype(jnp.bfloat16)
            value_m[t, h * BLOCK:(h + 1) * BLOCK] = jnp.where(mask, value, 0.0).astype(jnp.bfloat16)
            key_t[t, :, h * BLOCK:(h + 1) * BLOCK] = masked.T.astype(jnp.bfloat16)

    @pl.loop(0, count)
    def _(e):
        s = src_list[e]
        t = dst_list[e]
        query = load_ref[s, 0:BLOCK]
        grad = load_ref[s, BLOCK:2 * BLOCK]
        stats = load_ref[s, 2 * BLOCK:2 * BLOCK + STATS].astype(jnp.float32)

        def row(i):
            return jnp.concatenate([stats[2 * i:2 * i + 1], stats[2 * i + 1:2 * i + 2]], axis=1)

        score = nt(key_m[t], query)
        dprob = nt(value_m[t], grad)
        probs, dscores = [], []
        for h in range(2):
            part = slice(h * BLOCK, (h + 1) * BLOCK)
            prob = jnp.exp(score[part] - row(h))
            dscores.append((prob * (dprob[part] - row(2 + h))).astype(jnp.bfloat16))
            probs.append(prob.astype(jnp.bfloat16))
        dv_acc[t] += jnp.where(low, nn(probs[0], grad), nn(probs[1], grad))
        dk_acc[t] += jnp.where(low, nn(dscores[0], query), nn(dscores[1], query))
        dq_acc[s] += nn(key_t[t], jnp.concatenate(dscores, axis=0))

    dk_ref[...] = (dk_acc[...] * SCALE).astype(jnp.bfloat16)
    dv_ref[...] = dv_acc[...].astype(jnp.bfloat16)

    @pl.loop(0, blocks)
    def _(s):
        dq_ref[s] = dq_acc[s].astype(jnp.bfloat16)


def local_grads(here, slots, near, live, load, key, value):
    blocks, rows, _ = load.shape
    per_row = key.shape[0]
    smem = pl.BlockSpec(memory_space=pltpu.SMEM)
    vmem = pl.BlockSpec(memory_space=pltpu.VMEM)
    most = per_row * NEIGH * 4
    return pl.pallas_call(
        grads_kernel,
        out_shape=(
            jax.ShapeDtypeStruct((blocks, PAIR, BLOCK), jnp.bfloat16),
            jax.ShapeDtypeStruct(key.shape, jnp.bfloat16),
            jax.ShapeDtypeStruct(key.shape, jnp.bfloat16),
        ),
        in_specs=[smem] * 4 + [vmem] * 3,
        out_specs=(vmem, vmem, vmem),
        scratch_shapes=[
            pltpu.SMEM((most,), jnp.int32),
            pltpu.SMEM((most,), jnp.int32),
            pltpu.VMEM((blocks, PAIR, BLOCK), jnp.float32),
            pltpu.VMEM(key.shape, jnp.float32),
            pltpu.VMEM(key.shape, jnp.float32),
            pltpu.VMEM((per_row, 2 * BLOCK, PAIR), jnp.bfloat16),
            pltpu.VMEM((per_row, 2 * BLOCK, PAIR), jnp.bfloat16),
            pltpu.VMEM((per_row, PAIR, 2 * BLOCK), jnp.bfloat16),
        ],
        compiler_params=pltpu.CompilerParams(vmem_limit_bytes=56 * 2**20),
        cost_estimate=pl.CostEstimate(
            flops=10 * 32 * 2 * BLOCK * BLOCK * PAIR, bytes_accessed=8 * 2**20, transcendentals=0
        ),
    )(here, slots, near, live, load, key, value)


def body(queries, keys, values, attended, grad_out, log_norms, block_slot, neighbours, live_count):
    here = lax.axis_index("row").astype(jnp.int32).reshape(1)
    tokens, width = queries.shape
    per_row = tokens // BLOCK
    heads = log_norms.shape[1]
    near = neighbours.reshape(-1)
    delta = jnp.sum(
        (grad_out.astype(jnp.float32) * attended.astype(jnp.float32)).reshape(tokens, heads, HEAD),
        axis=2,
    ).astype(jnp.bfloat16)
    loads = []
    for c in range(heads // 2):
        lanes = slice(c * PAIR, (c + 1) * PAIR)
        stats = jnp.concatenate([log_norms[:, 2 * c:2 * c + 2], delta[:, 2 * c:2 * c + 2]], axis=1)
        stats = jnp.transpose(stats.reshape(per_row, BLOCK, 4), (0, 2, 1)).reshape(per_row, 8, PAIR)
        loads.append(jnp.concatenate([
            queries[:, lanes].reshape(per_row, BLOCK, PAIR),
            grad_out[:, lanes].reshape(per_row, BLOCK, PAIR),
            stats,
            jnp.zeros((per_row, STATS - 8, PAIR), jnp.bfloat16),
        ], axis=1))
    everyone = [lax.all_gather(load, "row", axis=0, tiled=True) for load in loads]
    dqs, dks, dvs = [], [], []
    for c in range(heads // 2):
        lanes = slice(c * PAIR, (c + 1) * PAIR)
        dq, dk, dv = local_grads(
            here, block_slot, near, live_count, everyone[c],
            keys[:, lanes].reshape(per_row, BLOCK, PAIR),
            values[:, lanes].reshape(per_row, BLOCK, PAIR),
        )
        dq = lax.psum_scatter(dq, "row", scatter_dimension=0, tiled=True)
        dqs.append(jnp.transpose(dq, (0, 2, 1)).reshape(tokens, PAIR))
        dks.append(dk.reshape(tokens, PAIR))
        dvs.append(dv.reshape(tokens, PAIR))
    return tuple(jnp.concatenate(x, axis=1) for x in (dqs, dks, dvs))


def solution(mesh):
    tokens = P(("groups", "row"), "col")
    return jax.shard_map(
        body,
        mesh=mesh,
        in_specs=(tokens,) * 6 + (P("groups"), P("groups", None), P("groups")),
        out_specs=(tokens,) * 3,
        check_vma=False,
    )
```

time: 597 us -> 313 us (0.52)
  local copies, waits for them, and re-layouts: 203 us -> 7.85 us
  blocking collectives: 98.4 us -> 0 us
  waiting for transfers between devices: 200 us -> 246 us
  matrix products: 44 us -> 0 us
  Pallas kernels: 0 us -> 38.6 us
  starting transfers between devices: 19.5 us -> 0.16 us
  other arithmetic: 23 us -> 4.09 us
  between operations: 0.86 us -> 13.9 us
    all_to_all x3 -> x0, waiting for transfers between devices: 200 us -> none  [the longest x1 70.2 us: body(): lax.all_to_all(send_values, 'row', split_axis=0, concat_axis=0, tiled=True)]
    all_gather x0 -> x2, waiting for transfers between devices: none -> 128 us  [body(): lax.all_gather(load, 'row', axis=0, tiled=True)]
    reduce_scatter x0 -> x2, waiting for transfers between devices: none -> 117 us  [body(): dq = lax.psum_scatter(dq, 'row', scatter_dimension=0, tiled=True)]
    all_to_all x1 -> x0, blocking collectives: 98.4 us -> none  [body(): lax.all_to_all(send_keys, 'row', split_axis=0, concat_axis=0, tiled=True)]
    dot_general x82 -> x0, matrix products: 44 us -> none  [the longest x16 13.3 us: entry_terms(): jnp.einsum('mqhe,mkhe->mhqk', query_h, key_h, preferred_element_type=jnp....]
    dynamic_slice x96 -> x0, local copies, waits for them, and re-layouts: 42.6 us -> none  [in_pairs(): results = lax.map(lambda items: entry_terms(*items), paired)]
    reshape x7 -> x3, local copies, waits for them, and re-layouts: 41.7 us -> 0.64 us  [the longest x1 0.61 us: body(): near = neighbours.reshape(-1)]
    pallas_call x0 -> x2, Pallas kernels: none -> 38.6 us  [local_grads(): pl.pallas_call(grads_kernel, out_shape=(jax.ShapeDtypeStruct((blocks, PAI...]
  transfers between devices with their start and end apart: 3 -> 4, of which waited for: 3 -> 4; matrix products, arithmetic and copies ran while one was open for 12% -> 2% of each run, Pallas kernels for 0% -> 12%
where the time goes in v1:
time: 313 us; the launch traced here: 311 us
  waiting for transfers between devices  246 us (79%)
  Pallas kernels  38.6 us (12%)
  between operations  13.9 us (4%)
  local copies, waits for them, and re-layouts  7.85 us (3%)
  other arithmetic  4.09 us (1%)
    all_gather x2, waiting for transfers between devices, body(): lax.all_gather(load, 'row', axis=0, tiled=True)  128 us
    reduce_scatter x2, waiting for transfers between devices, body(): dq = lax.psum_scatter(dq, 'row', scatter_dimension=0, tiled=True)  117 us
    pallas_call x2, Pallas kernels, local_grads(): pl.pallas_call(grads_kernel, out_shape=(jax.ShapeDtypeStruct((blocks, PAI...  38.6 us
  transfers between devices with their start and end apart: 4, of which 4 were waited for; matrix products, arithmetic and copies ran while one was open for 2% of the time, Pallas kernels for 12%

profile of v1, /device:TPU:10, one launch (start us, length us, event | category | flops | bytes accessed | tf_op | source)
XLA Modules:
  0.0 310.6 jit_solution(7229706741451127471)
XLA Ops:
  7.2 0.0 copy-start
  7.2 0.0 copy-start.9
  7.2 0.0 copy-start.1
  7.2 0.0 all-gather.3.cloned.1.call-start
  7.2 1.3 copy.22
  8.6 0.0 copy-done
  8.6 0.0 copy-done.9
  8.7 0.0 copy-done.1
  8.7 0.0 copy-start.2
  8.7 0.2 copy.23
  8.9 0.2 bitcast_reduce_fusion
  9.2 0.5 copy-done.2
  9.8 0.1 pad.15.clone
  9.8 1.3 maximum_maximum_fusion
  11.1 0.0 copy-start.10
  11.1 0.0 copy-start.3
  11.2 0.0 copy-start.4
  11.2 0.0 all-gather.3.cloned.1.call-update
  11.2 0.0 all-gather.5.cloned.1.call-start
  11.2 0.7 all-gather.5.cloned.1.call-update
  11.9 0.0 reduce-scatter.3.cloned.1.call-start
  12.0 0.0 copy-done.10
  12.0 0.1 copy.21
  12.1 0.6 reshape.70.near_ref
  12.7 0.0 copy-done.3
  12.7 0.8 fusion.1
  13.5 0.0 copy-done.4
  13.5 0.8 fusion
  14.3 72.4 %all-gather.3.cloned.1.call-done.load_ref = bf16[32,528,128]{2,1,0:T(8,128)(2,1)} async-done(((bf16[4,528,128]{2,1,0:T(8,128)(2,1)}), bf16[32,528,128]{2,1,0:T(8,128)(2,1)}) %all-gather.3.cloned.1.call-update) | async-done | bytes 4325392 | tf_op jit(solution)/shard_map/all_gather | solution.py:156
  86.7 19.3 %shard_map.112 = (bf16[32,128,256]{2,1,0:T(8,128)(2,1)}, bf16[4,256,128]{2,1,0:T(8,128)(2,1)}, bf16[4,256,128]{2,1,0:T(8,128)(2,1)}) custom-call(s32[1]{0:T(128)} %bitcast.here_ref, s32[32]{0:T(128)} %slot_ref.3, s32[256]{0:T(256)} %reshape.70.near_ref, s32[32]{0:T(128)} %live_ref.3, bf16[32,528,128]{2,1,0:T(8,128)(2,1)} %all-gather.3.cloned.1.call-done.load_ref, ...), custom_call_target="tpu_custom_call" | custom-call | flops 5368709120 | bytes 8388608 | tf_op jit(solution)/shard_map/pallas_call | solution.py:109
  106.1 0.0 reduce-scatter.3.cloned.1.call-update
  106.1 0.0 reduce-scatter.5.cloned.1.call-start
  106.1 56.1 %all-gather.5.cloned.1.call-done.load_ref = bf16[32,528,128]{2,1,0:T(8,128)(2,1)} async-done(((bf16[4,528,128]{2,1,0:T(8,128)(2,1)}), bf16[32,528,128]{2,1,0:T(8,128)(2,1)}) %all-gather.5.cloned.1.call-update) | async-done | bytes 4325392 | tf_op jit(solution)/shard_map/all_gather | solution.py:156
  162.2 19.3 %shard_map.113 = (bf16[32,128,256]{2,1,0:T(8,128)(2,1)}, bf16[4,256,128]{2,1,0:T(8,128)(2,1)}, bf16[4,256,128]{2,1,0:T(8,128)(2,1)}) custom-call(s32[1]{0:T(128)} %bitcast.here_ref, s32[32]{0:T(128)} %slot_ref.3, s32[256]{0:T(256)} %reshape.70.near_ref, s32[32]{0:T(128)} %live_ref.3, bf16[32,528,128]{2,1,0:T(8,128)(2,1)} %all-gather.5.cloned.1.call-done.load_ref, ...), custom_call_target="tpu_custom_call" | custom-call | flops 5368709120 | bytes 8388608 | tf_op jit(solution)/shard_map/pallas_call | solution.py:109
  181.5 0.0 copy-start.6
  181.5 0.0 copy-start.7
  181.5 0.0 reduce-scatter.5.cloned.1.call-update
  181.5 0.9 copy-done.6
  182.4 0.1 copy-done.8
  182.5 0.8 pad_maximum_fusion.1
  183.3 0.0 copy-done.5
  183.3 0.0 copy-done.7
  183.3 0.9 pad_maximum_fusion.2
  184.2 47.7 %reduce-scatter.3.cloned.1.call-done = bf16[4,128,256]{2,1,0:T(8,128)(2,1)} async-done(((bf16[32,128,256]{2,1,0:T(8,128)(2,1)}), bf16[4,128,256]{2,1,0:T(8,128)(2,1)}) %reduce-scatter.3.cloned.1.call-update) | async-done | bytes 262160 | tf_op jit(solution)/shard_map/reduce_scatter | solution.py:165
  231.9 1.1 copy.25
  233.0 69.1 %reduce-scatter.5.cloned.1.call-done = bf16[4,128,256]{2,1,0:T(8,128)(2,1)} async-done(((bf16[32,128,256]{2,1,0:T(8,128)(2,1)}), bf16[4,128,256]{2,1,0:T(8,128)(2,1)}) %reduce-scatter.5.cloned.1.call-update) | async-done | bytes 262160 | tf_op jit(solution)/shard_map/reduce_scatter | solution.py:165
  302.1 1.1 copy.27
  303.2 0.9 pad_maximum_fusion
  (10 shorter events, 0.1 us)
Async XLA Ops:
  7.2 1.4 copy-start
  7.2 1.4 copy-start.9
  7.2 1.5 copy-start.1
  7.2 79.6 %all-gather.3.cloned.1.call-start = ((), (), s32[]{:S(2)}) async-start(), calls=%async_computation.2 | async-start | bytes 4866048 | tf_op jit(solution)/shard_map/all_gather | solution.py:156
  8.7 1.0 copy-start.2
  11.1 0.8 copy-start.10
  11.1 1.5 copy-start.3
  11.2 2.4 copy-start.4
  11.2 151.0 %all-gather.5.cloned.1.call-start = ((), (), s32[]{:S(2)}) async-start(), calls=%async_computation.4 | async-start | bytes 4866048 | tf_op jit(solution)/shard_map/all_gather | solution.py:156
  11.9 219.9 %reduce-scatter.3.cloned.1.call-start = ((), (), s32[]{:S(2)}) async-start(), calls=%async_computation.3 | async-start | bytes 2359296 | tf_op jit(solution)/shard_map/reduce_scatter | solution.py:165
  106.1 196.0 %reduce-scatter.5.cloned.1.call-start = ((), (), s32[]{:S(2)}) async-start(), calls=%async_computation.5 | async-start | bytes 2359296 | tf_op jit(solution)/shard_map/reduce_scatter | solution.py:165
  181.5 1.0 copy-start.6
  181.5 1.0 copy-start.8
  181.5 1.9 copy-start.5
  181.5 1.9 copy-start.7
Sparse Core Ops, SparseCore 0:
  11.3 75.4 all-gather.2
  88.9 73.2 all-gather.4
  165.7 66.0 reduce-scatter.2
  235.2 66.8 reduce-scatter.4

commit v2 on v1

v2 whole, which is shorter than its diff:
```python
import functools

import jax
import jax.numpy as jnp
from jax import lax
from jax.experimental import pallas as pl
from jax.experimental.pallas import tpu as pltpu
from jax.sharding import PartitionSpec as P

BLOCK = 256
NEIGH = 8
SCALE = 0.125
HEAD = 64
PAIR = 2 * HEAD
STATS = 16


def nt(a, b):
    return lax.dot_general(a, b, (((1,), (1,)), ((), ())), preferred_element_type=jnp.float32)


def nn(a, b):
    return lax.dot_general(a, b, (((1,), (0,)), ((), ())), preferred_element_type=jnp.float32)


def scan_kernel(here_ref, slot_ref, near_ref, live_ref, count_ref, entry_ref):
    blocks = slot_ref.shape[0]
    n_row = count_ref.shape[0]
    per_row = blocks // n_row
    first = here_ref[0] * per_row
    room = NEIGH * per_row

    @pl.loop(0, n_row)
    def _(r):
        count_ref[r] = 0

    @pl.loop(0, blocks)
    def _(b):
        source = slot_ref[b]
        row = source // per_row
        live = live_ref[b]

        def scan_entry(j, count):
            target = slot_ref[near_ref[b * NEIGH + j]] - first
            mine = (target >= 0) & (target < per_row) & (j < live)

            @pl.when(mine)
            def _():
                entry_ref[row * room + count] = (source - row * per_row) * per_row + target

            return count + mine.astype(jnp.int32)

        count_ref[row] = lax.fori_loop(0, NEIGH, scan_entry, count_ref[row], unroll=True)


def scan_lists(here, slots, near, live, n_row):
    smem = pl.BlockSpec(memory_space=pltpu.SMEM)
    return pl.pallas_call(
        scan_kernel,
        out_shape=(
            jax.ShapeDtypeStruct((n_row,), jnp.int32),
            jax.ShapeDtypeStruct((slots.shape[0] * NEIGH,), jnp.int32),
        ),
        in_specs=[smem] * 4,
        out_specs=(smem, smem),
    )(here, slots, near, live)


def grads_kernel(n_load, first, row_ref, count_ref, entry_ref, key_ref, value_ref, *refs):
    loads, refs = refs[:n_load], refs[n_load:]
    if not first:
        dk_old, dv_old = refs[:2]
        refs = refs[2:]
    dqs, refs = refs[:n_load], refs[n_load:]
    dk_acc, dv_acc, dq_acc, key_m, value_m, key_t = refs
    per_row = key_ref.shape[0]
    pairs = key_ref.shape[2] // PAIR
    room = NEIGH * per_row
    if first:
        dk_acc[...] = jnp.zeros_like(dk_acc)
        dv_acc[...] = jnp.zeros_like(dv_acc)
    else:
        dk_acc[...] = dk_old[...]
        dv_acc[...] = dv_old[...]

    low = lax.broadcasted_iota(jnp.int32, (BLOCK, PAIR), 1) < HEAD
    for c in range(pairs):
        lanes = slice(c * PAIR, (c + 1) * PAIR)

        @pl.loop(0, per_row)
        def _(t):
            key = key_ref[t, :, lanes].astype(jnp.float32) * SCALE
            value = value_ref[t, :, lanes].astype(jnp.float32)
            for h in range(2):
                mask = low if h == 0 else ~low
                part = slice(h * BLOCK, (h + 1) * BLOCK)
                masked = jnp.where(mask, key, 0.0)
                key_m[c, t, part] = masked.astype(jnp.bfloat16)
                value_m[c, t, part] = jnp.where(mask, value, 0.0).astype(jnp.bfloat16)
                key_t[c, t, :, part] = masked.T.astype(jnp.bfloat16)

    for load_ref, dq_ref, i in zip(loads, dqs, range(n_load)):
        source_row = row_ref[i]
        dq_acc[...] = jnp.zeros_like(dq_acc)

        @pl.when(source_row >= 0)
        def _():
            @pl.loop(0, count_ref[source_row])
            def _(e):
                entry = entry_ref[source_row * room + e]
                s = entry // per_row
                t = entry % per_row
                for c in range(pairs):
                    lanes = slice(c * PAIR, (c + 1) * PAIR)
                    query = load_ref[s, 0:BLOCK, lanes]
                    grad = load_ref[s, BLOCK:2 * BLOCK, lanes]
                    stats = load_ref[s, 2 * BLOCK:2 * BLOCK + STATS].astype(jnp.float32)
                    score = nt(key_m[c, t], query)
                    dprob = nt(value_m[c, t], grad)
                    probs, dscores = [], []
                    for h in range(2):
                        part = slice(h * BLOCK, (h + 1) * BLOCK)
                        i_h = 2 * c + h
                        norm = stats[i_h:i_h + 1]
                        delta = stats[2 * pairs + i_h:2 * pairs + i_h + 1]
                        prob = jnp.exp(score[part] - norm)
                        dscores.append((prob * (dprob[part] - delta)).astype(jnp.bfloat16))
                        probs.append(prob.astype(jnp.bfloat16))
                    dv_acc[t, :, lanes] += jnp.where(low, nn(probs[0], grad), nn(probs[1], grad))
                    dk_acc[t, :, lanes] += jnp.where(low, nn(dscores[0], query), nn(dscores[1], query))
                    dq_acc[s, lanes] += nn(key_t[c, t], jnp.concatenate(dscores, axis=0))

        dq_ref[...] = dq_acc[...].astype(jnp.bfloat16)


def stage_grads(rows, counts, entries, key, value, loads, carry):
    per_row, _, width = key.shape
    pairs = width // PAIR
    n_load = len(loads)
    smem = pl.BlockSpec(memory_space=pltpu.SMEM)
    vmem = pl.BlockSpec(memory_space=pltpu.VMEM)
    part = jax.ShapeDtypeStruct((per_row, width, BLOCK), jnp.bfloat16)
    total = jax.ShapeDtypeStruct(key.shape, jnp.float32)
    outs = pl.pallas_call(
        functools.partial(grads_kernel, n_load, not carry),
        out_shape=(part,) * n_load + (total, total),
        in_specs=[smem] * 3 + [vmem] * (2 + n_load + len(carry)),
        out_specs=(vmem,) * (n_load + 2),
        scratch_shapes=[
            pltpu.VMEM((per_row, width, BLOCK), jnp.float32),
            pltpu.VMEM((pairs, per_row, 2 * BLOCK, PAIR), jnp.bfloat16),
            pltpu.VMEM((pairs, per_row, 2 * BLOCK, PAIR), jnp.bfloat16),
            pltpu.VMEM((pairs, per_row, PAIR, 2 * BLOCK), jnp.bfloat16),
        ],
        compiler_params=pltpu.CompilerParams(vmem_limit_bytes=40 * 2**20),
        cost_estimate=pl.CostEstimate(
            flops=n_load * 3000000000, bytes_accessed=n_load * 2**21, transcendentals=0
        ),
    )(rows, counts, entries, key, value, *loads, *carry)
    return outs[:n_load], outs[n_load:]


def body(queries, keys, values, attended, grad_out, log_norms, block_slot, neighbours, live_count):
    n_row = lax.axis_size("row")
    here = lax.axis_index("row").astype(jnp.int32)
    n_z = n_row // 2
    z, y = here // 2, here % 2
    tokens, width = queries.shape
    per_row = tokens // BLOCK
    heads = log_norms.shape[1]

    def swap(x, low, high):
        pairs = [(2 * k + j, 2 * k + 1 - j) for k in range(low, high) for j in range(2)]
        return lax.ppermute(x, "row", pairs)

    def shift(x, by, low, high):
        pairs = [(2 * k + j, 2 * (k + by) + j) for k in range(low, high) for j in range(2)]
        return lax.ppermute(x, "row", pairs)

    delta = jnp.sum(
        (grad_out.astype(jnp.float32) * attended.astype(jnp.float32)).reshape(tokens, heads, HEAD),
        axis=2,
    ).astype(jnp.bfloat16)
    stats = jnp.concatenate([log_norms, delta], axis=1).reshape(per_row, BLOCK, 2 * heads)
    own = jnp.concatenate([
        queries.reshape(per_row, BLOCK, width),
        grad_out.reshape(per_row, BLOCK, width),
        jnp.transpose(stats, (0, 2, 1)),
        jnp.zeros((per_row, STATS - 2 * heads, width), jnp.bfloat16),
    ], axis=1)
    key = keys.reshape(per_row, BLOCK, width)
    value = values.reshape(per_row, BLOCK, width)

    ups, downs, y_ups, y_downs = [own], [own], [swap(own, 0, n_z)], [None]
    for k in range(1, n_z):
        ups.append(shift(ups[-1], 1, k - 1, n_z - 1))
        downs.append(shift(downs[-1], -1, 1, n_z - k + 1))
        y_ups.append(swap(ups[k], k, n_z))
        y_downs.append(swap(downs[k], 0, n_z - k))

    counts, entries = scan_lists(
        here.reshape(1), block_slot, neighbours.reshape(-1), live_count, n_row
    )

    def named(kind, k):
        up = kind in ("up", "y_up")
        there = z - k if up else z + k
        side = 1 - y if kind in ("y_up", "y_down") else y
        valid = (there >= 0) & (there < n_z)
        return jnp.where(valid, 2 * there + side, -1)

    have = {"up": ups, "down": downs, "y_up": y_ups, "y_down": y_downs}
    stages = [[("up", 0), ("y_up", 0)]]
    for k in range(1, n_z + 1):
        stage = [("up", k), ("down", k)] if k < n_z else []
        stages.append(stage + ([("y_up", k - 1), ("y_down", k - 1)] if k > 1 else []))
    parts, carry = {}, ()
    for stage in stages:
        rows = jnp.stack([named(*name) for name in stage]).astype(jnp.int32)
        dqs, carry = stage_grads(
            rows, counts, entries, key, value, [have[kind][k] for kind, k in stage], carry
        )
        parts.update(zip(stage, dqs))

    def add(*terms):
        return sum(x.astype(jnp.float32) for x in terms)

    low = jnp.bfloat16
    up, down = None, None
    for k in range(n_z - 1, 0, -1):
        up_terms = [parts[("up", k)], swap(parts[("y_up", k)], k, n_z)]
        down_terms = [parts[("down", k)], swap(parts[("y_down", k)], 0, n_z - k)]
        if up is not None:
            up_terms.append(up)
            down_terms.append(down)
        up = shift(add(*up_terms).astype(low), -1, k, n_z)
        down = shift(add(*down_terms).astype(low), 1, 0, n_z - k)
    dq = add(parts[("up", 0)], swap(parts[("y_up", 0)], 0, n_z), up, down).astype(low)
    dk, dv = carry
    return (
        jnp.transpose(dq, (0, 2, 1)).reshape(tokens, width),
        (dk * SCALE).astype(low).reshape(tokens, width),
        dv.astype(low).reshape(tokens, width),
    )


def solution(mesh):
    tokens = P(("groups", "row"), "col")
    return jax.shard_map(
        body,
        mesh=mesh,
        in_specs=(tokens,) * 6 + (P("groups"), P("groups", None), P("groups")),
        out_specs=(tokens,) * 3,
        check_vma=False,
    )
```

time: 313 us -> 181 us (0.58)
  waiting for transfers between devices: 246 us -> 90.5 us
  starting transfers between devices: 0.16 us -> 46.3 us
  between operations: 13.9 us -> 1.15 us
  Pallas kernels: 38.6 us -> 30.9 us
    all_gather x2 -> x0, waiting for transfers between devices: 128 us -> none  [body(): lax.all_gather(load, 'row', axis=0, tiled=True)]
    reduce_scatter x2 -> x0, waiting for transfers between devices: 117 us -> none  [body(): dq = lax.psum_scatter(dq, 'row', scatter_dimension=0, tiled=True)]
    ppermute x0 -> x26, waiting for transfers between devices: none -> 90.5 us  [the longest x12 54.3 us: shift(): return lax.ppermute(x, 'row', pairs)]
    ppermute x0 -> x26, starting transfers between devices: none -> 46.3 us  [the longest x12 23.5 us: shift(): return lax.ppermute(x, 'row', pairs)]
    pallas_call x2 -> x6, Pallas kernels: 38.6 us -> 30.9 us  [the longest x5 28 us: stage_grads(): pl.pallas_call(functools.partial(grads_kernel, n_load, not carry), out_sh...]
    concatenate x5 -> x2, other arithmetic: 3.9 us -> 0.25 us  [the longest x1 0.24 us: body(): jnp.concatenate([queries.reshape(per_row, BLOCK, width), grad_out.reshape...]
  transfers between devices with their start and end apart: 4 -> 26, of which waited for: 4 -> 9; matrix products, arithmetic and copies ran while one was open for 2% -> 2% of each run, Pallas kernels for 12% -> 16%
where the time goes in v2:
time: 181 us; the launch traced here: 180 us
  waiting for transfers between devices  90.5 us (50%)
  starting transfers between devices  46.3 us (26%)
  Pallas kernels  30.9 us (17%)
  local copies, waits for them, and re-layouts  7.36 us (4%)
  other arithmetic  3.95 us (2%)
    ppermute x12, waiting for transfers between devices, shift(): return lax.ppermute(x, 'row', pairs)  54.3 us
    ppermute x14, waiting for transfers between devices, swap(): return lax.ppermute(x, 'row', pairs)  36.2 us
    pallas_call x5, Pallas kernels, stage_grads(): pl.pallas_call(functools.partial(grads_kernel, n_load, not carry), out_sh...  28 us
    ppermute x12, starting transfers between devices, shift(): return lax.ppermute(x, 'row', pairs)  23.5 us
    ppermute x14, starting transfers between devices, swap(): return lax.ppermute(x, 'row', pairs)  22.8 us
    unnamed x29, local copies, waits for them, and re-layouts  5.62 us
  transfers between devices with their start and end apart: 26, of which 9 were waited for; matrix products, arithmetic and copies ran while one was open for 2% of the time, Pallas kernels for 16%

profile of v2, /device:TPU:10, one launch (start us, length us, event | category | flops | bytes accessed | tf_op | source)
XLA Modules:
  0.0 180.1 jit_solution(11131519678657571154)
XLA Ops:
  0.6 1.3 copy.13
  3.4 3.5 %collective-permute-start.2 = (bf16[4,528,256]{2,1,0:T(8,128)(2,1)S(1)}, bf16[4,528,256]{2,1,0:T(8,128)(2,1)S(1)}, u32[]{:S(2)}, u32[]{:S(2)}) collective-permute-start(bf16[4,528,256]{2,1,0:T(8,128)(2,1)S(1)} %maximum_maximum_fusion.refs_0_), channel_id=1, source_target_pairs={{0,4},{2,6},{4,8},{6,10},{8,12},{10,14},{1,5},{3,7},{5,9},{7,11},{... | collective-permute-start | bytes 3244040 | tf_op jit(solution)/shard_map/ppermute | solution.py:178
  6.9 2.4 %collective-permute-start.3 = (bf16[4,528,256]{2,1,0:T(8,128)(2,1)S(1)}, bf16[4,528,256]{2,1,0:T(8,128)(2,1)S(1)}, u32[]{:S(2)}, u32[]{:S(2)}) collective-permute-start(bf16[4,528,256]{2,1,0:T(8,128)(2,1)S(1)} %maximum_maximum_fusion.refs_0_), channel_id=1, source_target_pairs={{4,0},{6,2},{8,4},{10,6},{12,8},{14,10},{5,1},{7,3},{9,5},{11,7},{... | collective-permute-start | bytes 3244040 | tf_op jit(solution)/shard_map/ppermute | solution.py:178
  9.3 1.6 collective-permute-start
  11.7 2.8 %shard_map.112 = (s32[8]{0:T(128)}, s32[256]{0:T(256)}) custom-call(s32[1]{0:T(128)} %bitcast.2.here_ref, s32[32]{0:T(128)} %slot_ref.1, s32[256]{0:T(256)} %reshape.40.near_ref, s32[32]{0:T(128)} %live_ref.1), custom_call_target="tpu_custom_call" | custom-call | tf_op jit(solution)/shard_map/pallas_call | solution.py:58
  14.9 16.0 %collective-permute-done.2.refs_0_ = bf16[4,528,256]{2,1,0:T(8,128)(2,1)S(1)} collective-permute-done((bf16[4,528,256]{2,1,0:T(8,128)(2,1)S(1)}, bf16[4,528,256]{2,1,0:T(8,128)(2,1)S(1)}, u32[]{:S(2)}, u32[]{:S(2)}) %collective-permute-start.2) | collective-permute-done | bytes 1081376 | tf_op jit(solution)/shard_map/ppermute | solution.py:178
  30.9 3.5 %collective-permute-start.4 = (bf16[4,528,256]{2,1,0:T(8,128)(2,1)S(1)}, bf16[4,528,256]{2,1,0:T(8,128)(2,1)S(1)}, u32[]{:S(2)}, u32[]{:S(2)}) collective-permute-start(bf16[4,528,256]{2,1,0:T(8,128)(2,1)S(1)} %collective-permute-done.2.refs_0_), channel_id=1, source_target_pairs={{4,8},{6,10},{8,12},{10,14},{5,9},{7,11},{9,13},{11,15},{20,24},{2... | collective-permute-start | bytes 3244040 | tf_op jit(solution)/shard_map/ppermute | solution.py:178
  34.5 3.4 %collective-permute-start.6 = (bf16[4,528,256]{2,1,0:T(8,128)(2,1)S(1)}, bf16[4,528,256]{2,1,0:T(8,128)(2,1)S(1)}, u32[]{:S(2)}, u32[]{:S(2)}) collective-permute-start(bf16[4,528,256]{2,1,0:T(8,128)(2,1)S(1)} %collective-permute-done.2.refs_0_), channel_id=1, source_target_pairs={{4,6},{6,4},{8,10},{10,8},{12,14},{14,12},{5,7},{7,5},{9,11},{11,9... | collective-permute-start | bytes 3244040 | tf_op jit(solution)/shard_map/ppermute | solution.py:174
  37.9 1.9 %collective-permute-start.5 = (bf16[4,528,256]{2,1,0:T(8,128)(2,1)S(1)}, bf16[4,528,256]{2,1,0:T(8,128)(2,1)S(1)}, u32[]{:S(2)}, u32[]{:S(2)}) collective-permute-start(bf16[4,528,256]{2,1,0:T(8,128)(2,1)S(1)} %collective-permute-done.3.refs_1_), channel_id=1, source_target_pairs={{4,0},{6,2},{8,4},{10,6},{5,1},{7,3},{9,5},{11,7},{20,16},{22,18},... | collective-permute-start | bytes 3244040 | tf_op jit(solution)/shard_map/ppermute | solution.py:178
  39.8 2.4 %collective-permute-start.7 = (bf16[4,528,256]{2,1,0:T(8,128)(2,1)S(1)}, bf16[4,528,256]{2,1,0:T(8,128)(2,1)S(1)}, u32[]{:S(2)}, u32[]{:S(2)}) collective-permute-start(bf16[4,528,256]{2,1,0:T(8,128)(2,1)S(1)} %collective-permute-done.3.refs_1_), channel_id=1, source_target_pairs={{0,2},{2,0},{4,6},{6,4},{8,10},{10,8},{1,3},{3,1},{5,7},{7,5},{9,1... | collective-permute-start | bytes 3244040 | tf_op jit(solution)/shard_map/ppermute | solution.py:174
  42.3 1.0 copy-done
  43.3 1.0 copy-done.2
  44.4 0.7 copy-done.6
  45.6 7.9 %shard_map.113 = (bf16[4,256,256]{2,1,0:T(8,128)(2,1)S(1)}, bf16[4,256,256]{2,1,0:T(8,128)(2,1)S(1)}, f32[4,256,256]{2,1,0:T(8,128)S(1)}, f32[4,256,256]{2,1,0:T(8,128)S(1)}) custom-call(s32[2]{0:T(128)S(1)} %pad_add_fusion.row_ref, s32[8]{0:T(128)S(1)} %copy-done.7, s32[256]{0:T(256)S(1)} %copy-done.6, bf16[4,256,256]{2,1,0:T(8,128)(2,1)S(1)} %bitcast.29, ...), custom_call_target="tpu_custom_call" | custom-call | flops 6000000000 | bytes 4194304 | tf_op jit(solution)/shard_map/pallas_call | solution.py:144
  53.5 7.1 %shard_map.114 = (bf16[4,256,256]{2,1,0:T(8,128)(2,1)S(1)}, bf16[4,256,256]{2,1,0:T(8,128)(2,1)S(1)}, f32[4,256,256]{2,1,0:T(8,128)S(1)}, f32[4,256,256]{2,1,0:T(8,128)S(1)}) custom-call(s32[2]{0:T(128)S(1)} %pad_add_fusion.1.row_ref, s32[8]{0:T(128)S(1)} %copy-done.7, s32[256]{0:T(256)S(1)} %copy-done.6, bf16[4,256,256]{2,1,0:T(8,128)(2,1)S(1)} %bitcast.30, ...), custom_call_target="tpu_custom_call" | custom-call | flops 6000000000 | bytes 4194304 | tf_op jit(solution)/shard_map/pallas_call | solution.py:144
  60.6 0.7 collective-permute-start.9
  61.4 0.7 collective-permute-start.11
  62.1 2.0 %collective-permute-done.5.refs_1_ = bf16[4,528,256]{2,1,0:T(8,128)(2,1)S(1)} collective-permute-done((bf16[4,528,256]{2,1,0:T(8,128)(2,1)S(1)}, bf16[4,528,256]{2,1,0:T(8,128)(2,1)S(1)}, u32[]{:S(2)}, u32[]{:S(2)}) %collective-permute-start.5) | collective-permute-done | bytes 1081376 | tf_op jit(solution)/shard_map/ppermute | solution.py:178
  64.1 2.3 %collective-permute-start.10 = (bf16[4,528,256]{2,1,0:T(8,128)(2,1)S(1)}, bf16[4,528,256]{2,1,0:T(8,128)(2,1)S(1)}, u32[]{:S(2)}, u32[]{:S(2)}) collective-permute-start(bf16[4,528,256]{2,1,0:T(8,128)(2,1)S(1)} %collective-permute-done.5.refs_1_), channel_id=1, source_target_pairs={{4,0},{6,2},{5,1},{7,3},{20,16},{22,18},{21,17},{23,19}} | collective-permute-start | bytes 3244040 | tf_op jit(solution)/shard_map/ppermute | solution.py:178
  66.4 2.4 %collective-permute-start.12 = (bf16[4,528,256]{2,1,0:T(8,128)(2,1)S(1)}, bf16[4,528,256]{2,1,0:T(8,128)(2,1)S(1)}, u32[]{:S(2)}, u32[]{:S(2)}) collective-permute-start(bf16[4,528,256]{2,1,0:T(8,128)(2,1)S(1)} %collective-permute-done.5.refs_1_), channel_id=1, source_target_pairs={{0,2},{2,0},{4,6},{6,4},{1,3},{3,1},{5,7},{7,5},{16,18},{18,16},{2... | collective-permute-start | bytes 3244040 | tf_op jit(solution)/shard_map/ppermute | solution.py:174
  68.8 17.6 %collective-permute-done.7.refs_3_ = bf16[4,528,256]{2,1,0:T(8,128)(2,1)S(1)} collective-permute-done((bf16[4,528,256]{2,1,0:T(8,128)(2,1)S(1)}, bf16[4,528,256]{2,1,0:T(8,128)(2,1)S(1)}, u32[]{:S(2)}, u32[]{:S(2)}) %collective-permute-start.7) | collective-permute-done | bytes 1081376 | tf_op jit(solution)/shard_map/ppermute | solution.py:174
  86.3 6.4 %shard_map.115 = (bf16[4,256,256]{2,1,0:T(8,128)(2,1)S(1)}, bf16[4,256,256]{2,1,0:T(8,128)(2,1)S(1)}, bf16[4,256,256]{2,1,0:T(8,128)(2,1)S(1)}, bf16[4,256,256]{...) custom-call(s32[4]{0:T(128)S(1)} %pad_add_fusion.2.row_ref, s32[8]{0:T(128)S(1)} %copy-done.7, ...), custom_call_target="tpu_custom_call" | custom-call | flops 12000000000 | bytes 8388608 | tf_op jit(solution)/shard_map/pallas_call | solution.py:144
  92.8 0.9 collective-permute-start.14
  93.7 0.7 collective-permute-start.15
  94.4 12.8 %collective-permute-done.12.refs_3_ = bf16[4,528,256]{2,1,0:T(8,128)(2,1)S(1)} collective-permute-done((bf16[4,528,256]{2,1,0:T(8,128)(2,1)S(1)}, bf16[4,528,256]{2,1,0:T(8,128)(2,1)S(1)}, u32[]{:S(2)}, u32[]{:S(2)}) %collective-permute-start.12) | collective-permute-done | bytes 1081376 | tf_op jit(solution)/shard_map/ppermute | solution.py:174
  107.3 4.7 %shard_map.116 = (bf16[4,256,256]{2,1,0:T(8,128)(2,1)S(1)}, bf16[4,256,256]{2,1,0:T(8,128)(2,1)S(1)}, bf16[4,256,256]{2,1,0:T(8,128)(2,1)S(1)}, bf16[4,256,256]{...) custom-call(s32[4]{0:T(128)S(1)} %pad_add_fusion.3.row_ref, s32[8]{0:T(128)S(1)} %copy-done.7, ...), custom_call_target="tpu_custom_call" | custom-call | flops 12000000000 | bytes 8388608 | tf_op jit(solution)/shard_map/pallas_call | solution.py:144
  112.0 1.9 %shard_map.117 = (bf16[4,256,256]{2,1,0:T(8,128)(2,1)S(1)}, bf16[4,256,256]{2,1,0:T(8,128)(2,1)S(1)}, f32[4,256,256]{2,1,0:T(8,128)S(1)}, f32[4,256,256]{2,1,0:T(8,128)S(1)}) custom-call(s32[2]{0:T(128)S(1)} %pad_add_fusion.4.row_ref, s32[8]{0:T(128)S(1)} %copy-done.7, s32[256]{0:T(256)S(1)} %copy-done.6, bf16[4,256,256]{2,1,0:T(8,128)(2,1)S(1)} %bitcast.33, ...), custom_call_target="tpu_custom_call" | custom-call | flops 6000000000 | bytes 4194304 | tf_op jit(solution)/shard_map/pallas_call | solution.py:144
  114.0 0.7 collective-permute-start.16
  114.7 0.7 collective-permute-start.22
  115.4 0.7 collective-permute-start.13
  116.2 0.7 collective-permute-start.17
  116.9 1.9 %collective-permute-start.21 = (bf16[4,256,256]{2,1,0:T(8,128)(2,1)S(1)}, bf16[4,256,256]{2,1,0:T(8,128)(2,1)S(1)}, u32[]{:S(2)}, u32[]{:S(2)}) collective-permute-start(bf16[4,256,256]{2,1,0:T(8,128)(2,1)S(1)} %get-tuple-element.50), channel_id=1, source_target_pairs={{0,2},{2,0},{4,6},{6,4},{1,3},{3,1},{5,7},{7,5},{16,18},{18,16},{2... | collective-permute-start | bytes 1572872 | tf_op jit(solution)/shard_map/ppermute | solution.py:174
  119.0 1.3 collective-permute-start.23
  120.3 3.9 %collective-permute-start.8 = (bf16[4,256,256]{2,1,0:T(8,128)(2,1)S(1)}, bf16[4,256,256]{2,1,0:T(8,128)(2,1)S(1)}, u32[]{:S(2)}, u32[]{:S(2)}) collective-permute-start(bf16[4,256,256]{2,1,0:T(8,128)(2,1)S(1)} %get-tuple-element.38), channel_id=1, source_target_pairs={{4,6},{6,4},{8,10},{10,8},{12,14},{14,12},{5,7},{7,5},{9,11},{11,9... | collective-permute-start | bytes 1572872 | tf_op jit(solution)/shard_map/ppermute | solution.py:174
  124.2 1.9 %collective-permute-start.20 = (bf16[4,256,256]{2,1,0:T(8,128)(2,1)S(1)}, bf16[4,256,256]{2,1,0:T(8,128)(2,1)S(1)}, u32[]{:S(2)}, u32[]{:S(2)}) collective-permute-start(bf16[4,256,256]{2,1,0:T(8,128)(2,1)S(1)} %get-tuple-element.48), channel_id=1, source_target_pairs={{0,2},{2,0},{4,6},{6,4},{8,10},{10,8},{1,3},{3,1},{5,7},{7,5},{9,1... | collective-permute-start | bytes 1572872 | tf_op jit(solution)/shard_map/ppermute | solution.py:174
  126.4 1.4 collective-permute-start.18
  127.8 5.8 %collective-permute-done.21 = bf16[4,256,256]{2,1,0:T(8,128)(2,1)S(1)} collective-permute-done((bf16[4,256,256]{2,1,0:T(8,128)(2,1)S(1)}, bf16[4,256,256]{2,1,0:T(8,128)(2,1)S(1)}, u32[]{:S(2)}, u32[]{:S(2)}) %collective-permute-start.21) | collective-permute-done | bytes 524320 | tf_op jit(solution)/shard_map/ppermute | solution.py:174
  133.7 17.2 %collective-permute-done.23 = bf16[4,256,256]{2,1,0:T(8,128)(2,1)S(1)} collective-permute-done((bf16[4,256,256]{2,1,0:T(8,128)(2,1)S(1)}, bf16[4,256,256]{2,1,0:T(8,128)(2,1)S(1)}, u32[]{:S(2)}, u32[]{:S(2)}) %collective-permute-start.23) | collective-permute-done | bytes 524320 | tf_op jit(solution)/shard_map/ppermute | solution.py:178
  151.1 1.9 %collective-permute-start.24 = (bf16[4,256,256]{2,1,0:T(8,128)(2,1)S(1)}, bf16[4,256,256]{2,1,0:T(8,128)(2,1)S(1)}, u32[]{:S(2)}, u32[]{:S(2)}) collective-permute-start(bf16[4,256,256]{2,1,0:T(8,128)(2,1)S(1)} %add_convert_fusion.2), channel_id=1, source_target_pairs={{0,4},{2,6},{4,8},{6,10},{1,5},{3,7},{5,9},{7,11},{16,20},{18,22},... | collective-permute-start | bytes 1572872 | tf_op jit(solution)/shard_map/ppermute | solution.py:178
  153.0 0.8 collective-permute-start.1
  153.8 5.1 %collective-permute-done.18 = bf16[4,256,256]{2,1,0:T(8,128)(2,1)S(1)} collective-permute-done((bf16[4,256,256]{2,1,0:T(8,128)(2,1)S(1)}, bf16[4,256,256]{2,1,0:T(8,128)(2,1)S(1)}, u32[]{:S(2)}, u32[]{:S(2)}) %collective-permute-start.18) | collective-permute-done | bytes 524320 | tf_op jit(solution)/shard_map/ppermute | solution.py:178
  159.1 1.9 %collective-permute-start.19 = (bf16[4,256,256]{2,1,0:T(8,128)(2,1)S(1)}, bf16[4,256,256]{2,1,0:T(8,128)(2,1)S(1)}, u32[]{:S(2)}, u32[]{:S(2)}) collective-permute-start(bf16[4,256,256]{2,1,0:T(8,128)(2,1)S(1)} %add_convert_fusion.4), channel_id=1, source_target_pairs={{4,0},{6,2},{8,4},{10,6},{12,8},{14,10},{5,1},{7,3},{9,5},{11,7},{... | collective-permute-start | bytes 1572872 | tf_op jit(solution)/shard_map/ppermute | solution.py:178
  161.1 6.5 %collective-permute-done.24 = bf16[4,256,256]{2,1,0:T(8,128)(2,1)S(1)} collective-permute-done((bf16[4,256,256]{2,1,0:T(8,128)(2,1)S(1)}, bf16[4,256,256]{2,1,0:T(8,128)(2,1)S(1)}, u32[]{:S(2)}, u32[]{:S(2)}) %collective-permute-start.24) | collective-permute-done | bytes 524320 | tf_op jit(solution)/shard_map/ppermute | solution.py:178
  167.8 1.9 %collective-permute-start.25 = (bf16[4,256,256]{2,1,0:T(8,128)(2,1)S(1)}, bf16[4,256,256]{2,1,0:T(8,128)(2,1)S(1)}, u32[]{:S(2)}, u32[]{:S(2)}) collective-permute-start(bf16[4,256,256]{2,1,0:T(8,128)(2,1)S(1)} %add_convert_fusion.1), channel_id=1, source_target_pairs={{0,4},{2,6},{4,8},{6,10},{8,12},{10,14},{1,5},{3,7},{5,9},{7,11},{... | collective-permute-start | bytes 1572872 | tf_op jit(solution)/shard_map/ppermute | solution.py:178
  169.7 0.8 convert_element_type.127
  170.6 0.9 multiply_convert_fusion
  171.5 7.4 %collective-permute-done.25 = bf16[4,256,256]{2,1,0:T(8,128)(2,1)S(1)} collective-permute-done((bf16[4,256,256]{2,1,0:T(8,128)(2,1)S(1)}, bf16[4,256,256]{2,1,0:T(8,128)(2,1)S(1)}, u32[]{:S(2)}, u32[]{:S(2)}) %collective-permute-start.25) | collective-permute-done | bytes 524320 | tf_op jit(solution)/shard_map/ppermute | solution.py:178
  179.1 1.0 copy.15
  (60 shorter events, 4.6 us)
Async XLA Ops:
  0.6 1.3 copy-start.10
  2.0 0.7 copy-start.11
  2.0 1.0 copy-start.8
  2.0 1.2 copy-start.9
  3.2 7.8 %copy-start.12 = (s32[32,8]{0,1:T(8,128)S(1)}, s32[32,8]{0,1:T(8,128)}, u32[]{:S(2)}) copy-start(s32[32,8]{0,1:T(8,128)} %param.16) | copy-start | bytes 3076
  3.4 27.5 %collective-permute-start.2 = (bf16[4,528,256]{2,1,0:T(8,128)(2,1)S(1)}, bf16[4,528,256]{2,1,0:T(8,128)(2,1)S(1)}, u32[]{:S(2)}, u32[]{:S(2)}) collective-permute-start(bf16[4,528,256]{2,1,0:T(8,128)(2,1)S(1)} %maximum_maximum_fusion.refs_0_), channel_id=1, source_target_pairs={{0,4},{2,6},{4,8},{6,10},{8,12},{10,14},{1,5},{3,7},{5,9},{7,11},{... | collective-permute-start | bytes 3244040 | tf_op jit(solution)/shard_map/ppermute | solution.py:178
  6.9 31.0 %collective-permute-start.3 = (bf16[4,528,256]{2,1,0:T(8,128)(2,1)S(1)}, bf16[4,528,256]{2,1,0:T(8,128)(2,1)S(1)}, u32[]{:S(2)}, u32[]{:S(2)}) collective-permute-start(bf16[4,528,256]{2,1,0:T(8,128)(2,1)S(1)} %maximum_maximum_fusion.refs_0_), channel_id=1, source_target_pairs={{4,0},{6,2},{8,4},{10,6},{12,8},{14,10},{5,1},{7,3},{9,5},{11,7},{... | collective-permute-start | bytes 3244040 | tf_op jit(solution)/shard_map/ppermute | solution.py:178
  9.3 32.9 %collective-permute-start = (bf16[4,528,256]{2,1,0:T(8,128)(2,1)S(1)}, bf16[4,528,256]{2,1,0:T(8,128)(2,1)}, u32[]{:S(2)}, u32[]{:S(2)}) collective-permute-start(bf16[4,528,256]{2,1,0:T(8,128)(2,1)S(1)} %maximum_maximum_fusion.refs_0_), channel_id=1, source_target_pairs={{0,2},{2,0},{4,6},{6,4},{8,10},{10,8},{12,14},{14,12},{1,3},{3,1},... | collective-permute-start | bytes 3244040 | tf_op jit(solution)/shard_map/ppermute | solution.py:174
  30.9 29.7 %collective-permute-start.4 = (bf16[4,528,256]{2,1,0:T(8,128)(2,1)S(1)}, bf16[4,528,256]{2,1,0:T(8,128)(2,1)S(1)}, u32[]{:S(2)}, u32[]{:S(2)}) collective-permute-start(bf16[4,528,256]{2,1,0:T(8,128)(2,1)S(1)} %collective-permute-done.2.refs_0_), channel_id=1, source_target_pairs={{4,8},{6,10},{8,12},{10,14},{5,9},{7,11},{9,13},{11,15},{20,24},{2... | collective-permute-start | bytes 3244040 | tf_op jit(solution)/shard_map/ppermute | solution.py:178
  34.5 31.9 %collective-permute-start.6 = (bf16[4,528,256]{2,1,0:T(8,128)(2,1)S(1)}, bf16[4,528,256]{2,1,0:T(8,128)(2,1)S(1)}, u32[]{:S(2)}, u32[]{:S(2)}) collective-permute-start(bf16[4,528,256]{2,1,0:T(8,128)(2,1)S(1)} %collective-permute-done.2.refs_0_), channel_id=1, source_target_pairs={{4,6},{6,4},{8,10},{10,8},{12,14},{14,12},{5,7},{7,5},{9,11},{11,9... | collective-permute-start | bytes 3244040 | tf_op jit(solution)/shard_map/ppermute | solution.py:174
  37.9 26.2 %collective-permute-start.5 = (bf16[4,528,256]{2,1,0:T(8,128)(2,1)S(1)}, bf16[4,528,256]{2,1,0:T(8,128)(2,1)S(1)}, u32[]{:S(2)}, u32[]{:S(2)}) collective-permute-start(bf16[4,528,256]{2,1,0:T(8,128)(2,1)S(1)} %collective-permute-done.3.refs_1_), channel_id=1, source_target_pairs={{4,0},{6,2},{8,4},{10,6},{5,1},{7,3},{9,5},{11,7},{20,16},{22,18},... | collective-permute-start | bytes 3244040 | tf_op jit(solution)/shard_map/ppermute | solution.py:178
  39.8 46.5 %collective-permute-start.7 = (bf16[4,528,256]{2,1,0:T(8,128)(2,1)S(1)}, bf16[4,528,256]{2,1,0:T(8,128)(2,1)S(1)}, u32[]{:S(2)}, u32[]{:S(2)}) collective-permute-start(bf16[4,528,256]{2,1,0:T(8,128)(2,1)S(1)} %collective-permute-done.3.refs_1_), channel_id=1, source_target_pairs={{0,2},{2,0},{4,6},{6,4},{8,10},{10,8},{1,3},{3,1},{5,7},{7,5},{9,1... | collective-permute-start | bytes 3244040 | tf_op jit(solution)/shard_map/ppermute | solution.py:174
  42.3 1.0 copy-start
  43.3 1.0 copy-start.2
  44.4 0.7 copy-start.6
  45.0 0.6 copy-start.7
  45.6 7.9 %copy-start.1 = (bf16[1024,256]{1,0:T(8,128)(2,1)S(1)}, bf16[1024,256]{1,0:T(8,128)(2,1)}, u32[]{:S(2)}) copy-start(bf16[1024,256]{1,0:T(8,128)(2,1)} %param.10) | copy-start | bytes 1572868
  53.5 7.1 %copy-start.4 = (bf16[4,256,256]{2,1,0:T(8,128)(2,1)}, bf16[4,256,256]{2,1,0:T(8,128)(2,1)S(1)}, u32[]{:S(2)}) copy-start(bf16[4,256,256]{2,1,0:T(8,128)(2,1)S(1)} %get-tuple-element.32) | copy-start | bytes 1572868
  53.5 32.8 %copy-start.3 = (bf16[1024,256]{1,0:T(8,128)(2,1)S(1)}, bf16[1024,256]{1,0:T(8,128)(2,1)}, u32[]{:S(2)}) copy-start(bf16[1024,256]{1,0:T(8,128)(2,1)} %param.11) | copy-start | bytes 1572868
  60.6 32.1 %collective-permute-start.9 = (bf16[4,528,256]{2,1,0:T(8,128)(2,1)S(1)}, bf16[4,528,256]{2,1,0:T(8,128)(2,1)S(1)}, u32[]{:S(2)}, u32[]{:S(2)}) collective-permute-start(bf16[4,528,256]{2,1,0:T(8,128)(2,1)S(1)} %collective-permute-done.4.refs_0_), channel_id=1, source_target_pairs={{8,12},{10,14},{9,13},{11,15},{24,28},{26,30},{25,29},{27,31}} | collective-permute-start | bytes 3244040 | tf_op jit(solution)/shard_map/ppermute | solution.py:178
  61.4 33.1 %collective-permute-start.11 = (bf16[4,528,256]{2,1,0:T(8,128)(2,1)S(1)}, bf16[4,528,256]{2,1,0:T(8,128)(2,1)S(1)}, u32[]{:S(2)}, u32[]{:S(2)}) collective-permute-start(bf16[4,528,256]{2,1,0:T(8,128)(2,1)S(1)} %collective-permute-done.4.refs_0_), channel_id=1, source_target_pairs={{8,10},{10,8},{12,14},{14,12},{9,11},{11,9},{13,15},{15,13},{24,26... | collective-permute-start | bytes 3244040 | tf_op jit(solution)/shard_map/ppermute | solution.py:174
  64.1 29.6 %collective-permute-start.10 = (bf16[4,528,256]{2,1,0:T(8,128)(2,1)S(1)}, bf16[4,528,256]{2,1,0:T(8,128)(2,1)S(1)}, u32[]{:S(2)}, u32[]{:S(2)}) collective-permute-start(bf16[4,528,256]{2,1,0:T(8,128)(2,1)S(1)} %collective-permute-done.5.refs_1_), channel_id=1, source_target_pairs={{4,0},{6,2},{5,1},{7,3},{20,16},{22,18},{21,17},{23,19}} | collective-permute-start | bytes 3244040 | tf_op jit(solution)/shard_map/ppermute | solution.py:178
  66.4 40.9 %collective-permute-start.12 = (bf16[4,528,256]{2,1,0:T(8,128)(2,1)S(1)}, bf16[4,528,256]{2,1,0:T(8,128)(2,1)S(1)}, u32[]{:S(2)}, u32[]{:S(2)}) collective-permute-start(bf16[4,528,256]{2,1,0:T(8,128)(2,1)S(1)} %collective-permute-done.5.refs_1_), channel_id=1, source_target_pairs={{0,2},{2,0},{4,6},{6,4},{1,3},{3,1},{5,7},{7,5},{16,18},{18,16},{2... | collective-permute-start | bytes 3244040 | tf_op jit(solution)/shard_map/ppermute | solution.py:174
  92.8 19.2 %collective-permute-start.14 = (bf16[4,528,256]{2,1,0:T(8,128)(2,1)S(1)}, bf16[4,528,256]{2,1,0:T(8,128)(2,1)S(1)}, u32[]{:S(2)}, u32[]{:S(2)}) collective-permute-start(bf16[4,528,256]{2,1,0:T(8,128)(2,1)S(1)} %collective-permute-done.9.refs_0_), channel_id=1, source_target_pairs={{12,14},{14,12},{13,15},{15,13},{28,30},{30,28},{29,31},{31,29}} | collective-permute-start | bytes 3244040 | tf_op jit(solution)/shard_map/ppermute | solution.py:174
  93.7 18.3 %collective-permute-start.15 = (bf16[4,528,256]{2,1,0:T(8,128)(2,1)S(1)}, bf16[4,528,256]{2,1,0:T(8,128)(2,1)S(1)}, u32[]{:S(2)}, u32[]{:S(2)}) collective-permute-start(bf16[4,528,256]{2,1,0:T(8,128)(2,1)S(1)} %collective-permute-done.10.refs_1_), channel_id=1, source_target_pairs={{0,2},{2,0},{1,3},{3,1},{16,18},{18,16},{17,19},{19,17}} | collective-permute-start | bytes 3244040 | tf_op jit(solution)/shard_map/ppermute | solution.py:174
  114.0 2.1 %collective-permute-start.16 = (bf16[4,256,256]{2,1,0:T(8,128)(2,1)S(1)}, bf16[4,256,256]{2,1,0:T(8,128)(2,1)S(1)}, u32[]{:S(2)}, u32[]{:S(2)}) collective-permute-start(bf16[4,256,256]{2,1,0:T(8,128)(2,1)S(1)} %get-tuple-element.46), channel_id=1, source_target_pairs={{12,14},{14,12},{13,15},{15,13},{28,30},{30,28},{29,31},{31,29}} | collective-permute-start | bytes 1572872 | tf_op jit(solution)/shard_map/ppermute | solution.py:174
  114.7 4.2 %collective-permute-start.22 = (bf16[4,256,256]{2,1,0:T(8,128)(2,1)S(1)}, bf16[4,256,256]{2,1,0:T(8,128)(2,1)S(1)}, u32[]{:S(2)}, u32[]{:S(2)}) collective-permute-start(bf16[4,256,256]{2,1,0:T(8,128)(2,1)S(1)} %get-tuple-element.52), channel_id=1, source_target_pairs={{0,2},{2,0},{1,3},{3,1},{16,18},{18,16},{17,19},{19,17}} | collective-permute-start | bytes 1572872 | tf_op jit(solution)/shard_map/ppermute | solution.py:174
  115.4 8.9 %collective-permute-start.13 = (bf16[4,256,256]{2,1,0:T(8,128)(2,1)S(1)}, bf16[4,256,256]{2,1,0:T(8,128)(2,1)S(1)}, u32[]{:S(2)}, u32[]{:S(2)}) collective-permute-start(bf16[4,256,256]{2,1,0:T(8,128)(2,1)S(1)} %get-tuple-element.42), channel_id=1, source_target_pairs={{8,10},{10,8},{12,14},{14,12},{9,11},{11,9},{13,15},{15,13},{24,26... | collective-permute-start | bytes 1572872 | tf_op jit(solution)/shard_map/ppermute | solution.py:174
  116.2 10.0 %collective-permute-start.17 = (bf16[4,256,256]{2,1,0:T(8,128)(2,1)S(1)}, bf16[4,256,256]{2,1,0:T(8,128)(2,1)S(1)}, u32[]{:S(2)}, u32[]{:S(2)}) collective-permute-start(bf16[4,256,256]{2,1,0:T(8,128)(2,1)S(1)} %add_convert_fusion.6), channel_id=1, source_target_pairs={{12,8},{14,10},{13,9},{15,11},{28,24},{30,26},{29,25},{31,27}} | collective-permute-start | bytes 1572872 | tf_op jit(solution)/shard_map/ppermute | solution.py:178
  116.9 16.8 %collective-permute-start.21 = (bf16[4,256,256]{2,1,0:T(8,128)(2,1)S(1)}, bf16[4,256,256]{2,1,0:T(8,128)(2,1)S(1)}, u32[]{:S(2)}, u32[]{:S(2)}) collective-permute-start(bf16[4,256,256]{2,1,0:T(8,128)(2,1)S(1)} %get-tuple-element.50), channel_id=1, source_target_pairs={{0,2},{2,0},{4,6},{6,4},{1,3},{3,1},{5,7},{7,5},{16,18},{18,16},{2... | collective-permute-start | bytes 1572872 | tf_op jit(solution)/shard_map/ppermute | solution.py:174
  119.0 31.9 %collective-permute-start.23 = (bf16[4,256,256]{2,1,0:T(8,128)(2,1)S(1)}, bf16[4,256,256]{2,1,0:T(8,128)(2,1)S(1)}, u32[]{:S(2)}, u32[]{:S(2)}) collective-permute-start(bf16[4,256,256]{2,1,0:T(8,128)(2,1)S(1)} %add_convert_fusion.3), channel_id=1, source_target_pairs={{0,4},{2,6},{1,5},{3,7},{16,20},{18,22},{17,21},{19,23}} | collective-permute-start | bytes 1572872 | tf_op jit(solution)/shard_map/ppermute | solution.py:178
  120.3 33.5 %collective-permute-start.8 = (bf16[4,256,256]{2,1,0:T(8,128)(2,1)S(1)}, bf16[4,256,256]{2,1,0:T(8,128)(2,1)S(1)}, u32[]{:S(2)}, u32[]{:S(2)}) collective-permute-start(bf16[4,256,256]{2,1,0:T(8,128)(2,1)S(1)} %get-tuple-element.38), channel_id=1, source_target_pairs={{4,6},{6,4},{8,10},{10,8},{12,14},{14,12},{5,7},{7,5},{9,11},{11,9... | collective-permute-start | bytes 1572872 | tf_op jit(solution)/shard_map/ppermute | solution.py:174
  124.2 36.8 %collective-permute-start.20 = (bf16[4,256,256]{2,1,0:T(8,128)(2,1)S(1)}, bf16[4,256,256]{2,1,0:T(8,128)(2,1)S(1)}, u32[]{:S(2)}, u32[]{:S(2)}) collective-permute-start(bf16[4,256,256]{2,1,0:T(8,128)(2,1)S(1)} %get-tuple-element.48), channel_id=1, source_target_pairs={{0,2},{2,0},{4,6},{6,4},{8,10},{10,8},{1,3},{3,1},{5,7},{7,5},{9,1... | collective-permute-start | bytes 1572872 | tf_op jit(solution)/shard_map/ppermute | solution.py:174
  126.4 26.6 %copy-start.5 = (bf16[4,256,256]{2,1,0:T(8,128)(2,1)S(1)}, bf16[4,256,256]{2,1,0:T(8,128)(2,1)}, u32[]{:S(2)}) copy-start(bf16[4,256,256]{2,1,0:T(8,128)(2,1)} %copy-done.4) | copy-start | bytes 1572868
  126.4 32.5 %collective-permute-start.18 = (bf16[4,256,256]{2,1,0:T(8,128)(2,1)S(1)}, bf16[4,256,256]{2,1,0:T(8,128)(2,1)S(1)}, u32[]{:S(2)}, u32[]{:S(2)}) collective-permute-start(bf16[4,256,256]{2,1,0:T(8,128)(2,1)S(1)} %add_convert_fusion.5), channel_id=1, source_target_pairs={{8,4},{10,6},{12,8},{14,10},{9,5},{11,7},{13,9},{15,11},{24,20},{2... | collective-permute-start | bytes 1572872 | tf_op jit(solution)/shard_map/ppermute | solution.py:178
  151.1 16.5 %collective-permute-start.24 = (bf16[4,256,256]{2,1,0:T(8,128)(2,1)S(1)}, bf16[4,256,256]{2,1,0:T(8,128)(2,1)S(1)}, u32[]{:S(2)}, u32[]{:S(2)}) collective-permute-start(bf16[4,256,256]{2,1,0:T(8,128)(2,1)S(1)} %add_convert_fusion.2), channel_id=1, source_target_pairs={{0,4},{2,6},{4,8},{6,10},{1,5},{3,7},{5,9},{7,11},{16,20},{18,22},... | collective-permute-start | bytes 1572872 | tf_op jit(solution)/shard_map/ppermute | solution.py:178
  153.0 18.4 %collective-permute-start.1 = (bf16[4,256,256]{2,1,0:T(8,128)(2,1)S(1)}, bf16[4,256,256]{2,1,0:T(8,128)(2,1)S(1)}, u32[]{:S(2)}, u32[]{:S(2)}) collective-permute-start(bf16[4,256,256]{2,1,0:T(8,128)(2,1)S(1)} %copy-done.5), channel_id=1, source_target_pairs={{0,2},{2,0},{4,6},{6,4},{8,10},{10,8},{12,14},{14,12},{1,3},{3,1},... | collective-permute-start | bytes 1572872 | tf_op jit(solution)/shard_map/ppermute | solution.py:174
  159.1 12.3 %collective-permute-start.19 = (bf16[4,256,256]{2,1,0:T(8,128)(2,1)S(1)}, bf16[4,256,256]{2,1,0:T(8,128)(2,1)S(1)}, u32[]{:S(2)}, u32[]{:S(2)}) collective-permute-start(bf16[4,256,256]{2,1,0:T(8,128)(2,1)S(1)} %add_convert_fusion.4), channel_id=1, source_target_pairs={{4,0},{6,2},{8,4},{10,6},{12,8},{14,10},{5,1},{7,3},{9,5},{11,7},{... | collective-permute-start | bytes 1572872 | tf_op jit(solution)/shard_map/ppermute | solution.py:178
  167.8 11.1 %collective-permute-start.25 = (bf16[4,256,256]{2,1,0:T(8,128)(2,1)S(1)}, bf16[4,256,256]{2,1,0:T(8,128)(2,1)S(1)}, u32[]{:S(2)}, u32[]{:S(2)}) collective-permute-start(bf16[4,256,256]{2,1,0:T(8,128)(2,1)S(1)} %add_convert_fusion.1), channel_id=1, source_target_pairs={{0,4},{2,6},{4,8},{6,10},{8,12},{10,14},{1,5},{3,7},{5,9},{7,11},{... | collective-permute-start | bytes 1572872 | tf_op jit(solution)/shard_map/ppermute | solution.py:178

commit v3 on v2

--- a/solution.py
+++ b/solution.py
@@ -66,7 +66,8 @@
     )(here, slots, near, live)
 
 
-def grads_kernel(n_load, first, row_ref, count_ref, entry_ref, key_ref, value_ref, *refs):
+def grads_kernel(offsets, first, row_ref, count_ref, entry_ref, key_ref, value_ref, *refs):
+    n_load = len(offsets)
     loads, refs = refs[:n_load], refs[n_load:]
     if not first:
         dk_old, dv_old = refs[:2]
@@ -99,51 +100,60 @@
                 value_m[c, t, part] = jnp.where(mask, value, 0.0).astype(jnp.bfloat16)
                 key_t[c, t, :, part] = masked.T.astype(jnp.bfloat16)
 
-    for load_ref, dq_ref, i in zip(loads, dqs, range(n_load)):
+    for i, (load_ref, dq_ref, offset) in enumerate(zip(loads, dqs, offsets)):
         source_row = row_ref[i]
-        dq_acc[...] = jnp.zeros_like(dq_acc)
+        held = load_ref.shape[0]
+        dq_acc[0:held] = jnp.zeros((held,) + dq_acc.shape[1:], jnp.float32)
+
+        def add_entry(s, t, load_ref=load_ref):
+            for c in range(pairs):
+                lanes = slice(c * PAIR, (c + 1) * PAIR)
+                query = load_ref[s, 0:BLOCK, lanes]
+                grad = load_ref[s, BLOCK:2 * BLOCK, lanes]
+                stats = load_ref[s, 2 * BLOCK:2 * BLOCK + STATS].astype(jnp.float32)
+                score = nt(key_m[c, t], query)
+                dprob = nt(value_m[c, t], grad)
+                probs, dscores = [], []
+                for h in range(2):
+                    part = slice(h * BLOCK, (h + 1) * BLOCK)
+                    i_h = 2 * c + h
+                    norm = stats[i_h:i_h + 1]
+                    delta = stats[2 * pairs + i_h:2 * pairs + i_h + 1]
+                    prob = jnp.exp(score[part] - norm)
+                    dscores.append((prob * (dprob[part] - delta)).astype(jnp.bfloat16))
+                    probs.append(prob.astype(jnp.bfloat16))
+                dv_acc[t, :, lanes] += jnp.where(low, nn(probs[0], grad), nn(probs[1], grad))
+                dk_acc[t, :, lanes] += jnp.where(low, nn(dscores[0], query), nn(dscores[1], query))
+                dq_acc[s, lanes] += nn(key_t[c, t], jnp.concatenate(dscores, axis=0))
 
         @pl.when(source_row >= 0)
         def _():
             @pl.loop(0, count_ref[source_row])
             def _(e):
                 entry = entry_ref[source_row * room + e]
-                s = entry // per_row
+                s = entry // per_row - offset
                 t = entry % per_row
-                for c in range(pairs):
-                    lanes = slice(c * PAIR, (c + 1) * PAIR)
-                    query = load_ref[s, 0:BLOCK, lanes]
-                    grad = load_ref[s, BLOCK:2 * BLOCK, lanes]
-                    stats = load_ref[s, 2 * BLOCK:2 * BLOCK + STATS].astype(jnp.float32)
-                    score = nt(key_m[c, t], query)
-                    dprob = nt(value_m[c, t], grad)
-                    probs, dscores = [], []
-                    for h in range(2):
-                        part = slice(h * BLOCK, (h + 1) * BLOCK)
-                        i_h = 2 * c + h
-                        norm = stats[i_h:i_h + 1]
-                        delta = stats[2 * pairs + i_h:2 * pairs + i_h + 1]
-                        prob = jnp.exp(score[part] - norm)
-                        dscores.append((prob * (dprob[part] - delta)).astype(jnp.bfloat16))
-                        probs.append(prob.astype(jnp.bfloat16))
-                    dv_acc[t, :, lanes] += jnp.where(low, nn(probs[0], grad), nn(probs[1], grad))
-                    dk_acc[t, :, lanes] += jnp.where(low, nn(dscores[0], query), nn(dscores[1], query))
-                    dq_acc[s, lanes] += nn(key_t[c, t], jnp.concatenate(dscores, axis=0))
-
-        dq_ref[...] = dq_acc[...].astype(jnp.bfloat16)
-
-
-def stage_grads(rows, counts, entries, key, value, loads, carry):
+                if held == per_row:
+                    add_entry(s, t)
+                else:
+                    pl.when((s >= 0) & (s < held))(lambda: add_entry(s, t))
+
+        dq_ref[...] = dq_acc[0:held].astype(jnp.bfloat16)
+
+
+def stage_grads(rows, counts, entries, key, value, loads, offsets, carry):
     per_row, _, width = key.shape
     pairs = width // PAIR
     n_load = len(loads)
     smem = pl.BlockSpec(memory_space=pltpu.SMEM)
     vmem = pl.BlockSpec(memory_space=pltpu.VMEM)
-    part = jax.ShapeDtypeStruct((per_row, width, BLOCK), jnp.bfloat16)
+    parts = tuple(
+        jax.ShapeDtypeStruct((load.shape[0], width, BLOCK), jnp.bfloat16) for load in loads
+    )
     total = jax.ShapeDtypeStruct(key.shape, jnp.float32)
     outs = pl.pallas_call(
-        functools.partial(grads_kernel, n_load, not carry),
-        out_shape=(part,) * n_load + (total, total),
+        functools.partial(grads_kernel, offsets, not carry),
+        out_shape=parts + (total, total),
         in_specs=[smem] * 3 + [vmem] * (2 + n_load + len(carry)),
         out_specs=(vmem,) * (n_load + 2),
         scratch_shapes=[
@@ -191,51 +201,85 @@
     key = keys.reshape(per_row, BLOCK, width)
     value = values.reshape(per_row, BLOCK, width)
 
-    ups, downs, y_ups, y_downs = [own], [own], [swap(own, 0, n_z)], [None]
+    last = n_z - 1
+    half = per_row // 2
+    edge = [(j, 2 + j) for j in range(2)] + [(2 * last + j, 2 * last - 2 + j) for j in range(2)]
+    have = {("up", 0): own, ("y", 0): swap(own, 0, n_z)}
+    ups, downs = own, own
     for k in range(1, n_z):
-        ups.append(shift(ups[-1], 1, k - 1, n_z - 1))
-        downs.append(shift(downs[-1], -1, 1, n_z - k + 1))
-        y_ups.append(swap(ups[k], k, n_z))
-        y_downs.append(swap(downs[k], 0, n_z - k))
+        ups = shift(ups, 1, k - 1, last)
+        downs = shift(downs, -1, 1, n_z - k + 1)
+        have[("up", k)], have[("down", k)] = ups, downs
+        if k == 1:
+            have[("y_up", 1)] = swap(ups, 2, n_z)
+            have[("y_down", 1)] = swap(downs, 0, n_z - 2)
+            have[("y_edge", 1)] = lax.ppermute(have[("y", 0)], "row", edge)
+        elif k < last:
+            have[("y_up", k)] = swap(ups, k, n_z)
+            have[("y_down", k)] = swap(downs, 0, n_z - k)
+        else:
+            have[("y_up_a", k)] = swap(ups[:half], last, n_z)
+            have[("y_down_a", k)] = swap(downs[:half], 0, 1)
+            have[("y_up_b", k)] = shift(have[("y_up", k - 1)][half:], 1, last - 1, last)
+            have[("y_down_b", k)] = shift(have[("y_down", k - 1)][half:], -1, 1, 2)
 
     counts, entries = scan_lists(
         here.reshape(1), block_slot, neighbours.reshape(-1), live_count, n_row
     )
 
     def named(kind, k):
-        up = kind in ("up", "y_up")
-        there = z - k if up else z + k
-        side = 1 - y if kind in ("y_up", "y_down") else y
-        valid = (there >= 0) & (there < n_z)
-        return jnp.where(valid, 2 * there + side, -1)
-
-    have = {"up": ups, "down": downs, "y_up": y_ups, "y_down": y_downs}
-    stages = [[("up", 0), ("y_up", 0)]]
-    for k in range(1, n_z + 1):
-        stage = [("up", k), ("down", k)] if k < n_z else []
-        stages.append(stage + ([("y_up", k - 1), ("y_down", k - 1)] if k > 1 else []))
+        if kind == "y_edge":
+            there = jnp.where(z == 1, 0, jnp.where(z == last - 1, last, -1))
+        else:
+            there = z + k if "down" in kind else z - k
+            if (kind, k) == ("y_up", 1):
+                there = jnp.where(there >= 1, there, -1)
+            if (kind, k) == ("y_down", 1):
+                there = jnp.where(there <= last - 1, there, -1)
+        side = 1 - y if kind.startswith("y") else y
+        return jnp.where((there >= 0) & (there < n_z), 2 * there + side, -1)
+
+    stages = [[("up", 0), ("y", 0)], [("up", 1), ("down", 1)]]
+    stages.append([("up", 2), ("down", 2), ("y_up", 1), ("y_down", 1), ("y_edge", 1)])
+    for k in range(3, n_z):
+        stages.append([("up", k), ("down", k), ("y_up", k - 1), ("y_down", k - 1)])
+    stages.append([(kind, last) for kind in ("y_up_a", "y_down_a", "y_up_b", "y_down_b")])
     parts, carry = {}, ()
     for stage in stages:
         rows = jnp.stack([named(*name) for name in stage]).astype(jnp.int32)
+        offsets = tuple(half if name[0].endswith("_b") else 0 for name in stage)
         dqs, carry = stage_grads(
-            rows, counts, entries, key, value, [have[kind][k] for kind, k in stage], carry
+            rows, counts, entries, key, value, [have[name] for name in stage], offsets, carry
         )
         parts.update(zip(stage, dqs))
 
+    low = jnp.bfloat16
+
     def add(*terms):
         return sum(x.astype(jnp.float32) for x in terms)
 
-    low = jnp.bfloat16
-    up, down = None, None
-    for k in range(n_z - 1, 0, -1):
-        up_terms = [parts[("up", k)], swap(parts[("y_up", k)], k, n_z)]
-        down_terms = [parts[("down", k)], swap(parts[("y_down", k)], 0, n_z - k)]
-        if up is not None:
-            up_terms.append(up)
-            down_terms.append(down)
-        up = shift(add(*up_terms).astype(low), -1, k, n_z)
-        down = shift(add(*down_terms).astype(low), 1, 0, n_z - k)
-    dq = add(parts[("up", 0)], swap(parts[("y_up", 0)], 0, n_z), up, down).astype(low)
+    def add_half(x, part, lead):
+        pads = ((0, per_row - half), (0, 0), (0, 0)) if lead else ((half, 0), (0, 0), (0, 0))
+        return add(x, jnp.pad(part, pads)).astype(low)
+
+    edge_back = lax.ppermute(parts[("y_edge", 1)], "row", [(j, i) for i, j in edge])
+    up_b = shift(parts[("y_up_b", last)], -1, last, n_z)
+    down_b = shift(parts[("y_down_b", last)], 1, 0, 1)
+    up = add_half(parts[("up", last)], swap(parts[("y_up_a", last)], last, n_z), True)
+    down = add_half(parts[("down", last)], swap(parts[("y_down_a", last)], 0, 1), True)
+    for k in range(last - 1, 0, -1):
+        up, down = shift(up, -1, k + 1, n_z), shift(down, 1, 0, n_z - k - 1)
+        y_up, y_down = parts[("y_up", k)], parts[("y_down", k)]
+        if k == last - 1:
+            y_up, y_down = add_half(y_up, up_b, False), add_half(y_down, down_b, False)
+        edged = k == 1
+        y_up = swap(y_up, 2 if edged else k, n_z)
+        y_down = swap(y_down, 0, n_z - 2 if edged else n_z - k)
+        up = add(parts[("up", k)], y_up, up).astype(low)
+        down = add(parts[("down", k)], y_down, down).astype(low)
+    up, down = shift(up, -1, 1, n_z), shift(down, 1, 0, last)
+    y_back = swap(add(parts[("y", 0)], edge_back).astype(low), 0, n_z)
+    dq = add(parts[("up", 0)], y_back, up, down).astype(low)
     dk, dv = carry
     return (
         jnp.transpose(dq, (0, 2, 1)).reshape(tokens, width),

time: 181 us -> 172 us (0.950)
  waiting for transfers between devices: 90.5 us -> 48.4 us
  starting transfers between devices: 46.3 us -> 64.2 us
  local copies, waits for them, and re-layouts: 7.36 us -> 16.6 us
  Pallas kernels: 30.9 us -> 36.4 us
    ppermute x14, waiting for transfers between devices: 36.2 us -> 7.06 us  [swap(): return lax.ppermute(x, 'row', pairs)]
    ppermute x12 -> x16, waiting for transfers between devices: 54.3 us -> 41.4 us  [shift(): return lax.ppermute(x, 'row', pairs)]
    ppermute x12 -> x16, starting transfers between devices: 23.5 us -> 36.2 us  [shift(): return lax.ppermute(x, 'row', pairs)]
    unnamed x29 -> x45, local copies, waits for them, and re-layouts: 5.62 us -> 14.6 us
    ppermute x0 -> x2, starting transfers between devices: none -> 5.94 us  [the longest x1 4.65 us: body(): lax.ppermute(parts['y_edge', 1], 'row', [(j, i) for i, j in edge])]
    pallas_call x5, Pallas kernels: 28 us -> 33.6 us  [stage_grads(): pl.pallas_call(functools.partial(grads_kernel, offsets, not carry), out_s...]
  transfers between devices with their start and end apart: 26 -> 32, of which waited for: 9 -> 9; matrix products, arithmetic and copies ran while one was open for 2% -> 2% of each run, Pallas kernels for 16% -> 20%
where the time goes in v3:
time: 172 us; the launch traced here: 171 us
  starting transfers between devices  64.2 us (37%)
  waiting for transfers between devices  48.4 us (28%)
  Pallas kernels  36.4 us (21%)
  local copies, waits for them, and re-layouts  16.6 us (10%)
  other arithmetic  4.03 us (2%)
    ppermute x16, waiting for transfers between devices, shift(): return lax.ppermute(x, 'row', pairs)  41.4 us
    ppermute x16, starting transfers between devices, shift(): return lax.ppermute(x, 'row', pairs)  36.2 us
    pallas_call x5, Pallas kernels, stage_grads(): pl.pallas_call(functools.partial(grads_kernel, offsets, not carry), out_s...  33.6 us
    ppermute x14, starting transfers between devices, swap(): return lax.ppermute(x, 'row', pairs)  22 us
    unnamed x45, local copies, waits for them, and re-layouts  14.6 us
    ppermute x14, waiting for transfers between devices, swap(): return lax.ppermute(x, 'row', pairs)  7.06 us
    ppermute x1, starting transfers between devices, body(): lax.ppermute(parts['y_edge', 1], 'row', [(j, i) for i, j in edge])  4.65 us
  transfers between devices with their start and end apart: 32, of which 9 were waited for; matrix products, arithmetic and copies ran while one was open for 2% of the time, Pallas kernels for 20%

profile of v3, /device:TPU:10, one launch (start us, length us, event | category | flops | bytes accessed | tf_op | source)
XLA Modules:
  0.0 170.9 jit_solution(17940858764672154896)
XLA Ops:
  0.6 1.3 copy.13
  3.4 3.5 %collective-permute-start.1 = (bf16[4,528,256]{2,1,0:T(8,128)(2,1)S(1)}, bf16[4,528,256]{2,1,0:T(8,128)(2,1)}, u32[]{:S(2)}, u32[]{:S(2)}) collective-permute-start(bf16[4,528,256]{2,1,0:T(8,128)(2,1)S(1)} %maximum_maximum_fusion.refs_0_), channel_id=1, source_target_pairs={{0,4},{2,6},{4,8},{6,10},{8,12},{10,14},{1,5},{3,7},{5,9},{7,11},{... | collective-permute-start | bytes 3244040 | tf_op jit(solution)/shard_map/ppermute | solution.py:188
  6.9 3.4 %collective-permute-start.3 = (bf16[4,528,256]{2,1,0:T(8,128)(2,1)S(1)}, bf16[4,528,256]{2,1,0:T(8,128)(2,1)S(1)}, u32[]{:S(2)}, u32[]{:S(2)}) collective-permute-start(bf16[4,528,256]{2,1,0:T(8,128)(2,1)S(1)} %maximum_maximum_fusion.refs_0_), channel_id=1, source_target_pairs={{4,0},{6,2},{8,4},{10,6},{12,8},{14,10},{5,1},{7,3},{9,5},{11,7},{... | collective-permute-start | bytes 3244040 | tf_op jit(solution)/shard_map/ppermute | solution.py:188
  10.3 1.6 collective-permute-start
  12.6 2.8 %shard_map.112 = (s32[8]{0:T(128)}, s32[256]{0:T(256)}) custom-call(s32[1]{0:T(128)} %bitcast.2.here_ref, s32[32]{0:T(128)} %slot_ref.1, s32[256]{0:T(256)} %reshape.40.near_ref, s32[32]{0:T(128)} %live_ref.1), custom_call_target="tpu_custom_call" | custom-call | tf_op jit(solution)/shard_map/pallas_call | solution.py:58
  15.9 15.2 %collective-permute-done.1.refs_0_ = bf16[4,528,256]{2,1,0:T(8,128)(2,1)} collective-permute-done((bf16[4,528,256]{2,1,0:T(8,128)(2,1)S(1)}, bf16[4,528,256]{2,1,0:T(8,128)(2,1)}, u32[]{:S(2)}, u32[]{:S(2)}) %collective-permute-start.1) | collective-permute-done | bytes 1081376 | tf_op jit(solution)/shard_map/ppermute | solution.py:188
  31.0 4.5 %collective-permute-start.2 = (bf16[4,528,256]{2,1,0:T(8,128)(2,1)}, bf16[4,528,256]{2,1,0:T(8,128)(2,1)}, u32[]{:S(2)}, u32[]{:S(2)}) collective-permute-start(bf16[4,528,256]{2,1,0:T(8,128)(2,1)} %collective-permute-done.1.refs_0_), channel_id=1, source_target_pairs={{4,8},{6,10},{8,12},{10,14},{5,9},{7,11},{9,13},{11,15},{20,24},{2... | collective-permute-start | bytes 3244040 | tf_op jit(solution)/shard_map/ppermute | solution.py:188
  36.2 1.9 %collective-permute-start.4 = (bf16[4,528,256]{2,1,0:T(8,128)(2,1)S(1)}, bf16[4,528,256]{2,1,0:T(8,128)(2,1)}, u32[]{:S(2)}, u32[]{:S(2)}) collective-permute-start(bf16[4,528,256]{2,1,0:T(8,128)(2,1)S(1)} %collective-permute-done.3.refs_1_), channel_id=1, source_target_pairs={{4,0},{6,2},{8,4},{10,6},{5,1},{7,3},{9,5},{11,7},{20,16},{22,18},... | collective-permute-start | bytes 3244040 | tf_op jit(solution)/shard_map/ppermute | solution.py:188
  38.2 3.4 %collective-permute-start.6 = (bf16[4,528,256]{2,1,0:T(8,128)(2,1)S(1)}, bf16[4,528,256]{2,1,0:T(8,128)(2,1)S(1)}, u32[]{:S(2)}, u32[]{:S(2)}) collective-permute-start(bf16[4,528,256]{2,1,0:T(8,128)(2,1)S(1)} %collective-permute-done.3.refs_1_), channel_id=1, source_target_pairs={{0,2},{2,0},{4,6},{6,4},{1,3},{3,1},{5,7},{7,5},{16,18},{18,16},{2... | collective-permute-start | bytes 3244040 | tf_op jit(solution)/shard_map/ppermute | solution.py:184
  41.6 1.3 collective-permute-start.7
  42.9 1.0 copy-done.6
  44.0 1.0 copy-done.9
  46.3 8.8 %shard_map.113 = (bf16[4,256,256]{2,1,0:T(8,128)(2,1)S(1)}, bf16[4,256,256]{2,1,0:T(8,128)(2,1)S(1)}, f32[4,256,256]{2,1,0:T(8,128)S(1)}, f32[4,256,256]{2,1,0:T(8,128)S(1)}) custom-call(s32[2]{0:T(128)S(1)} %pad_add_fusion.row_ref, s32[8]{0:T(128)S(1)} %copy-done.13, s32[256]{0:T(256)S(1)} %copy-done.12, bf16[4,256,256]{2,1,0:T(8,128)(2,1)S(1)} %bitcast.30, ...), custom_call_target="tpu_custom_call" | custom-call | flops 6000000000 | bytes 4194304 | tf_op jit(solution)/shard_map/pallas_call | solution.py:154
  55.2 6.1 %shard_map.114 = (bf16[4,256,256]{2,1,0:T(8,128)(2,1)S(1)}, bf16[4,256,256]{2,1,0:T(8,128)(2,1)S(1)}, f32[4,256,256]{2,1,0:T(8,128)S(1)}, f32[4,256,256]{2,1,0:T(8,128)S(1)}) custom-call(s32[2]{0:T(128)S(1)} %pad_add_fusion.1.row_ref, s32[8]{0:T(128)S(1)} %copy-done.13, s32[256]{0:T(256)S(1)} %copy-done.12, bf16[4,256,256]{2,1,0:T(8,128)(2,1)S(1)} %bitcast.31, ...), custom_call_target="tpu_custom_call" | custom-call | flops 6000000000 | bytes 4194304 | tf_op jit(solution)/shard_map/pallas_call | solution.py:154
  61.3 1.0 copy-done.14
  64.1 1.0 copy-done
  65.1 1.7 %collective-permute-start.12 = (bf16[4,528,256]{2,1,0:T(8,128)(2,1)}, bf16[4,528,256]{2,1,0:T(8,128)(2,1)S(1)}, u32[]{:S(2)}, u32[]{:S(2)}) collective-permute-start(bf16[4,528,256]{2,1,0:T(8,128)(2,1)} %collective-permute-done.4.refs_1_), channel_id=1, source_target_pairs={{4,0},{6,2},{5,1},{7,3},{20,16},{22,18},{21,17},{23,19}} | collective-permute-start | bytes 3244040 | tf_op jit(solution)/shard_map/ppermute | solution.py:188
  66.9 1.0 copy-done.2
  67.9 5.1 %collective-permute-start.14 = (bf16[4,528,256]{2,1,0:T(8,128)(2,1)}, bf16[4,528,256]{2,1,0:T(8,128)(2,1)S(1)}, u32[]{:S(2)}, u32[]{:S(2)}) collective-permute-start(bf16[4,528,256]{2,1,0:T(8,128)(2,1)} %collective-permute-done.4.refs_1_), channel_id=1, source_target_pairs={{0,2},{2,0},{4,6},{6,4},{1,3},{3,1},{5,7},{7,5},{16,18},{18,16},{2... | collective-permute-start | bytes 3244040 | tf_op jit(solution)/shard_map/ppermute | solution.py:184
  73.0 1.0 copy-done.4
  74.0 1.2 copy-done.1
  75.2 1.2 copy-done.3
  76.5 1.2 copy-done.5
  77.7 1.2 copy-done.15
  78.9 11.1 %shard_map.115 = (bf16[4,256,256]{2,1,0:T(8,128)(2,1)S(1)}, bf16[4,256,256]{2,1,0:T(8,128)(2,1)S(1)}, bf16[4,256,256]{2,1,0:T(8,128)(2,1)S(1)}, bf16[4,256,256]{...) custom-call(s32[5]{0:T(128)S(1)} %stack.70.row_ref, ...), custom_call_target="tpu_custom_call" | custom-call | flops 15000000512 | bytes 10485760 | tf_op jit(solution)/shard_map/pallas_call | solution.py:154
  90.9 0.8 collective-permute-start.16
  92.5 3.1 %collective-permute-done.14.refs_3_ = bf16[4,528,256]{2,1,0:T(8,128)(2,1)S(1)} collective-permute-done((bf16[4,528,256]{2,1,0:T(8,128)(2,1)}, bf16[4,528,256]{2,1,0:T(8,128)(2,1)S(1)}, u32[]{:S(2)}, u32[]{:S(2)}) %collective-permute-start.14) | collective-permute-done | bytes 1081376 | tf_op jit(solution)/shard_map/ppermute | solution.py:184
  95.6 3.9 %collective-permute-start.18 = (bf16[2,528,256]{2,1,0:T(8,128)(2,1)S(1)}, bf16[2,528,256]{2,1,0:T(8,128)(2,1)S(1)}, u32[]{:S(2)}, u32[]{:S(2)}) collective-permute-start(bf16[2,528,256]{2,1,0:T(8,128)(2,1)S(1)} %slice.19), channel_id=1, source_target_pairs={{4,0},{6,2},{5,1},{7,3},{20,16},{22,18},{21,17},{23,19}} | collective-permute-start | bytes 1622024 | tf_op jit(solution)/shard_map/ppermute | solution.py:188
  99.5 5.6 %shard_map.116 = (bf16[4,256,256]{2,1,0:T(8,128)(2,1)S(1)}, bf16[4,256,256]{2,1,0:T(8,128)(2,1)S(1)}, bf16[4,256,256]{2,1,0:T(8,128)(2,1)S(1)}, bf16[4,256,256]{...) custom-call(s32[4]{0:T(128)S(1)} %pad_add_fusion.2.row_ref, s32[8]{0:T(128)S(1)} %copy-done.13, ...), custom_call_target="tpu_custom_call" | custom-call | flops 12000000000 | bytes 8388608 | tf_op jit(solution)/shard_map/pallas_call | solution.py:154
  105.2 3.5 %collective-permute-done.18.refs_3_ = bf16[2,528,256]{2,1,0:T(8,128)(2,1)S(1)} collective-permute-done((bf16[2,528,256]{2,1,0:T(8,128)(2,1)S(1)}, bf16[2,528,256]{2,1,0:T(8,128)(2,1)S(1)}, u32[]{:S(2)}, u32[]{:S(2)}) %collective-permute-start.18) | collective-permute-done | bytes 540704 | tf_op jit(solution)/shard_map/ppermute | solution.py:188
  108.6 1.9 %shard_map.117 = (bf16[2,256,256]{2,1,0:T(8,128)(2,1)S(1)}, bf16[2,256,256]{2,1,0:T(8,128)(2,1)S(1)}, bf16[2,256,256]{2,1,0:T(8,128)(2,1)S(1)}, bf16[2,256,256]{...) custom-call(s32[4]{0:T(128)S(1)} %pad_add_fusion.3.row_ref, s32[8]{0:T(128)S(1)} %copy-done.13, ...), custom_call_target="tpu_custom_call" | custom-call | flops 12000000000 | bytes 8388608 | tf_op jit(solution)/shard_map/pallas_call | solution.py:154
  111.9 1.3 collective-permute-start.26
  115.5 8.1 %collective-permute-done.26 = bf16[2,256,256]{2,1,0:T(8,128)(2,1)S(1)} collective-permute-done((bf16[2,256,256]{2,1,0:T(8,128)(2,1)S(1)}, bf16[2,256,256]{2,1,0:T(8,128)(2,1)S(1)}, u32[]{:S(2)}, u32[]{:S(2)}) %collective-permute-start.26) | collective-permute-done | bytes 262176 | tf_op jit(solution)/shard_map/ppermute | solution.py:188
  123.7 2.2 %collective-permute-start.27 = (bf16[4,256,256]{2,1,0:T(8,128)(2,1)S(1)}, bf16[4,256,256]{2,1,0:T(8,128)(2,1)S(1)}, u32[]{:S(2)}, u32[]{:S(2)}) collective-permute-start(bf16[4,256,256]{2,1,0:T(8,128)(2,1)S(1)} %add_convert_fusion.4), channel_id=1, source_target_pairs={{0,2},{2,0},{4,6},{6,4},{1,3},{3,1},{5,7},{7,5},{16,18},{18,16},{2... | collective-permute-start | bytes 1572872 | tf_op jit(solution)/shard_map/ppermute | solution.py:184
  126.0 1.3 collective-permute-start.29
  128.0 3.6 %collective-permute-start.25 = (bf16[4,256,256]{2,1,0:T(8,128)(2,1)S(1)}, bf16[4,256,256]{2,1,0:T(8,128)(2,1)S(1)}, u32[]{:S(2)}, u32[]{:S(2)}) collective-permute-start(bf16[4,256,256]{2,1,0:T(8,128)(2,1)S(1)} %get-tuple-element.53), channel_id=1, source_target_pairs={{0,2},{2,0},{4,6},{6,4},{1,3},{3,1},{5,7},{7,5},{16,18},{18,16},{2... | collective-permute-start | bytes 1572872 | tf_op jit(solution)/shard_map/ppermute | solution.py:184
  131.6 4.6 %collective-permute-start.8 = (bf16[4,256,256]{2,1,0:T(8,128)(2,1)S(1)}, bf16[4,256,256]{2,1,0:T(8,128)(2,1)S(1)}, u32[]{:S(2)}, u32[]{:S(2)}) collective-permute-start(bf16[4,256,256]{2,1,0:T(8,128)(2,1)S(1)} %get-tuple-element.40), channel_id=1, source_target_pairs={{4,0},{6,2},{8,12},{10,14},{5,1},{7,3},{9,13},{11,15},{20,16},{22,... | collective-permute-start | bytes 1572872 | tf_op jit(solution)/shard_map/ppermute | solution.py:265
  136.5 3.9 %collective-permute-done.27 = bf16[4,256,256]{2,1,0:T(8,128)(2,1)S(1)} collective-permute-done((bf16[4,256,256]{2,1,0:T(8,128)(2,1)S(1)}, bf16[4,256,256]{2,1,0:T(8,128)(2,1)S(1)}, u32[]{:S(2)}, u32[]{:S(2)}) %collective-permute-start.27) | collective-permute-done | bytes 524320 | tf_op jit(solution)/shard_map/ppermute | solution.py:184
  140.4 1.3 collective-permute-start.23
  141.9 4.6 %collective-permute-start.30 = (bf16[4,256,256]{2,1,0:T(8,128)(2,1)S(1)}, bf16[4,256,256]{2,1,0:T(8,128)(2,1)S(1)}, u32[]{:S(2)}, u32[]{:S(2)}) collective-permute-start(bf16[4,256,256]{2,1,0:T(8,128)(2,1)S(1)} %add_convert_fusion.2), channel_id=1, source_target_pairs={{0,4},{2,6},{4,8},{6,10},{1,5},{3,7},{5,9},{7,11},{16,20},{18,22},... | collective-permute-start | bytes 1572872 | tf_op jit(solution)/shard_map/ppermute | solution.py:188
  147.0 9.1 %collective-permute-done.23 = bf16[4,256,256]{2,1,0:T(8,128)(2,1)S(1)} collective-permute-done((bf16[4,256,256]{2,1,0:T(8,128)(2,1)S(1)}, bf16[4,256,256]{2,1,0:T(8,128)(2,1)S(1)}, u32[]{:S(2)}, u32[]{:S(2)}) %collective-permute-start.23) | collective-permute-done | bytes 524320 | tf_op jit(solution)/shard_map/ppermute | solution.py:188
  156.4 1.9 %collective-permute-start.24 = (bf16[4,256,256]{2,1,0:T(8,128)(2,1)S(1)}, bf16[4,256,256]{2,1,0:T(8,128)(2,1)S(1)}, u32[]{:S(2)}, u32[]{:S(2)}) collective-permute-start(bf16[4,256,256]{2,1,0:T(8,128)(2,1)S(1)} %add_convert_fusion.5), channel_id=1, source_target_pairs={{4,0},{6,2},{8,4},{10,6},{12,8},{14,10},{5,1},{7,3},{9,5},{11,7},{... | collective-permute-start | bytes 1572872 | tf_op jit(solution)/shard_map/ppermute | solution.py:188
  158.6 4.2 %collective-permute-start.31 = (bf16[4,256,256]{2,1,0:T(8,128)(2,1)S(1)}, bf16[4,256,256]{2,1,0:T(8,128)(2,1)S(1)}, u32[]{:S(2)}, u32[]{:S(2)}) collective-permute-start(bf16[4,256,256]{2,1,0:T(8,128)(2,1)S(1)} %add_convert_fusion.1), channel_id=1, source_target_pairs={{0,4},{2,6},{4,8},{6,10},{8,12},{10,14},{1,5},{3,7},{5,9},{7,11},{... | collective-permute-start | bytes 1572872 | tf_op jit(solution)/shard_map/ppermute | solution.py:188
  162.8 0.8 convert_element_type.169
  163.6 0.9 multiply_convert_fusion
  164.5 3.0 %collective-permute-done.24 = bf16[4,256,256]{2,1,0:T(8,128)(2,1)S(1)} collective-permute-done((bf16[4,256,256]{2,1,0:T(8,128)(2,1)S(1)}, bf16[4,256,256]{2,1,0:T(8,128)(2,1)S(1)}, u32[]{:S(2)}, u32[]{:S(2)}) %collective-permute-start.24) | collective-permute-done | bytes 524320 | tf_op jit(solution)/shard_map/ppermute | solution.py:188
  167.5 2.2 %collective-permute-done.31 = bf16[4,256,256]{2,1,0:T(8,128)(2,1)S(1)} collective-permute-done((bf16[4,256,256]{2,1,0:T(8,128)(2,1)S(1)}, bf16[4,256,256]{2,1,0:T(8,128)(2,1)S(1)}, u32[]{:S(2)}, u32[]{:S(2)}) %collective-permute-start.31) | collective-permute-done | bytes 524320 | tf_op jit(solution)/shard_map/ppermute | solution.py:188
  169.9 1.0 copy.15
  (95 shorter events, 14.0 us)
Async XLA Ops:
  0.6 1.3 copy-start.18
  2.0 1.0 copy-start.16
  2.0 1.2 copy-start.17
  3.2 8.7 %copy-start.20 = (s32[32,8]{0,1:T(8,128)S(1)}, s32[32,8]{0,1:T(8,128)}, u32[]{:S(2)}) copy-start(s32[32,8]{0,1:T(8,128)} %param.16) | copy-start | bytes 3076
  3.4 27.6 %collective-permute-start.1 = (bf16[4,528,256]{2,1,0:T(8,128)(2,1)S(1)}, bf16[4,528,256]{2,1,0:T(8,128)(2,1)}, u32[]{:S(2)}, u32[]{:S(2)}) collective-permute-start(bf16[4,528,256]{2,1,0:T(8,128)(2,1)S(1)} %maximum_maximum_fusion.refs_0_), channel_id=1, source_target_pairs={{0,4},{2,6},{4,8},{6,10},{8,12},{10,14},{1,5},{3,7},{5,9},{7,11},{... | collective-permute-start | bytes 3244040 | tf_op jit(solution)/shard_map/ppermute | solution.py:188
  6.9 29.3 %collective-permute-start.3 = (bf16[4,528,256]{2,1,0:T(8,128)(2,1)S(1)}, bf16[4,528,256]{2,1,0:T(8,128)(2,1)S(1)}, u32[]{:S(2)}, u32[]{:S(2)}) collective-permute-start(bf16[4,528,256]{2,1,0:T(8,128)(2,1)S(1)} %maximum_maximum_fusion.refs_0_), channel_id=1, source_target_pairs={{4,0},{6,2},{8,4},{10,6},{12,8},{14,10},{5,1},{7,3},{9,5},{11,7},{... | collective-permute-start | bytes 3244040 | tf_op jit(solution)/shard_map/ppermute | solution.py:188
  10.3 31.3 %collective-permute-start = (bf16[4,528,256]{2,1,0:T(8,128)(2,1)S(1)}, bf16[4,528,256]{2,1,0:T(8,128)(2,1)S(1)}, u32[]{:S(2)}, u32[]{:S(2)}) collective-permute-start(bf16[4,528,256]{2,1,0:T(8,128)(2,1)S(1)} %maximum_maximum_fusion.refs_0_), channel_id=1, source_target_pairs={{0,2},{2,0},{4,6},{6,4},{8,10},{10,8},{12,14},{14,12},{1,3},{3,1},... | collective-permute-start | bytes 3244040 | tf_op jit(solution)/shard_map/ppermute | solution.py:184
  31.0 31.2 %collective-permute-start.2 = (bf16[4,528,256]{2,1,0:T(8,128)(2,1)}, bf16[4,528,256]{2,1,0:T(8,128)(2,1)}, u32[]{:S(2)}, u32[]{:S(2)}) collective-permute-start(bf16[4,528,256]{2,1,0:T(8,128)(2,1)} %collective-permute-done.1.refs_0_), channel_id=1, source_target_pairs={{4,8},{6,10},{8,12},{10,14},{5,9},{7,11},{9,13},{11,15},{20,24},{2... | collective-permute-start | bytes 3244040 | tf_op jit(solution)/shard_map/ppermute | solution.py:188
  35.5 28.6 %collective-permute-start.5 = (bf16[4,528,256]{2,1,0:T(8,128)(2,1)}, bf16[4,528,256]{2,1,0:T(8,128)(2,1)S(1)}, u32[]{:S(2)}, u32[]{:S(2)}) collective-permute-start(bf16[4,528,256]{2,1,0:T(8,128)(2,1)} %collective-permute-done.1.refs_0_), channel_id=1, source_target_pairs={{8,10},{10,8},{12,14},{14,12},{9,11},{11,9},{13,15},{15,13},{24,26... | collective-permute-start | bytes 3244040 | tf_op jit(solution)/shard_map/ppermute | solution.py:184
  36.2 27.1 %collective-permute-start.4 = (bf16[4,528,256]{2,1,0:T(8,128)(2,1)S(1)}, bf16[4,528,256]{2,1,0:T(8,128)(2,1)}, u32[]{:S(2)}, u32[]{:S(2)}) collective-permute-start(bf16[4,528,256]{2,1,0:T(8,128)(2,1)S(1)} %collective-permute-done.3.refs_1_), channel_id=1, source_target_pairs={{4,0},{6,2},{8,4},{10,6},{5,1},{7,3},{9,5},{11,7},{20,16},{22,18},... | collective-permute-start | bytes 3244040 | tf_op jit(solution)/shard_map/ppermute | solution.py:188
  38.2 28.7 %collective-permute-start.6 = (bf16[4,528,256]{2,1,0:T(8,128)(2,1)S(1)}, bf16[4,528,256]{2,1,0:T(8,128)(2,1)S(1)}, u32[]{:S(2)}, u32[]{:S(2)}) collective-permute-start(bf16[4,528,256]{2,1,0:T(8,128)(2,1)S(1)} %collective-permute-done.3.refs_1_), channel_id=1, source_target_pairs={{0,2},{2,0},{4,6},{6,4},{1,3},{3,1},{5,7},{7,5},{16,18},{18,16},{2... | collective-permute-start | bytes 3244040 | tf_op jit(solution)/shard_map/ppermute | solution.py:184
  41.6 31.4 %collective-permute-start.7 = (bf16[4,528,256]{2,1,0:T(8,128)(2,1)S(1)}, bf16[4,528,256]{2,1,0:T(8,128)(2,1)S(1)}, u32[]{:S(2)}, u32[]{:S(2)}) collective-permute-start(bf16[4,528,256]{2,1,0:T(8,128)(2,1)S(1)} %collective-permute-done.refs_1_), channel_id=1, source_target_pairs={{0,4},{2,6},{12,8},{14,10},{1,5},{3,7},{13,9},{15,11},{16,20},{18,... | collective-permute-start | bytes 3244040 | tf_op jit(solution)/shard_map/ppermute | solution.py:216
  42.9 1.0 copy-start.6
  44.0 1.0 copy-start.9
  46.3 8.8 %copy-start.7 = (bf16[1024,256]{1,0:T(8,128)(2,1)S(1)}, bf16[1024,256]{1,0:T(8,128)(2,1)}, u32[]{:S(2)}) copy-start(bf16[1024,256]{1,0:T(8,128)(2,1)} %param.10) | copy-start | bytes 1572868
  46.3 8.8 %copy-start.10 = (bf16[1024,256]{1,0:T(8,128)(2,1)S(1)}, bf16[1024,256]{1,0:T(8,128)(2,1)}, u32[]{:S(2)}) copy-start(bf16[1024,256]{1,0:T(8,128)(2,1)} %param.11) | copy-start | bytes 1572868
  55.1 18.9 %copy-start.11 = (bf16[1024,256]{1,0:T(8,128)(2,1)S(1)}, bf16[1024,256]{1,0:T(8,128)(2,1)}, u32[]{:S(2)}) copy-start(bf16[1024,256]{1,0:T(8,128)(2,1)} %param.11) | copy-start | bytes 1572868
  62.3 27.8 %collective-permute-start.11 = (bf16[4,528,256]{2,1,0:T(8,128)(2,1)}, bf16[4,528,256]{2,1,0:T(8,128)(2,1)S(1)}, u32[]{:S(2)}, u32[]{:S(2)}) collective-permute-start(bf16[4,528,256]{2,1,0:T(8,128)(2,1)} %collective-permute-done.2.refs_0_), channel_id=1, source_target_pairs={{8,12},{10,14},{9,13},{11,15},{24,28},{26,30},{25,29},{27,31}} | collective-permute-start | bytes 3244040 | tf_op jit(solution)/shard_map/ppermute | solution.py:188
  63.3 28.4 %collective-permute-start.13 = (bf16[4,528,256]{2,1,0:T(8,128)(2,1)}, bf16[4,528,256]{2,1,0:T(8,128)(2,1)S(1)}, u32[]{:S(2)}, u32[]{:S(2)}) collective-permute-start(bf16[4,528,256]{2,1,0:T(8,128)(2,1)} %collective-permute-done.2.refs_0_), channel_id=1, source_target_pairs={{8,10},{10,8},{12,14},{14,12},{9,11},{11,9},{13,15},{15,13},{24,26... | collective-permute-start | bytes 3244040 | tf_op jit(solution)/shard_map/ppermute | solution.py:184
  64.1 1.0 copy-start
  65.1 25.7 %collective-permute-start.12 = (bf16[4,528,256]{2,1,0:T(8,128)(2,1)}, bf16[4,528,256]{2,1,0:T(8,128)(2,1)S(1)}, u32[]{:S(2)}, u32[]{:S(2)}) collective-permute-start(bf16[4,528,256]{2,1,0:T(8,128)(2,1)} %collective-permute-done.4.refs_1_), channel_id=1, source_target_pairs={{4,0},{6,2},{5,1},{7,3},{20,16},{22,18},{21,17},{23,19}} | collective-permute-start | bytes 3244040 | tf_op jit(solution)/shard_map/ppermute | solution.py:188
  67.9 27.7 %collective-permute-start.14 = (bf16[4,528,256]{2,1,0:T(8,128)(2,1)}, bf16[4,528,256]{2,1,0:T(8,128)(2,1)S(1)}, u32[]{:S(2)}, u32[]{:S(2)}) collective-permute-start(bf16[4,528,256]{2,1,0:T(8,128)(2,1)} %collective-permute-done.4.refs_1_), channel_id=1, source_target_pairs={{0,2},{2,0},{4,6},{6,4},{1,3},{3,1},{5,7},{7,5},{16,18},{18,16},{2... | collective-permute-start | bytes 3244040 | tf_op jit(solution)/shard_map/ppermute | solution.py:184
  73.0 1.0 copy-start.4
  74.0 1.2 copy-start.1
  75.2 1.2 copy-start.3
  76.5 1.2 copy-start.5
  77.7 1.2 copy-start.15
  90.1 15.0 %collective-permute-start.15 = (bf16[2,528,256]{2,1,0:T(8,128)(2,1)S(1)}, bf16[2,528,256]{2,1,0:T(8,128)(2,1)S(1)}, u32[]{:S(2)}, u32[]{:S(2)}) collective-permute-start(bf16[2,528,256]{2,1,0:T(8,128)(2,1)S(1)} %slice.16), channel_id=1, source_target_pairs={{12,14},{14,12},{13,15},{15,13},{28,30},{30,28},{29,31},{31,29}} | collective-permute-start | bytes 1622024 | tf_op jit(solution)/shard_map/ppermute | solution.py:184
  90.9 8.6 %copy-start.8 = (bf16[1024,256]{1,0:T(8,128)(2,1)S(1)}, bf16[1024,256]{1,0:T(8,128)(2,1)}, u32[]{:S(2)}) copy-start(bf16[1024,256]{1,0:T(8,128)(2,1)} %param.10) | copy-start | bytes 1572868
  90.9 14.3 %collective-permute-start.16 = (bf16[2,528,256]{2,1,0:T(8,128)(2,1)S(1)}, bf16[2,528,256]{2,1,0:T(8,128)(2,1)S(1)}, u32[]{:S(2)}, u32[]{:S(2)}) collective-permute-start(bf16[2,528,256]{2,1,0:T(8,128)(2,1)S(1)} %slice.17), channel_id=1, source_target_pairs={{0,2},{2,0},{1,3},{3,1},{16,18},{18,16},{17,19},{19,17}} | collective-permute-start | bytes 1622024 | tf_op jit(solution)/shard_map/ppermute | solution.py:184
  91.8 13.4 %collective-permute-start.17 = (bf16[2,528,256]{2,1,0:T(8,128)(2,1)S(1)}, bf16[2,528,256]{2,1,0:T(8,128)(2,1)S(1)}, u32[]{:S(2)}, u32[]{:S(2)}) collective-permute-start(bf16[2,528,256]{2,1,0:T(8,128)(2,1)S(1)} %slice.18), channel_id=1, source_target_pairs={{8,12},{10,14},{9,13},{11,15},{24,28},{26,30},{25,29},{27,31}} | collective-permute-start | bytes 1622024 | tf_op jit(solution)/shard_map/ppermute | solution.py:188
  95.6 13.0 %collective-permute-start.18 = (bf16[2,528,256]{2,1,0:T(8,128)(2,1)S(1)}, bf16[2,528,256]{2,1,0:T(8,128)(2,1)S(1)}, u32[]{:S(2)}, u32[]{:S(2)}) collective-permute-start(bf16[2,528,256]{2,1,0:T(8,128)(2,1)S(1)} %slice.19), channel_id=1, source_target_pairs={{4,0},{6,2},{5,1},{7,3},{20,16},{22,18},{21,17},{23,19}} | collective-permute-start | bytes 1622024 | tf_op jit(solution)/shard_map/ppermute | solution.py:188
  110.6 3.4 %collective-permute-start.19 = (bf16[2,256,256]{2,1,0:T(8,128)(2,1)S(1)}, bf16[2,256,256]{2,1,0:T(8,128)(2,1)S(1)}, u32[]{:S(2)}, u32[]{:S(2)}) collective-permute-start(bf16[2,256,256]{2,1,0:T(8,128)(2,1)S(1)} %get-tuple-element.49), channel_id=1, source_target_pairs={{12,8},{14,10},{13,9},{15,11},{28,24},{30,26},{29,25},{31,27}} | collective-permute-start | bytes 786440 | tf_op jit(solution)/shard_map/ppermute | solution.py:188
  111.2 3.5 %collective-permute-start.21 = (bf16[2,256,256]{2,1,0:T(8,128)(2,1)S(1)}, bf16[2,256,256]{2,1,0:T(8,128)(2,1)S(1)}, u32[]{:S(2)}, u32[]{:S(2)}) collective-permute-start(bf16[2,256,256]{2,1,0:T(8,128)(2,1)S(1)} %get-tuple-element.51), channel_id=1, source_target_pairs={{12,14},{14,12},{13,15},{15,13},{28,30},{30,28},{29,31},{31,29}} | collective-permute-start | bytes 786440 | tf_op jit(solution)/shard_map/ppermute | solution.py:184
  111.9 11.7 %collective-permute-start.26 = (bf16[2,256,256]{2,1,0:T(8,128)(2,1)S(1)}, bf16[2,256,256]{2,1,0:T(8,128)(2,1)S(1)}, u32[]{:S(2)}, u32[]{:S(2)}) collective-permute-start(bf16[2,256,256]{2,1,0:T(8,128)(2,1)S(1)} %get-tuple-element.56), channel_id=1, source_target_pairs={{0,4},{2,6},{1,5},{3,7},{16,20},{18,22},{17,21},{19,23}} | collective-permute-start | bytes 786440 | tf_op jit(solution)/shard_map/ppermute | solution.py:188
  113.2 12.7 %collective-permute-start.28 = (bf16[2,256,256]{2,1,0:T(8,128)(2,1)S(1)}, bf16[2,256,256]{2,1,0:T(8,128)(2,1)S(1)}, u32[]{:S(2)}, u32[]{:S(2)}) collective-permute-start(bf16[2,256,256]{2,1,0:T(8,128)(2,1)S(1)} %get-tuple-element.58), channel_id=1, source_target_pairs={{0,2},{2,0},{1,3},{3,1},{16,18},{18,16},{17,19},{19,17}} | collective-permute-start | bytes 786440 | tf_op jit(solution)/shard_map/ppermute | solution.py:184
  114.0 14.0 %collective-permute-start.20 = (bf16[4,256,256]{2,1,0:T(8,128)(2,1)S(1)}, bf16[4,256,256]{2,1,0:T(8,128)(2,1)S(1)}, u32[]{:S(2)}, u32[]{:S(2)}) collective-permute-start(bf16[4,256,256]{2,1,0:T(8,128)(2,1)S(1)} %add_convert_fusion.8), channel_id=1, source_target_pairs={{8,10},{10,8},{12,14},{14,12},{9,11},{11,9},{13,15},{15,13},{24,26... | collective-permute-start | bytes 1572872 | tf_op jit(solution)/shard_map/ppermute | solution.py:184
  114.8 16.8 %collective-permute-start.22 = (bf16[4,256,256]{2,1,0:T(8,128)(2,1)S(1)}, bf16[4,256,256]{2,1,0:T(8,128)(2,1)S(1)}, u32[]{:S(2)}, u32[]{:S(2)}) collective-permute-start(bf16[4,256,256]{2,1,0:T(8,128)(2,1)S(1)} %add_convert_fusion.7), channel_id=1, source_target_pairs={{12,8},{14,10},{13,9},{15,11},{28,24},{30,26},{29,25},{31,27}} | collective-permute-start | bytes 1572872 | tf_op jit(solution)/shard_map/ppermute | solution.py:188
  123.7 16.8 %collective-permute-start.27 = (bf16[4,256,256]{2,1,0:T(8,128)(2,1)S(1)}, bf16[4,256,256]{2,1,0:T(8,128)(2,1)S(1)}, u32[]{:S(2)}, u32[]{:S(2)}) collective-permute-start(bf16[4,256,256]{2,1,0:T(8,128)(2,1)S(1)} %add_convert_fusion.4), channel_id=1, source_target_pairs={{0,2},{2,0},{4,6},{6,4},{1,3},{3,1},{5,7},{7,5},{16,18},{18,16},{2... | collective-permute-start | bytes 1572872 | tf_op jit(solution)/shard_map/ppermute | solution.py:184
  126.0 15.7 %collective-permute-start.29 = (bf16[4,256,256]{2,1,0:T(8,128)(2,1)S(1)}, bf16[4,256,256]{2,1,0:T(8,128)(2,1)S(1)}, u32[]{:S(2)}, u32[]{:S(2)}) collective-permute-start(bf16[4,256,256]{2,1,0:T(8,128)(2,1)S(1)} %add_convert_fusion.3), channel_id=1, source_target_pairs={{0,4},{2,6},{1,5},{3,7},{16,20},{18,22},{17,21},{19,23}} | collective-permute-start | bytes 1572872 | tf_op jit(solution)/shard_map/ppermute | solution.py:188
  127.3 19.7 %collective-permute-start.10 = (bf16[4,256,256]{2,1,0:T(8,128)(2,1)S(1)}, bf16[4,256,256]{2,1,0:T(8,128)(2,1)S(1)}, u32[]{:S(2)}, u32[]{:S(2)}) collective-permute-start(bf16[4,256,256]{2,1,0:T(8,128)(2,1)S(1)} %get-tuple-element.42), channel_id=1, source_target_pairs={{8,10},{10,8},{12,14},{14,12},{9,11},{11,9},{13,15},{15,13},{24,26... | collective-permute-start | bytes 1572872 | tf_op jit(solution)/shard_map/ppermute | solution.py:184
  128.0 30.3 %collective-permute-start.25 = (bf16[4,256,256]{2,1,0:T(8,128)(2,1)S(1)}, bf16[4,256,256]{2,1,0:T(8,128)(2,1)S(1)}, u32[]{:S(2)}, u32[]{:S(2)}) collective-permute-start(bf16[4,256,256]{2,1,0:T(8,128)(2,1)S(1)} %get-tuple-element.53), channel_id=1, source_target_pairs={{0,2},{2,0},{4,6},{6,4},{1,3},{3,1},{5,7},{7,5},{16,18},{18,16},{2... | collective-permute-start | bytes 1572872 | tf_op jit(solution)/shard_map/ppermute | solution.py:184
  131.6 14.9 %collective-permute-start.8 = (bf16[4,256,256]{2,1,0:T(8,128)(2,1)S(1)}, bf16[4,256,256]{2,1,0:T(8,128)(2,1)S(1)}, u32[]{:S(2)}, u32[]{:S(2)}) collective-permute-start(bf16[4,256,256]{2,1,0:T(8,128)(2,1)S(1)} %get-tuple-element.40), channel_id=1, source_target_pairs={{4,0},{6,2},{8,12},{10,14},{5,1},{7,3},{9,13},{11,15},{20,16},{22,... | collective-permute-start | bytes 1572872 | tf_op jit(solution)/shard_map/ppermute | solution.py:265
  140.4 15.7 %collective-permute-start.23 = (bf16[4,256,256]{2,1,0:T(8,128)(2,1)S(1)}, bf16[4,256,256]{2,1,0:T(8,128)(2,1)S(1)}, u32[]{:S(2)}, u32[]{:S(2)}) collective-permute-start(bf16[4,256,256]{2,1,0:T(8,128)(2,1)S(1)} %add_convert_fusion.6), channel_id=1, source_target_pairs={{8,4},{10,6},{12,8},{14,10},{9,5},{11,7},{13,9},{15,11},{24,20},{2... | collective-permute-start | bytes 1572872 | tf_op jit(solution)/shard_map/ppermute | solution.py:188
  141.9 16.4 %collective-permute-start.30 = (bf16[4,256,256]{2,1,0:T(8,128)(2,1)S(1)}, bf16[4,256,256]{2,1,0:T(8,128)(2,1)S(1)}, u32[]{:S(2)}, u32[]{:S(2)}) collective-permute-start(bf16[4,256,256]{2,1,0:T(8,128)(2,1)S(1)} %add_convert_fusion.2), channel_id=1, source_target_pairs={{0,4},{2,6},{4,8},{6,10},{1,5},{3,7},{5,9},{7,11},{16,20},{18,22},... | collective-permute-start | bytes 1572872 | tf_op jit(solution)/shard_map/ppermute | solution.py:188
  146.7 17.9 %collective-permute-start.9 = (bf16[4,256,256]{2,1,0:T(8,128)(2,1)S(1)}, bf16[4,256,256]{2,1,0:T(8,128)(2,1)S(1)}, u32[]{:S(2)}, u32[]{:S(2)}) collective-permute-start(bf16[4,256,256]{2,1,0:T(8,128)(2,1)S(1)} %add_convert_fusion.9), channel_id=1, source_target_pairs={{0,2},{2,0},{4,6},{6,4},{8,10},{10,8},{12,14},{14,12},{1,3},{3,1},... | collective-permute-start | bytes 1572872 | tf_op jit(solution)/shard_map/ppermute | solution.py:184
  156.4 11.1 %collective-permute-start.24 = (bf16[4,256,256]{2,1,0:T(8,128)(2,1)S(1)}, bf16[4,256,256]{2,1,0:T(8,128)(2,1)S(1)}, u32[]{:S(2)}, u32[]{:S(2)}) collective-permute-start(bf16[4,256,256]{2,1,0:T(8,128)(2,1)S(1)} %add_convert_fusion.5), channel_id=1, source_target_pairs={{4,0},{6,2},{8,4},{10,6},{12,8},{14,10},{5,1},{7,3},{9,5},{11,7},{... | collective-permute-start | bytes 1572872 | tf_op jit(solution)/shard_map/ppermute | solution.py:188
  158.6 11.1 %collective-permute-start.31 = (bf16[4,256,256]{2,1,0:T(8,128)(2,1)S(1)}, bf16[4,256,256]{2,1,0:T(8,128)(2,1)S(1)}, u32[]{:S(2)}, u32[]{:S(2)}) collective-permute-start(bf16[4,256,256]{2,1,0:T(8,128)(2,1)S(1)} %add_convert_fusion.1), channel_id=1, source_target_pairs={{0,4},{2,6},{4,8},{6,10},{8,12},{10,14},{1,5},{3,7},{5,9},{7,11},{... | collective-permute-start | bytes 1572872 | tf_op jit(solution)/shard_map/ppermute | solution.py:188
  (5 other events, 4.0 us)

commit v4 on v3

--- a/solution.py
+++ b/solution.py
@@ -239,7 +239,7 @@
         side = 1 - y if kind.startswith("y") else y
         return jnp.where((there >= 0) & (there < n_z), 2 * there + side, -1)
 
-    stages = [[("up", 0), ("y", 0)], [("up", 1), ("down", 1)]]
+    stages = [[("up", 0)], [("y", 0), ("up", 1), ("down", 1)]]
     stages.append([("up", 2), ("down", 2), ("y_up", 1), ("y_down", 1), ("y_edge", 1)])
     for k in range(3, n_z):
         stages.append([("up", k), ("down", k), ("y_up", k - 1), ("y_down", k - 1)])

time: 172 us -> 167 us (0.971)
  starting transfers between devices: 64.2 us -> 57.6 us
    ppermute x16, starting transfers between devices: 36.2 us -> 30.9 us  [shift(): return lax.ppermute(x, 'row', pairs)]
    ppermute x16, waiting for transfers between devices: 41.4 us -> 46.3 us  [shift(): return lax.ppermute(x, 'row', pairs)]
    ppermute x14, waiting for transfers between devices: 7.06 us -> 2.43 us  [swap(): return lax.ppermute(x, 'row', pairs)]
    ppermute x14, starting transfers between devices: 22 us -> 18.6 us  [swap(): return lax.ppermute(x, 'row', pairs)]
    ppermute x1, starting transfers between devices: 4.65 us -> 6.76 us  [body(): lax.ppermute(parts['y_edge', 1], 'row', [(j, i) for i, j in edge])]
  transfers between devices with their start and end apart: 32 -> 32, of which waited for: 9 -> 10; matrix products, arithmetic and copies ran while one was open for 2% -> 3% of each run, Pallas kernels for 20% -> 22%
where the time goes in v4:
time: 167 us; the launch traced here: 165 us
  starting transfers between devices  57.6 us (34%)
  waiting for transfers between devices  48.7 us (29%)
  Pallas kernels  38.1 us (23%)
  local copies, waits for them, and re-layouts  15.3 us (9%)
  other arithmetic  3.94 us (2%)
    ppermute x16, waiting for transfers between devices, shift(): return lax.ppermute(x, 'row', pairs)  46.3 us
    pallas_call x5, Pallas kernels, stage_grads(): pl.pallas_call(functools.partial(grads_kernel, offsets, not carry), out_s...  35.2 us
    ppermute x16, starting transfers between devices, shift(): return lax.ppermute(x, 'row', pairs)  30.9 us
    ppermute x14, starting transfers between devices, swap(): return lax.ppermute(x, 'row', pairs)  18.6 us
    unnamed x45, local copies, waits for them, and re-layouts  13.4 us
    ppermute x1, starting transfers between devices, body(): lax.ppermute(parts['y_edge', 1], 'row', [(j, i) for i, j in edge])  6.76 us
  transfers between devices with their start and end apart: 32, of which 10 were waited for; matrix products, arithmetic and copies ran while one was open for 3% of the time, Pallas kernels for 22%

profile of v4, /device:TPU:10, one launch (start us, length us, event | category | flops | bytes accessed | tf_op | source)
XLA Modules:
  0.0 165.0 jit_solution(14114104528568919411)
XLA Ops:
  0.6 1.3 copy.13
  3.4 3.5 %collective-permute-start.1 = (bf16[4,528,256]{2,1,0:T(8,128)(2,1)S(1)}, bf16[4,528,256]{2,1,0:T(8,128)(2,1)}, u32[]{:S(2)}, u32[]{:S(2)}) collective-permute-start(bf16[4,528,256]{2,1,0:T(8,128)(2,1)S(1)} %maximum_maximum_fusion.refs_0_), channel_id=1, source_target_pairs={{0,4},{2,6},{4,8},{6,10},{8,12},{10,14},{1,5},{3,7},{5,9},{7,11},{... | collective-permute-start | bytes 3244040 | tf_op jit(solution)/shard_map/ppermute | solution.py:188
  6.9 3.4 %collective-permute-start.2 = (bf16[4,528,256]{2,1,0:T(8,128)(2,1)S(1)}, bf16[4,528,256]{2,1,0:T(8,128)(2,1)S(1)}, u32[]{:S(2)}, u32[]{:S(2)}) collective-permute-start(bf16[4,528,256]{2,1,0:T(8,128)(2,1)S(1)} %maximum_maximum_fusion.refs_0_), channel_id=1, source_target_pairs={{4,0},{6,2},{8,4},{10,6},{12,8},{14,10},{5,1},{7,3},{9,5},{11,7},{... | collective-permute-start | bytes 3244040 | tf_op jit(solution)/shard_map/ppermute | solution.py:188
  10.3 1.6 collective-permute-start
  12.6 2.8 %shard_map.112 = (s32[8]{0:T(128)}, s32[256]{0:T(256)}) custom-call(s32[1]{0:T(128)} %bitcast.1.here_ref, s32[32]{0:T(128)} %slot_ref.1, s32[256]{0:T(256)} %reshape.40.near_ref, s32[32]{0:T(128)} %live_ref.1), custom_call_target="tpu_custom_call" | custom-call | tf_op jit(solution)/shard_map/pallas_call | solution.py:58
  15.8 15.2 %collective-permute-done.1.refs_1_ = bf16[4,528,256]{2,1,0:T(8,128)(2,1)} collective-permute-done((bf16[4,528,256]{2,1,0:T(8,128)(2,1)S(1)}, bf16[4,528,256]{2,1,0:T(8,128)(2,1)}, u32[]{:S(2)}, u32[]{:S(2)}) %collective-permute-start.1) | collective-permute-done | bytes 1081376 | tf_op jit(solution)/shard_map/ppermute | solution.py:188
  31.0 4.5 %collective-permute-start.3 = (bf16[4,528,256]{2,1,0:T(8,128)(2,1)}, bf16[4,528,256]{2,1,0:T(8,128)(2,1)}, u32[]{:S(2)}, u32[]{:S(2)}) collective-permute-start(bf16[4,528,256]{2,1,0:T(8,128)(2,1)} %collective-permute-done.1.refs_1_), channel_id=1, source_target_pairs={{4,8},{6,10},{8,12},{10,14},{5,9},{7,11},{9,13},{11,15},{20,24},{2... | collective-permute-start | bytes 3244040 | tf_op jit(solution)/shard_map/ppermute | solution.py:188
  36.2 1.9 %collective-permute-start.4 = (bf16[4,528,256]{2,1,0:T(8,128)(2,1)S(1)}, bf16[4,528,256]{2,1,0:T(8,128)(2,1)}, u32[]{:S(2)}, u32[]{:S(2)}) collective-permute-start(bf16[4,528,256]{2,1,0:T(8,128)(2,1)S(1)} %collective-permute-done.2.refs_2_), channel_id=1, source_target_pairs={{4,0},{6,2},{8,4},{10,6},{5,1},{7,3},{9,5},{11,7},{20,16},{22,18},... | collective-permute-start | bytes 3244040 | tf_op jit(solution)/shard_map/ppermute | solution.py:188
  38.2 3.4 %collective-permute-start.6 = (bf16[4,528,256]{2,1,0:T(8,128)(2,1)S(1)}, bf16[4,528,256]{2,1,0:T(8,128)(2,1)S(1)}, u32[]{:S(2)}, u32[]{:S(2)}) collective-permute-start(bf16[4,528,256]{2,1,0:T(8,128)(2,1)S(1)} %collective-permute-done.2.refs_2_), channel_id=1, source_target_pairs={{0,2},{2,0},{4,6},{6,4},{1,3},{3,1},{5,7},{7,5},{16,18},{18,16},{2... | collective-permute-start | bytes 3244040 | tf_op jit(solution)/shard_map/ppermute | solution.py:184
  41.6 1.3 collective-permute-start.7
  42.9 1.0 copy-done.6
  44.0 1.0 copy-done.9
  46.3 3.5 %shard_map.113 = (bf16[4,256,256]{2,1,0:T(8,128)(2,1)S(1)}, f32[4,256,256]{2,1,0:T(8,128)S(1)}, f32[4,256,256]{2,1,0:T(8,128)S(1)}) custom-call(s32[1]{0:T(128)} %bitcast.row_ref, s32[8]{0:T(128)S(1)} %copy-done.13, s32[256]{0:T(256)S(1)} %copy-done.12, bf16[4,256,256]{2,1,0:T(8,128)(2,1)S(1)} %bitcast.30, bf16[4,256,256]{2,1,0:T(8,128)(2,1)S(1)} %bitcast.35, ...), custom_call_target="tpu_custom_call" | custom-call | flops 3000000000 | bytes 2097152 | tf_op jit(solution)/shard_map/pallas_call | solution.py:154
  49.9 13.1 %shard_map.114 = (bf16[4,256,256]{2,1,0:T(8,128)(2,1)S(1)}, bf16[4,256,256]{2,1,0:T(8,128)(2,1)S(1)}, bf16[4,256,256]{2,1,0:T(8,128)(2,1)S(1)}, f32[4,256,256]{2,1,0:T(8,128)S(1)}, f32[4,256,256]{2,1,0:T(8,128)S(1)}) custom-call(s32[3]{0:T(128)S(1)} %pad_add_fusion.row_ref, s32[8]{0:T(128)S(1)} %copy-done.13, s32[256]{0:T(256)S(1)} %copy-done.12, ...), custom_call_target="tpu_custom_call" | custom-call | flops 8999999488 | bytes 6291456 | tf_op jit(solution)/shard_map/pallas_call | solution.py:154
  64.4 1.0 copy-done
  65.5 1.3 collective-permute-start.12
  66.9 1.0 copy-done.2
  67.8 3.3 %collective-permute-start.14 = (bf16[4,528,256]{2,1,0:T(8,128)(2,1)}, bf16[4,528,256]{2,1,0:T(8,128)(2,1)S(1)}, u32[]{:S(2)}, u32[]{:S(2)}) collective-permute-start(bf16[4,528,256]{2,1,0:T(8,128)(2,1)} %collective-permute-done.4.refs_1_), channel_id=1, source_target_pairs={{0,2},{2,0},{4,6},{6,4},{1,3},{3,1},{5,7},{7,5},{16,18},{18,16},{2... | collective-permute-start | bytes 3244040 | tf_op jit(solution)/shard_map/ppermute | solution.py:184
  71.2 1.0 copy-done.4
  72.2 1.2 copy-done.1
  73.4 1.2 copy-done.3
  74.6 1.2 copy-done.5
  75.9 13.7 %shard_map.115 = (bf16[4,256,256]{2,1,0:T(8,128)(2,1)S(1)}, bf16[4,256,256]{2,1,0:T(8,128)(2,1)S(1)}, bf16[4,256,256]{2,1,0:T(8,128)(2,1)S(1)}, bf16[4,256,256]{...) custom-call(s32[5]{0:T(128)S(1)} %stack.69.row_ref, ...), custom_call_target="tpu_custom_call" | custom-call | flops 15000000512 | bytes 10485760 | tf_op jit(solution)/shard_map/pallas_call | solution.py:154
  89.6 1.0 copy-done.14
  93.0 1.1 collective-permute-done.14.refs_3_
  94.1 2.9 %collective-permute-start.18 = (bf16[2,528,256]{2,1,0:T(8,128)(2,1)S(1)}, bf16[2,528,256]{2,1,0:T(8,128)(2,1)S(1)}, u32[]{:S(2)}, u32[]{:S(2)}) collective-permute-start(bf16[2,528,256]{2,1,0:T(8,128)(2,1)S(1)} %slice.19), channel_id=1, source_target_pairs={{4,0},{6,2},{5,1},{7,3},{20,16},{22,18},{21,17},{23,19}} | collective-permute-start | bytes 1622024 | tf_op jit(solution)/shard_map/ppermute | solution.py:188
  97.0 3.0 %shard_map.116 = (bf16[4,256,256]{2,1,0:T(8,128)(2,1)S(1)}, bf16[4,256,256]{2,1,0:T(8,128)(2,1)S(1)}, bf16[4,256,256]{2,1,0:T(8,128)(2,1)S(1)}, bf16[4,256,256]{...) custom-call(s32[4]{0:T(128)S(1)} %pad_add_fusion.1.row_ref, s32[8]{0:T(128)S(1)} %copy-done.13, ...), custom_call_target="tpu_custom_call" | custom-call | flops 12000000000 | bytes 8388608 | tf_op jit(solution)/shard_map/pallas_call | solution.py:154
  100.1 5.6 %collective-permute-done.18.refs_3_ = bf16[2,528,256]{2,1,0:T(8,128)(2,1)S(1)} collective-permute-done((bf16[2,528,256]{2,1,0:T(8,128)(2,1)S(1)}, bf16[2,528,256]{2,1,0:T(8,128)(2,1)S(1)}, u32[]{:S(2)}, u32[]{:S(2)}) %collective-permute-start.18) | collective-permute-done | bytes 540704 | tf_op jit(solution)/shard_map/ppermute | solution.py:188
  105.7 1.9 %shard_map.117 = (bf16[2,256,256]{2,1,0:T(8,128)(2,1)S(1)}, bf16[2,256,256]{2,1,0:T(8,128)(2,1)S(1)}, bf16[2,256,256]{2,1,0:T(8,128)(2,1)S(1)}, bf16[2,256,256]{...) custom-call(s32[4]{0:T(128)S(1)} %pad_add_fusion.2.row_ref, s32[8]{0:T(128)S(1)} %copy-done.13, ...), custom_call_target="tpu_custom_call" | custom-call | flops 12000000000 | bytes 8388608 | tf_op jit(solution)/shard_map/pallas_call | solution.py:154
  109.0 1.3 collective-permute-start.26
  112.5 8.1 %collective-permute-done.26 = bf16[2,256,256]{2,1,0:T(8,128)(2,1)S(1)} collective-permute-done((bf16[2,256,256]{2,1,0:T(8,128)(2,1)S(1)}, bf16[2,256,256]{2,1,0:T(8,128)(2,1)S(1)}, u32[]{:S(2)}, u32[]{:S(2)}) %collective-permute-start.26) | collective-permute-done | bytes 262176 | tf_op jit(solution)/shard_map/ppermute | solution.py:188
  120.7 1.9 %collective-permute-start.27 = (bf16[4,256,256]{2,1,0:T(8,128)(2,1)S(1)}, bf16[4,256,256]{2,1,0:T(8,128)(2,1)S(1)}, u32[]{:S(2)}, u32[]{:S(2)}) collective-permute-start(bf16[4,256,256]{2,1,0:T(8,128)(2,1)S(1)} %add_convert_fusion.4), channel_id=1, source_target_pairs={{0,2},{2,0},{4,6},{6,4},{1,3},{3,1},{5,7},{7,5},{16,18},{18,16},{2... | collective-permute-start | bytes 1572872 | tf_op jit(solution)/shard_map/ppermute | solution.py:184
  122.7 1.3 collective-permute-start.29
  124.0 6.8 %collective-permute-start.8 = (bf16[4,256,256]{2,1,0:T(8,128)(2,1)S(1)}, bf16[4,256,256]{2,1,0:T(8,128)(2,1)S(1)}, u32[]{:S(2)}, u32[]{:S(2)}) collective-permute-start(bf16[4,256,256]{2,1,0:T(8,128)(2,1)S(1)} %get-tuple-element.40), channel_id=1, source_target_pairs={{4,0},{6,2},{8,12},{10,14},{5,1},{7,3},{9,13},{11,15},{20,16},{22,... | collective-permute-start | bytes 1572872 | tf_op jit(solution)/shard_map/ppermute | solution.py:265
  131.5 1.9 %collective-permute-start.25 = (bf16[4,256,256]{2,1,0:T(8,128)(2,1)S(1)}, bf16[4,256,256]{2,1,0:T(8,128)(2,1)S(1)}, u32[]{:S(2)}, u32[]{:S(2)}) collective-permute-start(bf16[4,256,256]{2,1,0:T(8,128)(2,1)S(1)} %get-tuple-element.53), channel_id=1, source_target_pairs={{0,2},{2,0},{4,6},{6,4},{1,3},{3,1},{5,7},{7,5},{16,18},{18,16},{2... | collective-permute-start | bytes 1572872 | tf_op jit(solution)/shard_map/ppermute | solution.py:184
  133.7 1.3 collective-permute-done.27
  135.0 1.3 collective-permute-start.23
  136.3 1.9 %collective-permute-done.29 = bf16[4,256,256]{2,1,0:T(8,128)(2,1)S(1)} collective-permute-done((bf16[4,256,256]{2,1,0:T(8,128)(2,1)S(1)}, bf16[4,256,256]{2,1,0:T(8,128)(2,1)S(1)}, u32[]{:S(2)}, u32[]{:S(2)}) %collective-permute-start.29) | collective-permute-done | bytes 524320 | tf_op jit(solution)/shard_map/ppermute | solution.py:188
  138.4 2.7 %collective-permute-start.30 = (bf16[4,256,256]{2,1,0:T(8,128)(2,1)S(1)}, bf16[4,256,256]{2,1,0:T(8,128)(2,1)S(1)}, u32[]{:S(2)}, u32[]{:S(2)}) collective-permute-start(bf16[4,256,256]{2,1,0:T(8,128)(2,1)S(1)} %add_convert_fusion.2), channel_id=1, source_target_pairs={{0,4},{2,6},{4,8},{6,10},{1,5},{3,7},{5,9},{7,11},{16,20},{18,22},... | collective-permute-start | bytes 1572872 | tf_op jit(solution)/shard_map/ppermute | solution.py:188
  142.0 6.2 %collective-permute-done.23 = bf16[4,256,256]{2,1,0:T(8,128)(2,1)S(1)} collective-permute-done((bf16[4,256,256]{2,1,0:T(8,128)(2,1)S(1)}, bf16[4,256,256]{2,1,0:T(8,128)(2,1)S(1)}, u32[]{:S(2)}, u32[]{:S(2)}) %collective-permute-start.23) | collective-permute-done | bytes 524320 | tf_op jit(solution)/shard_map/ppermute | solution.py:188
  148.4 1.9 %collective-permute-start.24 = (bf16[4,256,256]{2,1,0:T(8,128)(2,1)S(1)}, bf16[4,256,256]{2,1,0:T(8,128)(2,1)S(1)}, u32[]{:S(2)}, u32[]{:S(2)}) collective-permute-start(bf16[4,256,256]{2,1,0:T(8,128)(2,1)S(1)} %add_convert_fusion.5), channel_id=1, source_target_pairs={{4,0},{6,2},{8,4},{10,6},{12,8},{14,10},{5,1},{7,3},{9,5},{11,7},{... | collective-permute-start | bytes 1572872 | tf_op jit(solution)/shard_map/ppermute | solution.py:188
  150.4 2.0 %collective-permute-done.30 = bf16[4,256,256]{2,1,0:T(8,128)(2,1)S(1)} collective-permute-done((bf16[4,256,256]{2,1,0:T(8,128)(2,1)S(1)}, bf16[4,256,256]{2,1,0:T(8,128)(2,1)S(1)}, u32[]{:S(2)}, u32[]{:S(2)}) %collective-permute-start.30) | collective-permute-done | bytes 524320 | tf_op jit(solution)/shard_map/ppermute | solution.py:188
  152.6 2.2 %collective-permute-start.31 = (bf16[4,256,256]{2,1,0:T(8,128)(2,1)S(1)}, bf16[4,256,256]{2,1,0:T(8,128)(2,1)S(1)}, u32[]{:S(2)}, u32[]{:S(2)}) collective-permute-start(bf16[4,256,256]{2,1,0:T(8,128)(2,1)S(1)} %add_convert_fusion.1), channel_id=1, source_target_pairs={{0,4},{2,6},{4,8},{6,10},{8,12},{10,14},{1,5},{3,7},{5,9},{7,11},{... | collective-permute-start | bytes 1572872 | tf_op jit(solution)/shard_map/ppermute | solution.py:188
  154.8 0.8 convert_element_type.169
  155.7 0.9 multiply_convert_fusion
  156.5 3.0 %collective-permute-done.24 = bf16[4,256,256]{2,1,0:T(8,128)(2,1)S(1)} collective-permute-done((bf16[4,256,256]{2,1,0:T(8,128)(2,1)S(1)}, bf16[4,256,256]{2,1,0:T(8,128)(2,1)S(1)}, u32[]{:S(2)}, u32[]{:S(2)}) %collective-permute-start.24) | collective-permute-done | bytes 524320 | tf_op jit(solution)/shard_map/ppermute | solution.py:188
  159.5 4.2 %collective-permute-done.31 = bf16[4,256,256]{2,1,0:T(8,128)(2,1)S(1)} collective-permute-done((bf16[4,256,256]{2,1,0:T(8,128)(2,1)S(1)}, bf16[4,256,256]{2,1,0:T(8,128)(2,1)S(1)}, u32[]{:S(2)}, u32[]{:S(2)}) %collective-permute-start.31) | collective-permute-done | bytes 524320 | tf_op jit(solution)/shard_map/ppermute | solution.py:188
  164.0 1.0 copy.15
  (94 shorter events, 14.8 us)
Async XLA Ops:
  0.6 1.3 copy-start.18
  2.0 1.0 copy-start.16
  2.0 1.2 copy-start.17
  3.2 8.7 %copy-start.20 = (s32[32,8]{0,1:T(8,128)S(1)}, s32[32,8]{0,1:T(8,128)}, u32[]{:S(2)}) copy-start(s32[32,8]{0,1:T(8,128)} %param.16) | copy-start | bytes 3076
  3.4 27.6 %collective-permute-start.1 = (bf16[4,528,256]{2,1,0:T(8,128)(2,1)S(1)}, bf16[4,528,256]{2,1,0:T(8,128)(2,1)}, u32[]{:S(2)}, u32[]{:S(2)}) collective-permute-start(bf16[4,528,256]{2,1,0:T(8,128)(2,1)S(1)} %maximum_maximum_fusion.refs_0_), channel_id=1, source_target_pairs={{0,4},{2,6},{4,8},{6,10},{8,12},{10,14},{1,5},{3,7},{5,9},{7,11},{... | collective-permute-start | bytes 3244040 | tf_op jit(solution)/shard_map/ppermute | solution.py:188
  6.9 29.3 %collective-permute-start.2 = (bf16[4,528,256]{2,1,0:T(8,128)(2,1)S(1)}, bf16[4,528,256]{2,1,0:T(8,128)(2,1)S(1)}, u32[]{:S(2)}, u32[]{:S(2)}) collective-permute-start(bf16[4,528,256]{2,1,0:T(8,128)(2,1)S(1)} %maximum_maximum_fusion.refs_0_), channel_id=1, source_target_pairs={{4,0},{6,2},{8,4},{10,6},{12,8},{14,10},{5,1},{7,3},{9,5},{11,7},{... | collective-permute-start | bytes 3244040 | tf_op jit(solution)/shard_map/ppermute | solution.py:188
  10.3 31.3 %collective-permute-start = (bf16[4,528,256]{2,1,0:T(8,128)(2,1)S(1)}, bf16[4,528,256]{2,1,0:T(8,128)(2,1)S(1)}, u32[]{:S(2)}, u32[]{:S(2)}) collective-permute-start(bf16[4,528,256]{2,1,0:T(8,128)(2,1)S(1)} %maximum_maximum_fusion.refs_0_), channel_id=1, source_target_pairs={{0,2},{2,0},{4,6},{6,4},{8,10},{10,8},{12,14},{14,12},{1,3},{3,1},... | collective-permute-start | bytes 3244040 | tf_op jit(solution)/shard_map/ppermute | solution.py:184
  31.0 31.9 %collective-permute-start.3 = (bf16[4,528,256]{2,1,0:T(8,128)(2,1)}, bf16[4,528,256]{2,1,0:T(8,128)(2,1)}, u32[]{:S(2)}, u32[]{:S(2)}) collective-permute-start(bf16[4,528,256]{2,1,0:T(8,128)(2,1)} %collective-permute-done.1.refs_1_), channel_id=1, source_target_pairs={{4,8},{6,10},{8,12},{10,14},{5,9},{7,11},{9,13},{11,15},{20,24},{2... | collective-permute-start | bytes 3244040 | tf_op jit(solution)/shard_map/ppermute | solution.py:188
  35.5 28.9 %collective-permute-start.5 = (bf16[4,528,256]{2,1,0:T(8,128)(2,1)}, bf16[4,528,256]{2,1,0:T(8,128)(2,1)S(1)}, u32[]{:S(2)}, u32[]{:S(2)}) collective-permute-start(bf16[4,528,256]{2,1,0:T(8,128)(2,1)} %collective-permute-done.1.refs_1_), channel_id=1, source_target_pairs={{8,10},{10,8},{12,14},{14,12},{9,11},{11,9},{13,15},{15,13},{24,26... | collective-permute-start | bytes 3244040 | tf_op jit(solution)/shard_map/ppermute | solution.py:184
  36.2 27.4 %collective-permute-start.4 = (bf16[4,528,256]{2,1,0:T(8,128)(2,1)S(1)}, bf16[4,528,256]{2,1,0:T(8,128)(2,1)}, u32[]{:S(2)}, u32[]{:S(2)}) collective-permute-start(bf16[4,528,256]{2,1,0:T(8,128)(2,1)S(1)} %collective-permute-done.2.refs_2_), channel_id=1, source_target_pairs={{4,0},{6,2},{8,4},{10,6},{5,1},{7,3},{9,5},{11,7},{20,16},{22,18},... | collective-permute-start | bytes 3244040 | tf_op jit(solution)/shard_map/ppermute | solution.py:188
  38.2 28.7 %collective-permute-start.6 = (bf16[4,528,256]{2,1,0:T(8,128)(2,1)S(1)}, bf16[4,528,256]{2,1,0:T(8,128)(2,1)S(1)}, u32[]{:S(2)}, u32[]{:S(2)}) collective-permute-start(bf16[4,528,256]{2,1,0:T(8,128)(2,1)S(1)} %collective-permute-done.2.refs_2_), channel_id=1, source_target_pairs={{0,2},{2,0},{4,6},{6,4},{1,3},{3,1},{5,7},{7,5},{16,18},{18,16},{2... | collective-permute-start | bytes 3244040 | tf_op jit(solution)/shard_map/ppermute | solution.py:184
  41.6 29.5 %collective-permute-start.7 = (bf16[4,528,256]{2,1,0:T(8,128)(2,1)S(1)}, bf16[4,528,256]{2,1,0:T(8,128)(2,1)S(1)}, u32[]{:S(2)}, u32[]{:S(2)}) collective-permute-start(bf16[4,528,256]{2,1,0:T(8,128)(2,1)S(1)} %collective-permute-done.refs_0_), channel_id=1, source_target_pairs={{0,4},{2,6},{12,8},{14,10},{1,5},{3,7},{13,9},{15,11},{16,20},{18,... | collective-permute-start | bytes 3244040 | tf_op jit(solution)/shard_map/ppermute | solution.py:216
  42.9 1.0 copy-start.6
  44.0 1.0 copy-start.9
  46.3 3.5 %copy-start.7 = (bf16[1024,256]{1,0:T(8,128)(2,1)S(1)}, bf16[1024,256]{1,0:T(8,128)(2,1)}, u32[]{:S(2)}) copy-start(bf16[1024,256]{1,0:T(8,128)(2,1)} %param.10) | copy-start | bytes 1572868
  46.3 3.6 %copy-start.10 = (bf16[1024,256]{1,0:T(8,128)(2,1)S(1)}, bf16[1024,256]{1,0:T(8,128)(2,1)}, u32[]{:S(2)}) copy-start(bf16[1024,256]{1,0:T(8,128)(2,1)} %param.11) | copy-start | bytes 1572868
  49.8 22.3 %copy-start.8 = (bf16[1024,256]{1,0:T(8,128)(2,1)S(1)}, bf16[1024,256]{1,0:T(8,128)(2,1)}, u32[]{:S(2)}) copy-start(bf16[1024,256]{1,0:T(8,128)(2,1)} %param.10) | copy-start | bytes 1572868
  49.9 22.3 %copy-start.11 = (bf16[1024,256]{1,0:T(8,128)(2,1)S(1)}, bf16[1024,256]{1,0:T(8,128)(2,1)}, u32[]{:S(2)}) copy-start(bf16[1024,256]{1,0:T(8,128)(2,1)} %param.11) | copy-start | bytes 1572868
  62.9 27.7 %collective-permute-start.11 = (bf16[4,528,256]{2,1,0:T(8,128)(2,1)}, bf16[4,528,256]{2,1,0:T(8,128)(2,1)S(1)}, u32[]{:S(2)}, u32[]{:S(2)}) collective-permute-start(bf16[4,528,256]{2,1,0:T(8,128)(2,1)} %collective-permute-done.3.refs_0_), channel_id=1, source_target_pairs={{8,12},{10,14},{9,13},{11,15},{24,28},{26,30},{25,29},{27,31}} | collective-permute-start | bytes 3244040 | tf_op jit(solution)/shard_map/ppermute | solution.py:188
  63.7 28.6 %collective-permute-start.13 = (bf16[4,528,256]{2,1,0:T(8,128)(2,1)}, bf16[4,528,256]{2,1,0:T(8,128)(2,1)S(1)}, u32[]{:S(2)}, u32[]{:S(2)}) collective-permute-start(bf16[4,528,256]{2,1,0:T(8,128)(2,1)} %collective-permute-done.3.refs_0_), channel_id=1, source_target_pairs={{8,10},{10,8},{12,14},{14,12},{9,11},{11,9},{13,15},{15,13},{24,26... | collective-permute-start | bytes 3244040 | tf_op jit(solution)/shard_map/ppermute | solution.py:184
  64.4 1.0 copy-start
  65.5 25.9 %collective-permute-start.12 = (bf16[4,528,256]{2,1,0:T(8,128)(2,1)}, bf16[4,528,256]{2,1,0:T(8,128)(2,1)S(1)}, u32[]{:S(2)}, u32[]{:S(2)}) collective-permute-start(bf16[4,528,256]{2,1,0:T(8,128)(2,1)} %collective-permute-done.4.refs_1_), channel_id=1, source_target_pairs={{4,0},{6,2},{5,1},{7,3},{20,16},{22,18},{21,17},{23,19}} | collective-permute-start | bytes 3244040 | tf_op jit(solution)/shard_map/ppermute | solution.py:188
  67.8 26.3 %collective-permute-start.14 = (bf16[4,528,256]{2,1,0:T(8,128)(2,1)}, bf16[4,528,256]{2,1,0:T(8,128)(2,1)S(1)}, u32[]{:S(2)}, u32[]{:S(2)}) collective-permute-start(bf16[4,528,256]{2,1,0:T(8,128)(2,1)} %collective-permute-done.4.refs_1_), channel_id=1, source_target_pairs={{0,2},{2,0},{4,6},{6,4},{1,3},{3,1},{5,7},{7,5},{16,18},{18,16},{2... | collective-permute-start | bytes 3244040 | tf_op jit(solution)/shard_map/ppermute | solution.py:184
  71.2 1.0 copy-start.4
  72.2 1.2 copy-start.1
  73.4 1.2 copy-start.3
  74.6 1.2 copy-start.5
  90.7 9.4 %collective-permute-start.15 = (bf16[2,528,256]{2,1,0:T(8,128)(2,1)S(1)}, bf16[2,528,256]{2,1,0:T(8,128)(2,1)S(1)}, u32[]{:S(2)}, u32[]{:S(2)}) collective-permute-start(bf16[2,528,256]{2,1,0:T(8,128)(2,1)S(1)} %slice.16), channel_id=1, source_target_pairs={{12,14},{14,12},{13,15},{15,13},{28,30},{30,28},{29,31},{31,29}} | collective-permute-start | bytes 1622024 | tf_op jit(solution)/shard_map/ppermute | solution.py:184
  91.4 5.6 %copy-start.15 = (f32[4,256,256]{2,1,0:T(8,128)S(1)}, f32[4,256,256]{2,1,0:T(8,128)}, u32[]{:S(2)}) copy-start(f32[4,256,256]{2,1,0:T(8,128)} %copy-done.14) | copy-start | bytes 3145732
  91.4 8.6 %collective-permute-start.16 = (bf16[2,528,256]{2,1,0:T(8,128)(2,1)S(1)}, bf16[2,528,256]{2,1,0:T(8,128)(2,1)S(1)}, u32[]{:S(2)}, u32[]{:S(2)}) collective-permute-start(bf16[2,528,256]{2,1,0:T(8,128)(2,1)S(1)} %slice.17), channel_id=1, source_target_pairs={{0,2},{2,0},{1,3},{3,1},{16,18},{18,16},{17,19},{19,17}} | collective-permute-start | bytes 1622024 | tf_op jit(solution)/shard_map/ppermute | solution.py:184
  92.3 7.8 %collective-permute-start.17 = (bf16[2,528,256]{2,1,0:T(8,128)(2,1)S(1)}, bf16[2,528,256]{2,1,0:T(8,128)(2,1)S(1)}, u32[]{:S(2)}, u32[]{:S(2)}) collective-permute-start(bf16[2,528,256]{2,1,0:T(8,128)(2,1)S(1)} %slice.18), channel_id=1, source_target_pairs={{8,12},{10,14},{9,13},{11,15},{24,28},{26,30},{25,29},{27,31}} | collective-permute-start | bytes 1622024 | tf_op jit(solution)/shard_map/ppermute | solution.py:188
  94.1 11.5 %collective-permute-start.18 = (bf16[2,528,256]{2,1,0:T(8,128)(2,1)S(1)}, bf16[2,528,256]{2,1,0:T(8,128)(2,1)S(1)}, u32[]{:S(2)}, u32[]{:S(2)}) collective-permute-start(bf16[2,528,256]{2,1,0:T(8,128)(2,1)S(1)} %slice.19), channel_id=1, source_target_pairs={{4,0},{6,2},{5,1},{7,3},{20,16},{22,18},{21,17},{23,19}} | collective-permute-start | bytes 1622024 | tf_op jit(solution)/shard_map/ppermute | solution.py:188
  107.6 3.4 %collective-permute-start.19 = (bf16[2,256,256]{2,1,0:T(8,128)(2,1)S(1)}, bf16[2,256,256]{2,1,0:T(8,128)(2,1)S(1)}, u32[]{:S(2)}, u32[]{:S(2)}) collective-permute-start(bf16[2,256,256]{2,1,0:T(8,128)(2,1)S(1)} %get-tuple-element.49), channel_id=1, source_target_pairs={{12,8},{14,10},{13,9},{15,11},{28,24},{30,26},{29,25},{31,27}} | collective-permute-start | bytes 786440 | tf_op jit(solution)/shard_map/ppermute | solution.py:188
  108.3 3.5 %collective-permute-start.21 = (bf16[2,256,256]{2,1,0:T(8,128)(2,1)S(1)}, bf16[2,256,256]{2,1,0:T(8,128)(2,1)S(1)}, u32[]{:S(2)}, u32[]{:S(2)}) collective-permute-start(bf16[2,256,256]{2,1,0:T(8,128)(2,1)S(1)} %get-tuple-element.51), channel_id=1, source_target_pairs={{12,14},{14,12},{13,15},{15,13},{28,30},{30,28},{29,31},{31,29}} | collective-permute-start | bytes 786440 | tf_op jit(solution)/shard_map/ppermute | solution.py:184
  109.0 11.7 %collective-permute-start.26 = (bf16[2,256,256]{2,1,0:T(8,128)(2,1)S(1)}, bf16[2,256,256]{2,1,0:T(8,128)(2,1)S(1)}, u32[]{:S(2)}, u32[]{:S(2)}) collective-permute-start(bf16[2,256,256]{2,1,0:T(8,128)(2,1)S(1)} %get-tuple-element.56), channel_id=1, source_target_pairs={{0,4},{2,6},{1,5},{3,7},{16,20},{18,22},{17,21},{19,23}} | collective-permute-start | bytes 786440 | tf_op jit(solution)/shard_map/ppermute | solution.py:188
  110.3 12.4 %collective-permute-start.28 = (bf16[2,256,256]{2,1,0:T(8,128)(2,1)S(1)}, bf16[2,256,256]{2,1,0:T(8,128)(2,1)S(1)}, u32[]{:S(2)}, u32[]{:S(2)}) collective-permute-start(bf16[2,256,256]{2,1,0:T(8,128)(2,1)S(1)} %get-tuple-element.58), channel_id=1, source_target_pairs={{0,2},{2,0},{1,3},{3,1},{16,18},{18,16},{17,19},{19,17}} | collective-permute-start | bytes 786440 | tf_op jit(solution)/shard_map/ppermute | solution.py:184
  111.0 19.8 %collective-permute-start.20 = (bf16[4,256,256]{2,1,0:T(8,128)(2,1)S(1)}, bf16[4,256,256]{2,1,0:T(8,128)(2,1)S(1)}, u32[]{:S(2)}, u32[]{:S(2)}) collective-permute-start(bf16[4,256,256]{2,1,0:T(8,128)(2,1)S(1)} %add_convert_fusion.8), channel_id=1, source_target_pairs={{8,10},{10,8},{12,14},{14,12},{9,11},{11,9},{13,15},{15,13},{24,26... | collective-permute-start | bytes 1572872 | tf_op jit(solution)/shard_map/ppermute | solution.py:184
  111.8 19.7 %collective-permute-start.22 = (bf16[4,256,256]{2,1,0:T(8,128)(2,1)S(1)}, bf16[4,256,256]{2,1,0:T(8,128)(2,1)S(1)}, u32[]{:S(2)}, u32[]{:S(2)}) collective-permute-start(bf16[4,256,256]{2,1,0:T(8,128)(2,1)S(1)} %add_convert_fusion.7), channel_id=1, source_target_pairs={{12,8},{14,10},{13,9},{15,11},{28,24},{30,26},{29,25},{31,27}} | collective-permute-start | bytes 1572872 | tf_op jit(solution)/shard_map/ppermute | solution.py:188
  120.7 14.3 %collective-permute-start.27 = (bf16[4,256,256]{2,1,0:T(8,128)(2,1)S(1)}, bf16[4,256,256]{2,1,0:T(8,128)(2,1)S(1)}, u32[]{:S(2)}, u32[]{:S(2)}) collective-permute-start(bf16[4,256,256]{2,1,0:T(8,128)(2,1)S(1)} %add_convert_fusion.4), channel_id=1, source_target_pairs={{0,2},{2,0},{4,6},{6,4},{1,3},{3,1},{5,7},{7,5},{16,18},{18,16},{2... | collective-permute-start | bytes 1572872 | tf_op jit(solution)/shard_map/ppermute | solution.py:184
  122.7 15.4 %collective-permute-start.29 = (bf16[4,256,256]{2,1,0:T(8,128)(2,1)S(1)}, bf16[4,256,256]{2,1,0:T(8,128)(2,1)S(1)}, u32[]{:S(2)}, u32[]{:S(2)}) collective-permute-start(bf16[4,256,256]{2,1,0:T(8,128)(2,1)S(1)} %add_convert_fusion.3), channel_id=1, source_target_pairs={{0,4},{2,6},{1,5},{3,7},{16,20},{18,22},{17,21},{19,23}} | collective-permute-start | bytes 1572872 | tf_op jit(solution)/shard_map/ppermute | solution.py:188
  124.0 17.1 %collective-permute-start.8 = (bf16[4,256,256]{2,1,0:T(8,128)(2,1)S(1)}, bf16[4,256,256]{2,1,0:T(8,128)(2,1)S(1)}, u32[]{:S(2)}, u32[]{:S(2)}) collective-permute-start(bf16[4,256,256]{2,1,0:T(8,128)(2,1)S(1)} %get-tuple-element.40), channel_id=1, source_target_pairs={{4,0},{6,2},{8,12},{10,14},{5,1},{7,3},{9,13},{11,15},{20,16},{22,... | collective-permute-start | bytes 1572872 | tf_op jit(solution)/shard_map/ppermute | solution.py:265
  130.8 11.2 %collective-permute-start.10 = (bf16[4,256,256]{2,1,0:T(8,128)(2,1)S(1)}, bf16[4,256,256]{2,1,0:T(8,128)(2,1)S(1)}, u32[]{:S(2)}, u32[]{:S(2)}) collective-permute-start(bf16[4,256,256]{2,1,0:T(8,128)(2,1)S(1)} %get-tuple-element.42), channel_id=1, source_target_pairs={{8,10},{10,8},{12,14},{14,12},{9,11},{11,9},{13,15},{15,13},{24,26... | collective-permute-start | bytes 1572872 | tf_op jit(solution)/shard_map/ppermute | solution.py:184
  131.5 18.9 %collective-permute-start.25 = (bf16[4,256,256]{2,1,0:T(8,128)(2,1)S(1)}, bf16[4,256,256]{2,1,0:T(8,128)(2,1)S(1)}, u32[]{:S(2)}, u32[]{:S(2)}) collective-permute-start(bf16[4,256,256]{2,1,0:T(8,128)(2,1)S(1)} %get-tuple-element.53), channel_id=1, source_target_pairs={{0,2},{2,0},{4,6},{6,4},{1,3},{3,1},{5,7},{7,5},{16,18},{18,16},{2... | collective-permute-start | bytes 1572872 | tf_op jit(solution)/shard_map/ppermute | solution.py:184
  135.0 13.2 %collective-permute-start.23 = (bf16[4,256,256]{2,1,0:T(8,128)(2,1)S(1)}, bf16[4,256,256]{2,1,0:T(8,128)(2,1)S(1)}, u32[]{:S(2)}, u32[]{:S(2)}) collective-permute-start(bf16[4,256,256]{2,1,0:T(8,128)(2,1)S(1)} %add_convert_fusion.6), channel_id=1, source_target_pairs={{8,4},{10,6},{12,8},{14,10},{9,5},{11,7},{13,9},{15,11},{24,20},{2... | collective-permute-start | bytes 1572872 | tf_op jit(solution)/shard_map/ppermute | solution.py:188
  138.4 14.1 %collective-permute-start.30 = (bf16[4,256,256]{2,1,0:T(8,128)(2,1)S(1)}, bf16[4,256,256]{2,1,0:T(8,128)(2,1)S(1)}, u32[]{:S(2)}, u32[]{:S(2)}) collective-permute-start(bf16[4,256,256]{2,1,0:T(8,128)(2,1)S(1)} %add_convert_fusion.2), channel_id=1, source_target_pairs={{0,4},{2,6},{4,8},{6,10},{1,5},{3,7},{5,9},{7,11},{16,20},{18,22},... | collective-permute-start | bytes 1572872 | tf_op jit(solution)/shard_map/ppermute | solution.py:188
  141.2 15.3 %collective-permute-start.9 = (bf16[4,256,256]{2,1,0:T(8,128)(2,1)S(1)}, bf16[4,256,256]{2,1,0:T(8,128)(2,1)S(1)}, u32[]{:S(2)}, u32[]{:S(2)}) collective-permute-start(bf16[4,256,256]{2,1,0:T(8,128)(2,1)S(1)} %add_convert_fusion.9), channel_id=1, source_target_pairs={{0,2},{2,0},{4,6},{6,4},{8,10},{10,8},{12,14},{14,12},{1,3},{3,1},... | collective-permute-start | bytes 1572872 | tf_op jit(solution)/shard_map/ppermute | solution.py:184
  148.4 11.1 %collective-permute-start.24 = (bf16[4,256,256]{2,1,0:T(8,128)(2,1)S(1)}, bf16[4,256,256]{2,1,0:T(8,128)(2,1)S(1)}, u32[]{:S(2)}, u32[]{:S(2)}) collective-permute-start(bf16[4,256,256]{2,1,0:T(8,128)(2,1)S(1)} %add_convert_fusion.5), channel_id=1, source_target_pairs={{4,0},{6,2},{8,4},{10,6},{12,8},{14,10},{5,1},{7,3},{9,5},{11,7},{... | collective-permute-start | bytes 1572872 | tf_op jit(solution)/shard_map/ppermute | solution.py:188
  152.6 11.1 %collective-permute-start.31 = (bf16[4,256,256]{2,1,0:T(8,128)(2,1)S(1)}, bf16[4,256,256]{2,1,0:T(8,128)(2,1)S(1)}, u32[]{:S(2)}, u32[]{:S(2)}) collective-permute-start(bf16[4,256,256]{2,1,0:T(8,128)(2,1)S(1)} %add_convert_fusion.1), channel_id=1, source_target_pairs={{0,4},{2,6},{4,8},{6,10},{8,12},{10,14},{1,5},{3,7},{5,9},{7,11},{... | collective-permute-start | bytes 1572872 | tf_op jit(solution)/shard_map/ppermute | solution.py:188
  (5 other events, 4.0 us)

commit v5 on v4

--- a/solution.py
+++ b/solution.py
@@ -162,7 +162,7 @@
             pltpu.VMEM((pairs, per_row, 2 * BLOCK, PAIR), jnp.bfloat16),
             pltpu.VMEM((pairs, per_row, PAIR, 2 * BLOCK), jnp.bfloat16),
         ],
-        compiler_params=pltpu.CompilerParams(vmem_limit_bytes=40 * 2**20),
+        compiler_params=pltpu.CompilerParams(vmem_limit_bytes=58 * 2**20),
         cost_estimate=pl.CostEstimate(
             flops=n_load * 3000000000, bytes_accessed=n_load * 2**21, transcendentals=0
         ),
@@ -204,11 +204,20 @@
     last = n_z - 1
     half = per_row // 2
     edge = [(j, 2 + j) for j in range(2)] + [(2 * last + j, 2 * last - 2 + j) for j in range(2)]
+    counts, entries = scan_lists(
+        here.reshape(1), block_slot, neighbours.reshape(-1), live_count, n_row
+    )
+
     have = {("up", 0): own, ("y", 0): swap(own, 0, n_z)}
+    (own_part,), carry = stage_grads(
+        here.reshape(1), counts, entries, key, value, [own], (0,), ()
+    )
     ups, downs = own, own
     for k in range(1, n_z):
         ups = shift(ups, 1, k - 1, last)
         downs = shift(downs, -1, 1, n_z - k + 1)
+        if k == 1:
+            ups, downs, carry, own_part = lax.optimization_barrier((ups, downs, carry, own_part))
         have[("up", k)], have[("down", k)] = ups, downs
         if k == 1:
             have[("y_up", 1)] = swap(ups, 2, n_z)
@@ -223,10 +232,6 @@
             have[("y_up_b", k)] = shift(have[("y_up", k - 1)][half:], 1, last - 1, last)
             have[("y_down_b", k)] = shift(have[("y_down", k - 1)][half:], -1, 1, 2)
 
-    counts, entries = scan_lists(
-        here.reshape(1), block_slot, neighbours.reshape(-1), live_count, n_row
-    )
-
     def named(kind, k):
         if kind == "y_edge":
             there = jnp.where(z == 1, 0, jnp.where(z == last - 1, last, -1))
@@ -239,12 +244,12 @@
         side = 1 - y if kind.startswith("y") else y
         return jnp.where((there >= 0) & (there < n_z), 2 * there + side, -1)
 
-    stages = [[("up", 0)], [("y", 0), ("up", 1), ("down", 1)]]
+    stages = [[("y", 0), ("up", 1), ("down", 1)]]
     stages.append([("up", 2), ("down", 2), ("y_up", 1), ("y_down", 1), ("y_edge", 1)])
     for k in range(3, n_z):
         stages.append([("up", k), ("down", k), ("y_up", k - 1), ("y_down", k - 1)])
     stages.append([(kind, last) for kind in ("y_up_a", "y_down_a", "y_up_b", "y_down_b")])
-    parts, carry = {}, ()
+    parts = {("up", 0): own_part}
     for stage in stages:
         rows = jnp.stack([named(*name) for name in stage]).astype(jnp.int32)
         offsets = tuple(half if name[0].endswith("_b") else 0 for name in stage)

time: 167 us -> 174 us (1.042)
  Pallas kernels: 38.1 us -> 55.1 us
  waiting for transfers between devices: 48.7 us -> 33.1 us
  starting transfers between devices: 57.6 us -> 69.6 us
  local copies, waits for them, and re-layouts: 15.3 us -> 6.88 us
    pallas_call x5, Pallas kernels: 35.2 us -> 52.3 us  [stage_grads(): pl.pallas_call(functools.partial(grads_kernel, offsets, not carry), out_s...]
    ppermute x16, waiting for transfers between devices: 46.3 us -> 31.9 us  [shift(): return lax.ppermute(x, 'row', pairs)]
    unnamed x45 -> x57, local copies, waits for them, and re-layouts: 13.4 us -> 3.29 us
    ppermute x16, starting transfers between devices: 30.9 us -> 38.2 us  [shift(): return lax.ppermute(x, 'row', pairs)]
    ppermute x14, starting transfers between devices: 18.6 us -> 25.6 us  [swap(): return lax.ppermute(x, 'row', pairs)]
    ppermute x1, starting transfers between devices: 6.76 us -> 4.61 us  [body(): lax.ppermute(parts['y_edge', 1], 'row', [(j, i) for i, j in edge])]
  transfers between devices with their start and end apart: 32 -> 32, of which waited for: 10 -> 10; matrix products, arithmetic and copies ran while one was open for 3% -> 4% of each run, Pallas kernels for 22% -> 29%
where the time goes in v5:
time: 174 us; the launch traced here: 171 us
  starting transfers between devices  69.6 us (40%)
  Pallas kernels  55.1 us (32%)
  waiting for transfers between devices  33.1 us (19%)
  local copies, waits for them, and re-layouts  6.88 us (4%)
  other arithmetic  5.33 us (3%)
    pallas_call x5, Pallas kernels, stage_grads(): pl.pallas_call(functools.partial(grads_kernel, offsets, not carry), out_s...  52.3 us
    ppermute x16, starting transfers between devices, shift(): return lax.ppermute(x, 'row', pairs)  38.2 us
    ppermute x16, waiting for transfers between devices, shift(): return lax.ppermute(x, 'row', pairs)  31.9 us
    ppermute x14, starting transfers between devices, swap(): return lax.ppermute(x, 'row', pairs)  25.6 us
    ppermute x1, starting transfers between devices, body(): lax.ppermute(parts['y_edge', 1], 'row', [(j, i) for i, j in edge])  4.61 us
  transfers between devices with their start and end apart: 32, of which 10 were waited for; matrix products, arithmetic and copies ran while one was open for 4% of the time, Pallas kernels for 29%

profile of v5, /device:TPU:10, one launch (start us, length us, event | category | flops | bytes accessed | tf_op | source)
XLA Modules:
  0.0 171.4 jit_solution(17389645393050558500)
XLA Ops:
  0.6 1.3 copy.12
  3.4 3.5 %collective-permute-start = (bf16[4,528,256]{2,1,0:T(8,128)(2,1)S(1)}, bf16[4,528,256]{2,1,0:T(8,128)(2,1)S(1)}, u32[]{:S(2)}, u32[]{:S(2)}) collective-permute-start(bf16[4,528,256]{2,1,0:T(8,128)(2,1)S(1)} %maximum_maximum_fusion.refs_0_), channel_id=1, source_target_pairs={{0,4},{2,6},{4,8},{6,10},{8,12},{10,14},{1,5},{3,7},{5,9},{7,11},{... | collective-permute-start | bytes 3244040 | tf_op jit(solution)/shard_map/ppermute | solution.py:188
  6.9 2.4 %collective-permute-start.1 = (bf16[4,528,256]{2,1,0:T(8,128)(2,1)S(1)}, bf16[4,528,256]{2,1,0:T(8,128)(2,1)}, u32[]{:S(2)}, u32[]{:S(2)}) collective-permute-start(bf16[4,528,256]{2,1,0:T(8,128)(2,1)S(1)} %maximum_maximum_fusion.refs_0_), channel_id=1, source_target_pairs={{4,0},{6,2},{8,4},{10,6},{12,8},{14,10},{5,1},{7,3},{9,5},{11,7},{... | collective-permute-start | bytes 3244040 | tf_op jit(solution)/shard_map/ppermute | solution.py:188
  9.4 1.6 collective-permute-start.2
  11.7 2.8 %shard_map.112 = (s32[8]{0:T(128)}, s32[256]{0:T(256)}) custom-call(s32[1]{0:T(128)} %bitcast.5.here_ref.row_ref, s32[32]{0:T(128)} %slot_ref.1, s32[256]{0:T(256)} %reshape.45.near_ref, s32[32]{0:T(128)} %live_ref.1), custom_call_target="tpu_custom_call" | custom-call | tf_op jit(solution)/shard_map/pallas_call | solution.py:58
  14.5 7.7 %shard_map.113 = (bf16[4,256,256]{2,1,0:T(8,128)(2,1)}, f32[4,256,256]{2,1,0:T(8,128)}, f32[4,256,256]{2,1,0:T(8,128)}) custom-call(s32[1]{0:T(128)} %bitcast.5.here_ref.row_ref, s32[8]{0:T(128)} %get-tuple-element.37.count_ref, s32[256]{0:T(256)} %get-tuple-element.38.entry_ref, bf16[4,256,256]{2,1,0:T(8,128)(2,1)} %bitcast.35, ...), custom_call_target="tpu_custom_call" | custom-call | flops 3000000000 | bytes 2097152 | tf_op jit(solution)/shard_map/pallas_call | solution.py:154
  22.2 8.7 %collective-permute-done.refs_1_ = bf16[4,528,256]{2,1,0:T(8,128)(2,1)S(1)} collective-permute-done((bf16[4,528,256]{2,1,0:T(8,128)(2,1)S(1)}, bf16[4,528,256]{2,1,0:T(8,128)(2,1)S(1)}, u32[]{:S(2)}, u32[]{:S(2)}) %collective-permute-start) | collective-permute-done | bytes 1081376 | tf_op jit(solution)/shard_map/ppermute | solution.py:188
  30.9 3.3 %collective-permute-done.1.refs_2_ = bf16[4,528,256]{2,1,0:T(8,128)(2,1)} collective-permute-done((bf16[4,528,256]{2,1,0:T(8,128)(2,1)S(1)}, bf16[4,528,256]{2,1,0:T(8,128)(2,1)}, u32[]{:S(2)}, u32[]{:S(2)}) %collective-permute-start.1) | collective-permute-done | bytes 1081376 | tf_op jit(solution)/shard_map/ppermute | solution.py:188
  34.3 4.5 %collective-permute-start.3 = (bf16[4,528,256]{2,1,0:T(8,128)(2,1)S(1)}, bf16[4,528,256]{2,1,0:T(8,128)(2,1)}, u32[]{:S(2)}, u32[]{:S(2)}) collective-permute-start(bf16[4,528,256]{2,1,0:T(8,128)(2,1)S(1)} %collective-permute-done.refs_1_), channel_id=1, source_target_pairs={{4,8},{6,10},{8,12},{10,14},{5,9},{7,11},{9,13},{11,15},{20,24},{2... | collective-permute-start | bytes 3244040 | tf_op jit(solution)/shard_map/ppermute | solution.py:188
  38.7 1.7 collective-permute-start.5
  40.4 1.9 %collective-permute-start.4 = (bf16[4,528,256]{2,1,0:T(8,128)(2,1)}, bf16[4,528,256]{2,1,0:T(8,128)(2,1)}, u32[]{:S(2)}, u32[]{:S(2)}) collective-permute-start(bf16[4,528,256]{2,1,0:T(8,128)(2,1)} %collective-permute-done.1.refs_2_), channel_id=1, source_target_pairs={{4,0},{6,2},{8,4},{10,6},{5,1},{7,3},{9,5},{11,7},{20,16},{22,18},... | collective-permute-start | bytes 3244040 | tf_op jit(solution)/shard_map/ppermute | solution.py:188
  42.3 3.4 %collective-permute-start.6 = (bf16[4,528,256]{2,1,0:T(8,128)(2,1)}, bf16[4,528,256]{2,1,0:T(8,128)(2,1)}, u32[]{:S(2)}, u32[]{:S(2)}) collective-permute-start(bf16[4,528,256]{2,1,0:T(8,128)(2,1)} %collective-permute-done.1.refs_2_), channel_id=1, source_target_pairs={{0,2},{2,0},{4,6},{6,4},{1,3},{3,1},{5,7},{7,5},{16,18},{18,16},{2... | collective-permute-start | bytes 3244040 | tf_op jit(solution)/shard_map/ppermute | solution.py:184
  45.8 1.3 collective-permute-start.7
  49.5 12.1 %shard_map.114 = (bf16[4,256,256]{2,1,0:T(8,128)(2,1)}, bf16[4,256,256]{2,1,0:T(8,128)(2,1)}, bf16[4,256,256]{2,1,0:T(8,128)(2,1)}, f32[4,256,256]{2,1,0:T(8,128)}, f32[4,256,256]{2,1,0:T(8,128)}) custom-call(s32[3]{0:T(128)} %pad_add_fusion.row_ref, s32[8]{0:T(128)} %get-tuple-element.37.count_ref, s32[256]{0:T(256)} %get-tuple-element.38.entry_ref, ...), custom_call_target="tpu_custom_call" | custom-call | flops 8999999488 | bytes 6291456 | tf_op jit(solution)/shard_map/pallas_call | solution.py:154
  61.5 0.7 collective-permute-start.11
  62.3 4.5 %collective-permute-done.4.refs_1_ = bf16[4,528,256]{2,1,0:T(8,128)(2,1)} collective-permute-done((bf16[4,528,256]{2,1,0:T(8,128)(2,1)}, bf16[4,528,256]{2,1,0:T(8,128)(2,1)}, u32[]{:S(2)}, u32[]{:S(2)}) %collective-permute-start.4) | collective-permute-done | bytes 1081376 | tf_op jit(solution)/shard_map/ppermute | solution.py:188
  67.5 2.3 %collective-permute-start.12 = (bf16[4,528,256]{2,1,0:T(8,128)(2,1)}, bf16[4,528,256]{2,1,0:T(8,128)(2,1)S(1)}, u32[]{:S(2)}, u32[]{:S(2)}) collective-permute-start(bf16[4,528,256]{2,1,0:T(8,128)(2,1)} %collective-permute-done.4.refs_1_), channel_id=1, source_target_pairs={{4,0},{6,2},{5,1},{7,3},{20,16},{22,18},{21,17},{23,19}} | collective-permute-start | bytes 3244040 | tf_op jit(solution)/shard_map/ppermute | solution.py:188
  69.8 3.4 %collective-permute-start.14 = (bf16[4,528,256]{2,1,0:T(8,128)(2,1)}, bf16[4,528,256]{2,1,0:T(8,128)(2,1)}, u32[]{:S(2)}, u32[]{:S(2)}) collective-permute-start(bf16[4,528,256]{2,1,0:T(8,128)(2,1)} %collective-permute-done.4.refs_1_), channel_id=1, source_target_pairs={{0,2},{2,0},{4,6},{6,4},{1,3},{3,1},{5,7},{7,5},{16,18},{18,16},{2... | collective-permute-start | bytes 3244040 | tf_op jit(solution)/shard_map/ppermute | solution.py:184
  73.2 16.8 %shard_map.115 = (bf16[4,256,256]{2,1,0:T(8,128)(2,1)}, bf16[4,256,256]{2,1,0:T(8,128)(2,1)}, bf16[4,256,256]{2,1,0:T(8,128)(2,1)}, bf16[4,256,256]{2,1,0:T(8,12...) custom-call(s32[5]{0:T(128)} %stack.65.row_ref, ...), custom_call_target="tpu_custom_call" | custom-call | flops 15000000512 | bytes 10485760 | tf_op jit(solution)/shard_map/pallas_call | solution.py:154
  91.0 1.5 collective-permute-start.16
  92.6 1.5 collective-permute-start.17
  94.1 1.1 collective-permute-done.14.refs_3_
  95.2 1.1 slice.19
  96.3 5.2 %collective-permute-start.18 = (bf16[2,528,256]{2,1,0:T(8,128)(2,1)S(1)}, bf16[2,528,256]{2,1,0:T(8,128)(2,1)S(1)}, u32[]{:S(2)}, u32[]{:S(2)}) collective-permute-start(bf16[2,528,256]{2,1,0:T(8,128)(2,1)S(1)} %slice.19), channel_id=1, source_target_pairs={{4,0},{6,2},{5,1},{7,3},{20,16},{22,18},{21,17},{23,19}} | collective-permute-start | bytes 1622024 | tf_op jit(solution)/shard_map/ppermute | solution.py:188
  101.5 10.2 %shard_map.116 = (bf16[4,256,256]{2,1,0:T(8,128)(2,1)}, bf16[4,256,256]{2,1,0:T(8,128)(2,1)}, bf16[4,256,256]{2,1,0:T(8,128)(2,1)}, bf16[4,256,256]{2,1,0:T(8,12...) custom-call(s32[4]{0:T(128)} %pad_add_fusion.1.row_ref, s32[8]{0:T(128)} %get-tuple-element.37.count_ref, ...), custom_call_target="tpu_custom_call" | custom-call | flops 12000000000 | bytes 8388608 | tf_op jit(solution)/shard_map/pallas_call | solution.py:154
  111.8 0.8 copy-done.22
  112.7 5.6 %shard_map.117 = (bf16[2,256,256]{2,1,0:T(8,128)(2,1)}, bf16[2,256,256]{2,1,0:T(8,128)(2,1)}, bf16[2,256,256]{2,1,0:T(8,128)(2,1)}, bf16[2,256,256]{2,1,0:T(8,12...) custom-call(s32[4]{0:T(128)} %pad_add_fusion.2.row_ref, s32[8]{0:T(128)} %get-tuple-element.37.count_ref, ...), custom_call_target="tpu_custom_call" | custom-call | flops 12000000000 | bytes 8388608 | tf_op jit(solution)/shard_map/pallas_call | solution.py:154
  118.3 0.8 collective-permute-start.19
  119.8 1.3 collective-permute-start.26
  121.9 0.8 collective-permute-start.20
  122.8 0.8 collective-permute-start.22
  123.6 4.6 %collective-permute-done.26 = bf16[2,256,256]{2,1,0:T(8,128)(2,1)S(1)} collective-permute-done((bf16[2,256,256]{2,1,0:T(8,128)(2,1)}, bf16[2,256,256]{2,1,0:T(8,128)(2,1)S(1)}, u32[]{:S(2)}, u32[]{:S(2)}) %collective-permute-start.26) | collective-permute-done | bytes 262176 | tf_op jit(solution)/shard_map/ppermute | solution.py:188
  128.4 4.5 %collective-permute-start.27 = (bf16[4,256,256]{2,1,0:T(8,128)(2,1)S(1)}, bf16[4,256,256]{2,1,0:T(8,128)(2,1)S(1)}, u32[]{:S(2)}, u32[]{:S(2)}) collective-permute-start(bf16[4,256,256]{2,1,0:T(8,128)(2,1)S(1)} %add_convert_fusion.4), channel_id=1, source_target_pairs={{0,2},{2,0},{4,6},{6,4},{1,3},{3,1},{5,7},{7,5},{16,18},{18,16},{2... | collective-permute-start | bytes 1572872 | tf_op jit(solution)/shard_map/ppermute | solution.py:184
  132.9 1.4 collective-permute-start.29
  134.4 4.6 %collective-permute-start.8 = (bf16[4,256,256]{2,1,0:T(8,128)(2,1)S(1)}, bf16[4,256,256]{2,1,0:T(8,128)(2,1)S(1)}, u32[]{:S(2)}, u32[]{:S(2)}) collective-permute-start(bf16[4,256,256]{2,1,0:T(8,128)(2,1)S(1)} %copy-done.26), channel_id=1, source_target_pairs={{4,0},{6,2},{8,12},{10,14},{5,1},{7,3},{9,13},{11,15},{20,16},{22,... | collective-permute-start | bytes 1572872 | tf_op jit(solution)/shard_map/ppermute | solution.py:270
  139.7 3.8 %collective-permute-start.25 = (bf16[4,256,256]{2,1,0:T(8,128)(2,1)S(1)}, bf16[4,256,256]{2,1,0:T(8,128)(2,1)S(1)}, u32[]{:S(2)}, u32[]{:S(2)}) collective-permute-start(bf16[4,256,256]{2,1,0:T(8,128)(2,1)S(1)} %copy-done.24), channel_id=1, source_target_pairs={{0,2},{2,0},{4,6},{6,4},{1,3},{3,1},{5,7},{7,5},{16,18},{18,16},{2... | collective-permute-start | bytes 1572872 | tf_op jit(solution)/shard_map/ppermute | solution.py:184
  143.8 1.4 collective-permute-start.23
  145.5 4.7 %collective-permute-start.30 = (bf16[4,256,256]{2,1,0:T(8,128)(2,1)S(1)}, bf16[4,256,256]{2,1,0:T(8,128)(2,1)S(1)}, u32[]{:S(2)}, u32[]{:S(2)}) collective-permute-start(bf16[4,256,256]{2,1,0:T(8,128)(2,1)S(1)} %add_convert_fusion.2), channel_id=1, source_target_pairs={{0,4},{2,6},{4,8},{6,10},{1,5},{3,7},{5,9},{7,11},{16,20},{18,22},... | collective-permute-start | bytes 1572872 | tf_op jit(solution)/shard_map/ppermute | solution.py:188
  150.3 1.4 collective-permute-start.9
  151.8 3.2 %collective-permute-done.23 = bf16[4,256,256]{2,1,0:T(8,128)(2,1)S(1)} collective-permute-done((bf16[4,256,256]{2,1,0:T(8,128)(2,1)S(1)}, bf16[4,256,256]{2,1,0:T(8,128)(2,1)S(1)}, u32[]{:S(2)}, u32[]{:S(2)}) %collective-permute-start.23) | collective-permute-done | bytes 524320 | tf_op jit(solution)/shard_map/ppermute | solution.py:188
  155.2 2.1 %collective-permute-start.24 = (bf16[4,256,256]{2,1,0:T(8,128)(2,1)S(1)}, bf16[4,256,256]{2,1,0:T(8,128)(2,1)S(1)}, u32[]{:S(2)}, u32[]{:S(2)}) collective-permute-start(bf16[4,256,256]{2,1,0:T(8,128)(2,1)S(1)} %add_convert_fusion.5), channel_id=1, source_target_pairs={{4,0},{6,2},{8,4},{10,6},{12,8},{14,10},{5,1},{7,3},{9,5},{11,7},{... | collective-permute-start | bytes 1572872 | tf_op jit(solution)/shard_map/ppermute | solution.py:188
  157.3 1.1 collective-permute-done.30
  158.6 3.6 %collective-permute-start.31 = (bf16[4,256,256]{2,1,0:T(8,128)(2,1)S(1)}, bf16[4,256,256]{2,1,0:T(8,128)(2,1)S(1)}, u32[]{:S(2)}, u32[]{:S(2)}) collective-permute-start(bf16[4,256,256]{2,1,0:T(8,128)(2,1)S(1)} %add_convert_fusion.1), channel_id=1, source_target_pairs={{0,4},{2,6},{4,8},{6,10},{8,12},{10,14},{1,5},{3,7},{5,9},{7,11},{... | collective-permute-start | bytes 1572872 | tf_op jit(solution)/shard_map/ppermute | solution.py:188
  162.2 0.8 convert_element_type.169
  163.1 0.9 multiply_convert_fusion
  164.0 4.6 %collective-permute-done.24 = bf16[4,256,256]{2,1,0:T(8,128)(2,1)S(1)} collective-permute-done((bf16[4,256,256]{2,1,0:T(8,128)(2,1)S(1)}, bf16[4,256,256]{2,1,0:T(8,128)(2,1)S(1)}, u32[]{:S(2)}, u32[]{:S(2)}) %collective-permute-start.24) | collective-permute-done | bytes 524320 | tf_op jit(solution)/shard_map/ppermute | solution.py:188
  168.6 1.6 collective-permute-done.31
  170.4 1.0 copy.15
  (106 shorter events, 10.1 us)
Async XLA Ops:
  3.2 7.8 %copy-start.20 = (s32[32,8]{0,1:T(8,128)S(1)}, s32[32,8]{0,1:T(8,128)}, u32[]{:S(2)}) copy-start(s32[32,8]{0,1:T(8,128)} %param.16) | copy-start | bytes 3076
  3.4 11.1 %copy-start.1 = (bf16[4,528,256]{2,1,0:T(8,128)(2,1)}, bf16[4,528,256]{2,1,0:T(8,128)(2,1)S(1)}, u32[]{:S(2)}) copy-start(bf16[4,528,256]{2,1,0:T(8,128)(2,1)S(1)} %maximum_maximum_fusion.refs_0_) | copy-start | bytes 3244036
  3.4 27.5 %collective-permute-start = (bf16[4,528,256]{2,1,0:T(8,128)(2,1)S(1)}, bf16[4,528,256]{2,1,0:T(8,128)(2,1)S(1)}, u32[]{:S(2)}, u32[]{:S(2)}) collective-permute-start(bf16[4,528,256]{2,1,0:T(8,128)(2,1)S(1)} %maximum_maximum_fusion.refs_0_), channel_id=1, source_target_pairs={{0,4},{2,6},{4,8},{6,10},{8,12},{10,14},{1,5},{3,7},{5,9},{7,11},{... | collective-permute-start | bytes 3244040 | tf_op jit(solution)/shard_map/ppermute | solution.py:188
  6.9 27.3 %collective-permute-start.1 = (bf16[4,528,256]{2,1,0:T(8,128)(2,1)S(1)}, bf16[4,528,256]{2,1,0:T(8,128)(2,1)}, u32[]{:S(2)}, u32[]{:S(2)}) collective-permute-start(bf16[4,528,256]{2,1,0:T(8,128)(2,1)S(1)} %maximum_maximum_fusion.refs_0_), channel_id=1, source_target_pairs={{4,0},{6,2},{8,4},{10,6},{12,8},{14,10},{5,1},{7,3},{9,5},{11,7},{... | collective-permute-start | bytes 3244040 | tf_op jit(solution)/shard_map/ppermute | solution.py:188
  9.4 36.4 %collective-permute-start.2 = (bf16[4,528,256]{2,1,0:T(8,128)(2,1)S(1)}, bf16[4,528,256]{2,1,0:T(8,128)(2,1)}, u32[]{:S(2)}, u32[]{:S(2)}) collective-permute-start(bf16[4,528,256]{2,1,0:T(8,128)(2,1)S(1)} %maximum_maximum_fusion.refs_0_), channel_id=1, source_target_pairs={{0,2},{2,0},{4,6},{6,4},{8,10},{10,8},{12,14},{14,12},{1,3},{3,1},... | collective-permute-start | bytes 3244040 | tf_op jit(solution)/shard_map/ppermute | solution.py:184
  30.9 18.5 %copy-start.21 = (bf16[4,528,256]{2,1,0:T(8,128)(2,1)}, bf16[4,528,256]{2,1,0:T(8,128)(2,1)S(1)}, u32[]{:S(2)}) copy-start(bf16[4,528,256]{2,1,0:T(8,128)(2,1)S(1)} %collective-permute-done.refs_1_) | copy-start | bytes 3244036
  34.3 27.3 %collective-permute-start.3 = (bf16[4,528,256]{2,1,0:T(8,128)(2,1)S(1)}, bf16[4,528,256]{2,1,0:T(8,128)(2,1)}, u32[]{:S(2)}, u32[]{:S(2)}) collective-permute-start(bf16[4,528,256]{2,1,0:T(8,128)(2,1)S(1)} %collective-permute-done.refs_1_), channel_id=1, source_target_pairs={{4,8},{6,10},{8,12},{10,14},{5,9},{7,11},{9,13},{11,15},{20,24},{2... | collective-permute-start | bytes 3244040 | tf_op jit(solution)/shard_map/ppermute | solution.py:188
  38.7 28.7 %collective-permute-start.5 = (bf16[4,528,256]{2,1,0:T(8,128)(2,1)S(1)}, bf16[4,528,256]{2,1,0:T(8,128)(2,1)}, u32[]{:S(2)}, u32[]{:S(2)}) collective-permute-start(bf16[4,528,256]{2,1,0:T(8,128)(2,1)S(1)} %collective-permute-done.refs_1_), channel_id=1, source_target_pairs={{8,10},{10,8},{12,14},{14,12},{9,11},{11,9},{13,15},{15,13},{24,26... | collective-permute-start | bytes 3244040 | tf_op jit(solution)/shard_map/ppermute | solution.py:184
  40.4 26.3 %collective-permute-start.4 = (bf16[4,528,256]{2,1,0:T(8,128)(2,1)}, bf16[4,528,256]{2,1,0:T(8,128)(2,1)}, u32[]{:S(2)}, u32[]{:S(2)}) collective-permute-start(bf16[4,528,256]{2,1,0:T(8,128)(2,1)} %collective-permute-done.1.refs_2_), channel_id=1, source_target_pairs={{4,0},{6,2},{8,4},{10,6},{5,1},{7,3},{9,5},{11,7},{20,16},{22,18},... | collective-permute-start | bytes 3244040 | tf_op jit(solution)/shard_map/ppermute | solution.py:188
  42.3 27.4 %collective-permute-start.6 = (bf16[4,528,256]{2,1,0:T(8,128)(2,1)}, bf16[4,528,256]{2,1,0:T(8,128)(2,1)}, u32[]{:S(2)}, u32[]{:S(2)}) collective-permute-start(bf16[4,528,256]{2,1,0:T(8,128)(2,1)} %collective-permute-done.1.refs_2_), channel_id=1, source_target_pairs={{0,2},{2,0},{4,6},{6,4},{1,3},{3,1},{5,7},{7,5},{16,18},{18,16},{2... | collective-permute-start | bytes 3244040 | tf_op jit(solution)/shard_map/ppermute | solution.py:184
  45.8 27.4 %collective-permute-start.7 = (bf16[4,528,256]{2,1,0:T(8,128)(2,1)}, bf16[4,528,256]{2,1,0:T(8,128)(2,1)}, u32[]{:S(2)}, u32[]{:S(2)}) collective-permute-start(bf16[4,528,256]{2,1,0:T(8,128)(2,1)} %collective-permute-done.2.refs_0_), channel_id=1, source_target_pairs={{0,4},{2,6},{12,8},{14,10},{1,5},{3,7},{13,9},{15,11},{16,20},{18,... | collective-permute-start | bytes 3244040 | tf_op jit(solution)/shard_map/ppermute | solution.py:225
  61.5 28.5 %collective-permute-start.11 = (bf16[4,528,256]{2,1,0:T(8,128)(2,1)}, bf16[4,528,256]{2,1,0:T(8,128)(2,1)S(1)}, u32[]{:S(2)}, u32[]{:S(2)}) collective-permute-start(bf16[4,528,256]{2,1,0:T(8,128)(2,1)} %collective-permute-done.3.refs_0_), channel_id=1, source_target_pairs={{8,12},{10,14},{9,13},{11,15},{24,28},{26,30},{25,29},{27,31}} | collective-permute-start | bytes 3244040 | tf_op jit(solution)/shard_map/ppermute | solution.py:188
  66.8 25.8 %collective-permute-start.13 = (bf16[4,528,256]{2,1,0:T(8,128)(2,1)}, bf16[4,528,256]{2,1,0:T(8,128)(2,1)S(1)}, u32[]{:S(2)}, u32[]{:S(2)}) collective-permute-start(bf16[4,528,256]{2,1,0:T(8,128)(2,1)} %collective-permute-done.3.refs_0_), channel_id=1, source_target_pairs={{8,10},{10,8},{12,14},{14,12},{9,11},{11,9},{13,15},{15,13},{24,26... | collective-permute-start | bytes 3244040 | tf_op jit(solution)/shard_map/ppermute | solution.py:184
  67.5 23.5 %collective-permute-start.12 = (bf16[4,528,256]{2,1,0:T(8,128)(2,1)}, bf16[4,528,256]{2,1,0:T(8,128)(2,1)S(1)}, u32[]{:S(2)}, u32[]{:S(2)}) collective-permute-start(bf16[4,528,256]{2,1,0:T(8,128)(2,1)} %collective-permute-done.4.refs_1_), channel_id=1, source_target_pairs={{4,0},{6,2},{5,1},{7,3},{20,16},{22,18},{21,17},{23,19}} | collective-permute-start | bytes 3244040 | tf_op jit(solution)/shard_map/ppermute | solution.py:188
  69.8 25.4 %collective-permute-start.14 = (bf16[4,528,256]{2,1,0:T(8,128)(2,1)}, bf16[4,528,256]{2,1,0:T(8,128)(2,1)}, u32[]{:S(2)}, u32[]{:S(2)}) collective-permute-start(bf16[4,528,256]{2,1,0:T(8,128)(2,1)} %collective-permute-done.4.refs_1_), channel_id=1, source_target_pairs={{0,2},{2,0},{4,6},{6,4},{1,3},{3,1},{5,7},{7,5},{16,18},{18,16},{2... | collective-permute-start | bytes 3244040 | tf_op jit(solution)/shard_map/ppermute | solution.py:184
  90.1 21.7 %collective-permute-start.15 = (bf16[2,528,256]{2,1,0:T(8,128)(2,1)S(1)}, bf16[2,528,256]{2,1,0:T(8,128)(2,1)S(1)}, u32[]{:S(2)}, u32[]{:S(2)}) collective-permute-start(bf16[2,528,256]{2,1,0:T(8,128)(2,1)S(1)} %slice.16), channel_id=1, source_target_pairs={{12,14},{14,12},{13,15},{15,13},{28,30},{30,28},{29,31},{31,29}} | collective-permute-start | bytes 1622024 | tf_op jit(solution)/shard_map/ppermute | solution.py:184
  91.0 20.7 %collective-permute-start.16 = (bf16[2,528,256]{2,1,0:T(8,128)(2,1)S(1)}, bf16[2,528,256]{2,1,0:T(8,128)(2,1)}, u32[]{:S(2)}, u32[]{:S(2)}) collective-permute-start(bf16[2,528,256]{2,1,0:T(8,128)(2,1)S(1)} %slice.17), channel_id=1, source_target_pairs={{0,2},{2,0},{1,3},{3,1},{16,18},{18,16},{17,19},{19,17}} | collective-permute-start | bytes 1622024 | tf_op jit(solution)/shard_map/ppermute | solution.py:184
  92.5 9.0 %copy-start.17 = (bf16[4,528,256]{2,1,0:T(8,128)(2,1)}, bf16[4,528,256]{2,1,0:T(8,128)(2,1)S(1)}, u32[]{:S(2)}) copy-start(bf16[4,528,256]{2,1,0:T(8,128)(2,1)S(1)} %collective-permute-done.13.refs_2_) | copy-start | bytes 3244036
  92.6 19.2 %collective-permute-start.17 = (bf16[2,528,256]{2,1,0:T(8,128)(2,1)S(1)}, bf16[2,528,256]{2,1,0:T(8,128)(2,1)}, u32[]{:S(2)}, u32[]{:S(2)}) collective-permute-start(bf16[2,528,256]{2,1,0:T(8,128)(2,1)S(1)} %slice.18), channel_id=1, source_target_pairs={{8,12},{10,14},{9,13},{11,15},{24,28},{26,30},{25,29},{27,31}} | collective-permute-start | bytes 1622024 | tf_op jit(solution)/shard_map/ppermute | solution.py:188
  96.3 15.5 %collective-permute-start.18 = (bf16[2,528,256]{2,1,0:T(8,128)(2,1)S(1)}, bf16[2,528,256]{2,1,0:T(8,128)(2,1)S(1)}, u32[]{:S(2)}, u32[]{:S(2)}) collective-permute-start(bf16[2,528,256]{2,1,0:T(8,128)(2,1)S(1)} %slice.19), channel_id=1, source_target_pairs={{4,0},{6,2},{5,1},{7,3},{20,16},{22,18},{21,17},{23,19}} | collective-permute-start | bytes 1622024 | tf_op jit(solution)/shard_map/ppermute | solution.py:188
  112.7 9.1 %copy-start.11 = (bf16[4,256,256]{2,1,0:T(8,128)(2,1)S(1)}, bf16[4,256,256]{2,1,0:T(8,128)(2,1)}, u32[]{:S(2)}) copy-start(bf16[4,256,256]{2,1,0:T(8,128)(2,1)} %get-tuple-element.56) | copy-start | bytes 1572868
  118.3 3.5 %collective-permute-start.19 = (bf16[2,256,256]{2,1,0:T(8,128)(2,1)}, bf16[2,256,256]{2,1,0:T(8,128)(2,1)S(1)}, u32[]{:S(2)}, u32[]{:S(2)}) collective-permute-start(bf16[2,256,256]{2,1,0:T(8,128)(2,1)} %get-tuple-element.59), channel_id=1, source_target_pairs={{12,8},{14,10},{13,9},{15,11},{28,24},{30,26},{29,25},{31,27}} | collective-permute-start | bytes 786440 | tf_op jit(solution)/shard_map/ppermute | solution.py:188
  119.1 3.6 %collective-permute-start.21 = (bf16[2,256,256]{2,1,0:T(8,128)(2,1)}, bf16[2,256,256]{2,1,0:T(8,128)(2,1)S(1)}, u32[]{:S(2)}, u32[]{:S(2)}) collective-permute-start(bf16[2,256,256]{2,1,0:T(8,128)(2,1)} %get-tuple-element.61), channel_id=1, source_target_pairs={{12,14},{14,12},{13,15},{15,13},{28,30},{30,28},{29,31},{31,29}} | collective-permute-start | bytes 786440 | tf_op jit(solution)/shard_map/ppermute | solution.py:184
  119.8 8.5 %collective-permute-start.26 = (bf16[2,256,256]{2,1,0:T(8,128)(2,1)}, bf16[2,256,256]{2,1,0:T(8,128)(2,1)S(1)}, u32[]{:S(2)}, u32[]{:S(2)}) collective-permute-start(bf16[2,256,256]{2,1,0:T(8,128)(2,1)} %get-tuple-element.66), channel_id=1, source_target_pairs={{0,4},{2,6},{1,5},{3,7},{16,20},{18,22},{17,21},{19,23}} | collective-permute-start | bytes 786440 | tf_op jit(solution)/shard_map/ppermute | solution.py:188
  121.1 11.8 %collective-permute-start.28 = (bf16[2,256,256]{2,1,0:T(8,128)(2,1)}, bf16[2,256,256]{2,1,0:T(8,128)(2,1)S(1)}, u32[]{:S(2)}, u32[]{:S(2)}) collective-permute-start(bf16[2,256,256]{2,1,0:T(8,128)(2,1)} %get-tuple-element.68), channel_id=1, source_target_pairs={{0,2},{2,0},{1,3},{3,1},{16,18},{18,16},{17,19},{19,17}} | collective-permute-start | bytes 786440 | tf_op jit(solution)/shard_map/ppermute | solution.py:184
  121.8 6.5 %copy-start.9 = (bf16[4,256,256]{2,1,0:T(8,128)(2,1)S(1)}, bf16[4,256,256]{2,1,0:T(8,128)(2,1)}, u32[]{:S(2)}) copy-start(bf16[4,256,256]{2,1,0:T(8,128)(2,1)} %get-tuple-element.65) | copy-start | bytes 1572868
  121.9 17.1 %collective-permute-start.20 = (bf16[4,256,256]{2,1,0:T(8,128)(2,1)S(1)}, bf16[4,256,256]{2,1,0:T(8,128)(2,1)S(1)}, u32[]{:S(2)}, u32[]{:S(2)}) collective-permute-start(bf16[4,256,256]{2,1,0:T(8,128)(2,1)S(1)} %add_convert_fusion.8), channel_id=1, source_target_pairs={{8,10},{10,8},{12,14},{14,12},{9,11},{11,9},{13,15},{15,13},{24,26... | collective-permute-start | bytes 1572872 | tf_op jit(solution)/shard_map/ppermute | solution.py:184
  122.7 10.1 %copy-start.8 = (bf16[4,256,256]{2,1,0:T(8,128)(2,1)S(1)}, bf16[4,256,256]{2,1,0:T(8,128)(2,1)}, u32[]{:S(2)}) copy-start(bf16[4,256,256]{2,1,0:T(8,128)(2,1)} %get-tuple-element.67) | copy-start | bytes 1572868
  122.8 16.9 %collective-permute-start.22 = (bf16[4,256,256]{2,1,0:T(8,128)(2,1)S(1)}, bf16[4,256,256]{2,1,0:T(8,128)(2,1)S(1)}, u32[]{:S(2)}, u32[]{:S(2)}) collective-permute-start(bf16[4,256,256]{2,1,0:T(8,128)(2,1)S(1)} %add_convert_fusion.7), channel_id=1, source_target_pairs={{12,8},{14,10},{13,9},{15,11},{28,24},{30,26},{29,25},{31,27}} | collective-permute-start | bytes 1572872 | tf_op jit(solution)/shard_map/ppermute | solution.py:188
  128.3 10.7 %copy-start.25 = (bf16[4,256,256]{2,1,0:T(8,128)(2,1)S(1)}, bf16[4,256,256]{2,1,0:T(8,128)(2,1)}, u32[]{:S(2)}) copy-start(bf16[4,256,256]{2,1,0:T(8,128)(2,1)} %get-tuple-element.52) | copy-start | bytes 1572868
  128.3 11.5 %copy-start.24 = (bf16[4,256,256]{2,1,0:T(8,128)(2,1)S(1)}, bf16[4,256,256]{2,1,0:T(8,128)(2,1)}, u32[]{:S(2)}) copy-start(bf16[4,256,256]{2,1,0:T(8,128)(2,1)} %get-tuple-element.63) | copy-start | bytes 1572868
  128.3 15.3 %copy-start.15 = (bf16[4,256,256]{2,1,0:T(8,128)(2,1)S(1)}, bf16[4,256,256]{2,1,0:T(8,128)(2,1)}, u32[]{:S(2)}) copy-start(bf16[4,256,256]{2,1,0:T(8,128)(2,1)} %get-tuple-element.53) | copy-start | bytes 1572868
  128.4 15.4 %collective-permute-start.27 = (bf16[4,256,256]{2,1,0:T(8,128)(2,1)S(1)}, bf16[4,256,256]{2,1,0:T(8,128)(2,1)S(1)}, u32[]{:S(2)}, u32[]{:S(2)}) collective-permute-start(bf16[4,256,256]{2,1,0:T(8,128)(2,1)S(1)} %add_convert_fusion.4), channel_id=1, source_target_pairs={{0,2},{2,0},{4,6},{6,4},{1,3},{3,1},{5,7},{7,5},{16,18},{18,16},{2... | collective-permute-start | bytes 1572872 | tf_op jit(solution)/shard_map/ppermute | solution.py:184
  132.9 12.3 %copy-start.14 = (bf16[4,256,256]{2,1,0:T(8,128)(2,1)S(1)}, bf16[4,256,256]{2,1,0:T(8,128)(2,1)}, u32[]{:S(2)}) copy-start(bf16[4,256,256]{2,1,0:T(8,128)(2,1)} %get-tuple-element.64) | copy-start | bytes 1572868
  132.9 12.3 %collective-permute-start.29 = (bf16[4,256,256]{2,1,0:T(8,128)(2,1)S(1)}, bf16[4,256,256]{2,1,0:T(8,128)(2,1)S(1)}, u32[]{:S(2)}, u32[]{:S(2)}) collective-permute-start(bf16[4,256,256]{2,1,0:T(8,128)(2,1)S(1)} %add_convert_fusion.3), channel_id=1, source_target_pairs={{0,4},{2,6},{1,5},{3,7},{16,20},{18,22},{17,21},{19,23}} | collective-permute-start | bytes 1572872 | tf_op jit(solution)/shard_map/ppermute | solution.py:188
  134.4 15.8 %collective-permute-start.8 = (bf16[4,256,256]{2,1,0:T(8,128)(2,1)S(1)}, bf16[4,256,256]{2,1,0:T(8,128)(2,1)S(1)}, u32[]{:S(2)}, u32[]{:S(2)}) collective-permute-start(bf16[4,256,256]{2,1,0:T(8,128)(2,1)S(1)} %copy-done.26), channel_id=1, source_target_pairs={{4,0},{6,2},{8,12},{10,14},{5,1},{7,3},{9,13},{11,15},{20,16},{22,... | collective-permute-start | bytes 1572872 | tf_op jit(solution)/shard_map/ppermute | solution.py:270
  139.0 12.7 %collective-permute-start.10 = (bf16[4,256,256]{2,1,0:T(8,128)(2,1)S(1)}, bf16[4,256,256]{2,1,0:T(8,128)(2,1)S(1)}, u32[]{:S(2)}, u32[]{:S(2)}) collective-permute-start(bf16[4,256,256]{2,1,0:T(8,128)(2,1)S(1)} %copy-done.25), channel_id=1, source_target_pairs={{8,10},{10,8},{12,14},{14,12},{9,11},{11,9},{13,15},{15,13},{24,26... | collective-permute-start | bytes 1572872 | tf_op jit(solution)/shard_map/ppermute | solution.py:184
  139.7 17.5 %collective-permute-start.25 = (bf16[4,256,256]{2,1,0:T(8,128)(2,1)S(1)}, bf16[4,256,256]{2,1,0:T(8,128)(2,1)S(1)}, u32[]{:S(2)}, u32[]{:S(2)}) collective-permute-start(bf16[4,256,256]{2,1,0:T(8,128)(2,1)S(1)} %copy-done.24), channel_id=1, source_target_pairs={{0,2},{2,0},{4,6},{6,4},{1,3},{3,1},{5,7},{7,5},{16,18},{18,16},{2... | collective-permute-start | bytes 1572872 | tf_op jit(solution)/shard_map/ppermute | solution.py:184
  143.8 6.4 %copy-start.6 = (bf16[4,256,256]{2,1,0:T(8,128)(2,1)S(1)}, bf16[4,256,256]{2,1,0:T(8,128)(2,1)}, u32[]{:S(2)}) copy-start(bf16[4,256,256]{2,1,0:T(8,128)(2,1)} %get-tuple-element.47) | copy-start | bytes 1572868
  143.8 11.2 %collective-permute-start.23 = (bf16[4,256,256]{2,1,0:T(8,128)(2,1)S(1)}, bf16[4,256,256]{2,1,0:T(8,128)(2,1)S(1)}, u32[]{:S(2)}, u32[]{:S(2)}) collective-permute-start(bf16[4,256,256]{2,1,0:T(8,128)(2,1)S(1)} %add_convert_fusion.6), channel_id=1, source_target_pairs={{8,4},{10,6},{12,8},{14,10},{9,5},{11,7},{13,9},{15,11},{24,20},{2... | collective-permute-start | bytes 1572872 | tf_op jit(solution)/shard_map/ppermute | solution.py:188
  145.4 9.5 %copy-start.13 = (bf16[4,256,256]{2,1,0:T(8,128)(2,1)S(1)}, bf16[4,256,256]{2,1,0:T(8,128)(2,1)}, u32[]{:S(2)}) copy-start(bf16[4,256,256]{2,1,0:T(8,128)(2,1)} %get-tuple-element.51) | copy-start | bytes 1572868
  145.5 13.0 %collective-permute-start.30 = (bf16[4,256,256]{2,1,0:T(8,128)(2,1)S(1)}, bf16[4,256,256]{2,1,0:T(8,128)(2,1)S(1)}, u32[]{:S(2)}, u32[]{:S(2)}) collective-permute-start(bf16[4,256,256]{2,1,0:T(8,128)(2,1)S(1)} %add_convert_fusion.2), channel_id=1, source_target_pairs={{0,4},{2,6},{4,8},{6,10},{1,5},{3,7},{5,9},{7,11},{16,20},{18,22},... | collective-permute-start | bytes 1572872 | tf_op jit(solution)/shard_map/ppermute | solution.py:188
  150.3 8.1 %copy-start.12 = (bf16[4,256,256]{2,1,0:T(8,128)(2,1)S(1)}, bf16[4,256,256]{2,1,0:T(8,128)(2,1)}, u32[]{:S(2)}) copy-start(bf16[4,256,256]{2,1,0:T(8,128)(2,1)} %get-tuple-element.62) | copy-start | bytes 1572868
  150.3 13.7 %collective-permute-start.9 = (bf16[4,256,256]{2,1,0:T(8,128)(2,1)S(1)}, bf16[4,256,256]{2,1,0:T(8,128)(2,1)S(1)}, u32[]{:S(2)}, u32[]{:S(2)}) collective-permute-start(bf16[4,256,256]{2,1,0:T(8,128)(2,1)S(1)} %add_convert_fusion.9), channel_id=1, source_target_pairs={{0,2},{2,0},{4,6},{6,4},{8,10},{10,8},{12,14},{14,12},{1,3},{3,1},... | collective-permute-start | bytes 1572872 | tf_op jit(solution)/shard_map/ppermute | solution.py:184
  155.2 7.0 %copy-start.3 = (f32[4,256,256]{2,1,0:T(8,128)S(1)}, f32[4,256,256]{2,1,0:T(8,128)}, u32[]{:S(2)}) copy-start(f32[4,256,256]{2,1,0:T(8,128)} %get-tuple-element.70) | copy-start | bytes 3145732
  155.2 13.4 %collective-permute-start.24 = (bf16[4,256,256]{2,1,0:T(8,128)(2,1)S(1)}, bf16[4,256,256]{2,1,0:T(8,128)(2,1)S(1)}, u32[]{:S(2)}, u32[]{:S(2)}) collective-permute-start(bf16[4,256,256]{2,1,0:T(8,128)(2,1)S(1)} %add_convert_fusion.5), channel_id=1, source_target_pairs={{4,0},{6,2},{8,4},{10,6},{12,8},{14,10},{5,1},{7,3},{9,5},{11,7},{... | collective-permute-start | bytes 1572872 | tf_op jit(solution)/shard_map/ppermute | solution.py:188
  158.6 11.6 %collective-permute-start.31 = (bf16[4,256,256]{2,1,0:T(8,128)(2,1)S(1)}, bf16[4,256,256]{2,1,0:T(8,128)(2,1)S(1)}, u32[]{:S(2)}, u32[]{:S(2)}) collective-permute-start(bf16[4,256,256]{2,1,0:T(8,128)(2,1)S(1)} %add_convert_fusion.1), channel_id=1, source_target_pairs={{0,4},{2,6},{4,8},{6,10},{8,12},{10,14},{1,5},{3,7},{5,9},{7,11},{... | collective-permute-start | bytes 1572872 | tf_op jit(solution)/shard_map/ppermute | solution.py:188
  163.1 7.1 %copy-start.5 = (bf16[4,256,256]{2,1,0:T(8,128)(2,1)S(1)}, bf16[4,256,256]{2,1,0:T(8,128)(2,1)}, u32[]{:S(2)}) copy-start(bf16[4,256,256]{2,1,0:T(8,128)(2,1)} %get-tuple-element.42) | copy-start | bytes 1572868
  (11 other events, 28.9 us)

commit v6 on v5

--- a/solution.py
+++ b/solution.py
@@ -162,7 +162,7 @@
             pltpu.VMEM((pairs, per_row, 2 * BLOCK, PAIR), jnp.bfloat16),
             pltpu.VMEM((pairs, per_row, PAIR, 2 * BLOCK), jnp.bfloat16),
         ],
-        compiler_params=pltpu.CompilerParams(vmem_limit_bytes=58 * 2**20),
+        compiler_params=pltpu.CompilerParams(vmem_limit_bytes=40 * 2**20),
         cost_estimate=pl.CostEstimate(
             flops=n_load * 3000000000, bytes_accessed=n_load * 2**21, transcendentals=0
         ),
@@ -217,7 +217,7 @@
         ups = shift(ups, 1, k - 1, last)
         downs = shift(downs, -1, 1, n_z - k + 1)
         if k == 1:
-            ups, downs, carry, own_part = lax.optimization_barrier((ups, downs, carry, own_part))
+            ups, carry, own_part = lax.optimization_barrier((ups, carry, own_part))
         have[("up", k)], have[("down", k)] = ups, downs
         if k == 1:
             have[("y_up", 1)] = swap(ups, 2, n_z)

time: 174 us -> 165 us (0.948)
  Pallas kernels: 55.1 us -> 38.4 us
  waiting for transfers between devices: 33.1 us -> 47.1 us
  starting transfers between devices: 69.6 us -> 60.5 us
  local copies, waits for them, and re-layouts: 6.88 us -> 12.1 us
    pallas_call x5, Pallas kernels: 52.3 us -> 35.6 us  [stage_grads(): pl.pallas_call(functools.partial(grads_kernel, offsets, not carry), out_s...]
    ppermute x16, waiting for transfers between devices: 31.9 us -> 42.2 us  [shift(): return lax.ppermute(x, 'row', pairs)]
    unnamed x57 -> x35, local copies, waits for them, and re-layouts: 3.29 us -> 10.2 us
    ppermute x14, starting transfers between devices: 25.6 us -> 19.4 us  [swap(): return lax.ppermute(x, 'row', pairs)]
    ppermute x16, starting transfers between devices: 38.2 us -> 33 us  [shift(): return lax.ppermute(x, 'row', pairs)]
    ppermute x14, waiting for transfers between devices: 1.13 us -> 4.88 us  [swap(): return lax.ppermute(x, 'row', pairs)]
    ppermute x1, starting transfers between devices: 4.61 us -> 6.78 us  [body(): lax.ppermute(parts['y_edge', 1], 'row', [(j, i) for i, j in edge])]
  transfers between devices with their start and end apart: 32 -> 32, of which waited for: 10 -> 13; matrix products, arithmetic and copies ran while one was open for 4% -> 3% of each run, Pallas kernels for 29% -> 22%
where the time goes in v6:
time: 165 us; the launch traced here: 163 us
  starting transfers between devices  60.5 us (37%)
  waiting for transfers between devices  47.1 us (29%)
  Pallas kernels  38.4 us (23%)
  local copies, waits for them, and re-layouts  12.1 us (7%)
  other arithmetic  3.96 us (2%)
    ppermute x16, waiting for transfers between devices, shift(): return lax.ppermute(x, 'row', pairs)  42.2 us
    pallas_call x5, Pallas kernels, stage_grads(): pl.pallas_call(functools.partial(grads_kernel, offsets, not carry), out_s...  35.6 us
    ppermute x16, starting transfers between devices, shift(): return lax.ppermute(x, 'row', pairs)  33 us
    ppermute x14, starting transfers between devices, swap(): return lax.ppermute(x, 'row', pairs)  19.4 us
    unnamed x35, local copies, waits for them, and re-layouts  10.2 us
    ppermute x1, starting transfers between devices, body(): lax.ppermute(parts['y_edge', 1], 'row', [(j, i) for i, j in edge])  6.78 us
    ppermute x14, waiting for transfers between devices, swap(): return lax.ppermute(x, 'row', pairs)  4.88 us
  transfers between devices with their start and end apart: 32, of which 13 were waited for; matrix products, arithmetic and copies ran while one was open for 3% of the time, Pallas kernels for 22%

profile of v6, /device:TPU:10, one launch (start us, length us, event | category | flops | bytes accessed | tf_op | source)
XLA Modules:
  0.0 163.4 jit_solution(13241537313030134041)
XLA Ops:
  0.6 1.3 copy.12
  3.4 3.5 %collective-permute-start = (bf16[4,528,256]{2,1,0:T(8,128)(2,1)S(1)}, bf16[4,528,256]{2,1,0:T(8,128)(2,1)}, u32[]{:S(2)}, u32[]{:S(2)}) collective-permute-start(bf16[4,528,256]{2,1,0:T(8,128)(2,1)S(1)} %maximum_maximum_fusion.refs_0_), channel_id=1, source_target_pairs={{0,4},{2,6},{4,8},{6,10},{8,12},{10,14},{1,5},{3,7},{5,9},{7,11},{... | collective-permute-start | bytes 3244040 | tf_op jit(solution)/shard_map/ppermute | solution.py:188
  6.9 3.3 %collective-permute-start.2 = (bf16[4,528,256]{2,1,0:T(8,128)(2,1)S(1)}, bf16[4,528,256]{2,1,0:T(8,128)(2,1)}, u32[]{:S(2)}, u32[]{:S(2)}) collective-permute-start(bf16[4,528,256]{2,1,0:T(8,128)(2,1)S(1)} %maximum_maximum_fusion.refs_0_), channel_id=1, source_target_pairs={{4,0},{6,2},{8,4},{10,6},{12,8},{14,10},{5,1},{7,3},{9,5},{11,7},{... | collective-permute-start | bytes 3244040 | tf_op jit(solution)/shard_map/ppermute | solution.py:188
  10.3 1.6 collective-permute-start.1
  12.6 2.8 %shard_map.112 = (s32[8]{0:T(128)}, s32[256]{0:T(256)}) custom-call(s32[1]{0:T(128)} %bitcast.5.here_ref.row_ref, s32[32]{0:T(128)} %slot_ref.1, s32[256]{0:T(256)} %reshape.45.near_ref, s32[32]{0:T(128)} %live_ref.1), custom_call_target="tpu_custom_call" | custom-call | tf_op jit(solution)/shard_map/pallas_call | solution.py:58
  15.5 1.0 copy-done.1
  17.8 5.3 %shard_map.113 = (bf16[4,256,256]{2,1,0:T(8,128)(2,1)S(1)}, f32[4,256,256]{2,1,0:T(8,128)S(1)}, f32[4,256,256]{2,1,0:T(8,128)S(1)}) custom-call(s32[1]{0:T(128)} %bitcast.5.here_ref.row_ref, s32[8]{0:T(128)S(1)} %copy-done.5, s32[256]{0:T(256)S(1)} %copy-done.3, bf16[4,256,256]{2,1,0:T(8,128)(2,1)S(1)} %bitcast.29, bf16[4,256,256]{2,1,0:T(8,128)(2,1)S(1)} %bitcast.34, ...), custom_call_target="tpu_custom_call" | custom-call | flops 3000000000 | bytes 2097152 | tf_op jit(solution)/shard_map/pallas_call | solution.py:154
  23.1 1.0 copy-done.7
  24.2 1.0 copy-done.9
  25.1 5.9 %collective-permute-done.refs_1_ = bf16[4,528,256]{2,1,0:T(8,128)(2,1)} collective-permute-done((bf16[4,528,256]{2,1,0:T(8,128)(2,1)S(1)}, bf16[4,528,256]{2,1,0:T(8,128)(2,1)}, u32[]{:S(2)}, u32[]{:S(2)}) %collective-permute-start) | collective-permute-done | bytes 1081376 | tf_op jit(solution)/shard_map/ppermute | solution.py:188
  31.0 4.5 %collective-permute-start.3 = (bf16[4,528,256]{2,1,0:T(8,128)(2,1)}, bf16[4,528,256]{2,1,0:T(8,128)(2,1)}, u32[]{:S(2)}, u32[]{:S(2)}) collective-permute-start(bf16[4,528,256]{2,1,0:T(8,128)(2,1)} %collective-permute-done.refs_1_), channel_id=1, source_target_pairs={{4,8},{6,10},{8,12},{10,14},{5,9},{7,11},{9,13},{11,15},{20,24},{2... | collective-permute-start | bytes 3244040 | tf_op jit(solution)/shard_map/ppermute | solution.py:188
  35.5 1.7 %collective-permute-start.5 = (bf16[4,528,256]{2,1,0:T(8,128)(2,1)}, bf16[4,528,256]{2,1,0:T(8,128)(2,1)}, u32[]{:S(2)}, u32[]{:S(2)}) collective-permute-start(bf16[4,528,256]{2,1,0:T(8,128)(2,1)} %collective-permute-done.refs_1_), channel_id=1, source_target_pairs={{8,10},{10,8},{12,14},{14,12},{9,11},{11,9},{13,15},{15,13},{24,26... | collective-permute-start | bytes 3244040 | tf_op jit(solution)/shard_map/ppermute | solution.py:184
  37.2 1.9 %collective-permute-start.4 = (bf16[4,528,256]{2,1,0:T(8,128)(2,1)}, bf16[4,528,256]{2,1,0:T(8,128)(2,1)}, u32[]{:S(2)}, u32[]{:S(2)}) collective-permute-start(bf16[4,528,256]{2,1,0:T(8,128)(2,1)} %collective-permute-done.2.refs_2_), channel_id=1, source_target_pairs={{4,0},{6,2},{8,4},{10,6},{5,1},{7,3},{9,5},{11,7},{20,16},{22,18},... | collective-permute-start | bytes 3244040 | tf_op jit(solution)/shard_map/ppermute | solution.py:188
  39.1 3.4 %collective-permute-start.6 = (bf16[4,528,256]{2,1,0:T(8,128)(2,1)}, bf16[4,528,256]{2,1,0:T(8,128)(2,1)}, u32[]{:S(2)}, u32[]{:S(2)}) collective-permute-start(bf16[4,528,256]{2,1,0:T(8,128)(2,1)} %collective-permute-done.2.refs_2_), channel_id=1, source_target_pairs={{0,2},{2,0},{4,6},{6,4},{1,3},{3,1},{5,7},{7,5},{16,18},{18,16},{2... | collective-permute-start | bytes 3244040 | tf_op jit(solution)/shard_map/ppermute | solution.py:184
  42.5 1.3 collective-permute-start.7
  44.2 1.0 copy-done.2
  45.3 1.2 copy-done.8
  46.5 1.2 copy-done.10
  47.7 9.0 %shard_map.114 = (bf16[4,256,256]{2,1,0:T(8,128)(2,1)S(1)}, bf16[4,256,256]{2,1,0:T(8,128)(2,1)S(1)}, bf16[4,256,256]{2,1,0:T(8,128)(2,1)S(1)}, f32[4,256,256]{2,1,0:T(8,128)S(1)}, f32[4,256,256]{2,1,0:T(8,128)S(1)}) custom-call(s32[3]{0:T(128)S(1)} %pad_add_fusion.row_ref, s32[8]{0:T(128)S(1)} %copy-done.6, s32[256]{0:T(256)S(1)} %copy-done.4, ...), custom_call_target="tpu_custom_call" | custom-call | flops 8999999488 | bytes 6291456 | tf_op jit(solution)/shard_map/pallas_call | solution.py:154
  58.5 5.3 %collective-permute-done.4.refs_1_ = bf16[4,528,256]{2,1,0:T(8,128)(2,1)} collective-permute-done((bf16[4,528,256]{2,1,0:T(8,128)(2,1)}, bf16[4,528,256]{2,1,0:T(8,128)(2,1)}, u32[]{:S(2)}, u32[]{:S(2)}) %collective-permute-start.4) | collective-permute-done | bytes 1081376 | tf_op jit(solution)/shard_map/ppermute | solution.py:188
  63.8 2.3 %collective-permute-start.12 = (bf16[4,528,256]{2,1,0:T(8,128)(2,1)}, bf16[4,528,256]{2,1,0:T(8,128)(2,1)S(1)}, u32[]{:S(2)}, u32[]{:S(2)}) collective-permute-start(bf16[4,528,256]{2,1,0:T(8,128)(2,1)} %collective-permute-done.4.refs_1_), channel_id=1, source_target_pairs={{4,0},{6,2},{5,1},{7,3},{20,16},{22,18},{21,17},{23,19}} | collective-permute-start | bytes 3244040 | tf_op jit(solution)/shard_map/ppermute | solution.py:188
  66.1 3.4 %collective-permute-start.14 = (bf16[4,528,256]{2,1,0:T(8,128)(2,1)}, bf16[4,528,256]{2,1,0:T(8,128)(2,1)S(1)}, u32[]{:S(2)}, u32[]{:S(2)}) collective-permute-start(bf16[4,528,256]{2,1,0:T(8,128)(2,1)} %collective-permute-done.4.refs_1_), channel_id=1, source_target_pairs={{0,2},{2,0},{4,6},{6,4},{1,3},{3,1},{5,7},{7,5},{16,18},{18,16},{2... | collective-permute-start | bytes 3244040 | tf_op jit(solution)/shard_map/ppermute | solution.py:184
  69.5 13.8 %shard_map.115 = (bf16[4,256,256]{2,1,0:T(8,128)(2,1)S(1)}, bf16[4,256,256]{2,1,0:T(8,128)(2,1)S(1)}, bf16[4,256,256]{2,1,0:T(8,128)(2,1)S(1)}, bf16[4,256,256]{...) custom-call(s32[5]{0:T(128)S(1)} %stack.65.row_ref, ...), custom_call_target="tpu_custom_call" | custom-call | flops 15000000512 | bytes 10485760 | tf_op jit(solution)/shard_map/pallas_call | solution.py:154
  84.9 2.8 %collective-permute-done.12.refs_1_ = bf16[4,528,256]{2,1,0:T(8,128)(2,1)S(1)} collective-permute-done((bf16[4,528,256]{2,1,0:T(8,128)(2,1)}, bf16[4,528,256]{2,1,0:T(8,128)(2,1)S(1)}, u32[]{:S(2)}, u32[]{:S(2)}) %collective-permute-start.12) | collective-permute-done | bytes 1081376 | tf_op jit(solution)/shard_map/ppermute | solution.py:188
  88.4 3.3 %collective-permute-done.14.refs_3_ = bf16[4,528,256]{2,1,0:T(8,128)(2,1)S(1)} collective-permute-done((bf16[4,528,256]{2,1,0:T(8,128)(2,1)}, bf16[4,528,256]{2,1,0:T(8,128)(2,1)S(1)}, u32[]{:S(2)}, u32[]{:S(2)}) %collective-permute-start.14) | collective-permute-done | bytes 1081376 | tf_op jit(solution)/shard_map/ppermute | solution.py:184
  91.8 3.7 %collective-permute-start.18 = (bf16[2,528,256]{2,1,0:T(8,128)(2,1)S(1)}, bf16[2,528,256]{2,1,0:T(8,128)(2,1)S(1)}, u32[]{:S(2)}, u32[]{:S(2)}) collective-permute-start(bf16[2,528,256]{2,1,0:T(8,128)(2,1)S(1)} %slice.19), channel_id=1, source_target_pairs={{4,0},{6,2},{5,1},{7,3},{20,16},{22,18},{21,17},{23,19}} | collective-permute-start | bytes 1622024 | tf_op jit(solution)/shard_map/ppermute | solution.py:188
  95.5 5.6 %shard_map.116 = (bf16[4,256,256]{2,1,0:T(8,128)(2,1)S(1)}, bf16[4,256,256]{2,1,0:T(8,128)(2,1)S(1)}, bf16[4,256,256]{2,1,0:T(8,128)(2,1)S(1)}, bf16[4,256,256]{...) custom-call(s32[4]{0:T(128)S(1)} %pad_add_fusion.1.row_ref, s32[8]{0:T(128)S(1)} %copy-done.6, ...), custom_call_target="tpu_custom_call" | custom-call | flops 12000000000 | bytes 8388608 | tf_op jit(solution)/shard_map/pallas_call | solution.py:154
  101.1 2.9 %collective-permute-done.18.refs_3_ = bf16[2,528,256]{2,1,0:T(8,128)(2,1)S(1)} collective-permute-done((bf16[2,528,256]{2,1,0:T(8,128)(2,1)S(1)}, bf16[2,528,256]{2,1,0:T(8,128)(2,1)S(1)}, u32[]{:S(2)}, u32[]{:S(2)}) %collective-permute-start.18) | collective-permute-done | bytes 540704 | tf_op jit(solution)/shard_map/ppermute | solution.py:188
  104.0 1.9 %shard_map.117 = (bf16[2,256,256]{2,1,0:T(8,128)(2,1)S(1)}, bf16[2,256,256]{2,1,0:T(8,128)(2,1)S(1)}, bf16[2,256,256]{2,1,0:T(8,128)(2,1)S(1)}, bf16[2,256,256]{...) custom-call(s32[4]{0:T(128)S(1)} %pad_add_fusion.2.row_ref, s32[8]{0:T(128)S(1)} %copy-done.6, ...), custom_call_target="tpu_custom_call" | custom-call | flops 12000000000 | bytes 8388608 | tf_op jit(solution)/shard_map/pallas_call | solution.py:154
  107.3 1.3 collective-permute-start.26
  110.8 8.1 %collective-permute-done.26 = bf16[2,256,256]{2,1,0:T(8,128)(2,1)S(1)} collective-permute-done((bf16[2,256,256]{2,1,0:T(8,128)(2,1)S(1)}, bf16[2,256,256]{2,1,0:T(8,128)(2,1)S(1)}, u32[]{:S(2)}, u32[]{:S(2)}) %collective-permute-start.26) | collective-permute-done | bytes 262176 | tf_op jit(solution)/shard_map/ppermute | solution.py:188
  119.0 1.9 %collective-permute-start.27 = (bf16[4,256,256]{2,1,0:T(8,128)(2,1)S(1)}, bf16[4,256,256]{2,1,0:T(8,128)(2,1)S(1)}, u32[]{:S(2)}, u32[]{:S(2)}) collective-permute-start(bf16[4,256,256]{2,1,0:T(8,128)(2,1)S(1)} %add_convert_fusion.4), channel_id=1, source_target_pairs={{0,2},{2,0},{4,6},{6,4},{1,3},{3,1},{5,7},{7,5},{16,18},{18,16},{2... | collective-permute-start | bytes 1572872 | tf_op jit(solution)/shard_map/ppermute | solution.py:184
  121.0 1.3 collective-permute-start.29
  122.3 6.8 %collective-permute-start.8 = (bf16[4,256,256]{2,1,0:T(8,128)(2,1)S(1)}, bf16[4,256,256]{2,1,0:T(8,128)(2,1)S(1)}, u32[]{:S(2)}, u32[]{:S(2)}) collective-permute-start(bf16[4,256,256]{2,1,0:T(8,128)(2,1)S(1)} %get-tuple-element.48), channel_id=1, source_target_pairs={{4,0},{6,2},{8,12},{10,14},{5,1},{7,3},{9,13},{11,15},{20,16},{22,... | collective-permute-start | bytes 1572872 | tf_op jit(solution)/shard_map/ppermute | solution.py:270
  129.9 1.9 %collective-permute-start.25 = (bf16[4,256,256]{2,1,0:T(8,128)(2,1)S(1)}, bf16[4,256,256]{2,1,0:T(8,128)(2,1)S(1)}, u32[]{:S(2)}, u32[]{:S(2)}) collective-permute-start(bf16[4,256,256]{2,1,0:T(8,128)(2,1)S(1)} %get-tuple-element.61), channel_id=1, source_target_pairs={{0,2},{2,0},{4,6},{6,4},{1,3},{3,1},{5,7},{7,5},{16,18},{18,16},{2... | collective-permute-start | bytes 1572872 | tf_op jit(solution)/shard_map/ppermute | solution.py:184
  132.0 1.5 collective-permute-done.27
  133.5 1.3 collective-permute-start.23
  134.8 1.7 %collective-permute-done.29 = bf16[4,256,256]{2,1,0:T(8,128)(2,1)S(1)} collective-permute-done((bf16[4,256,256]{2,1,0:T(8,128)(2,1)S(1)}, bf16[4,256,256]{2,1,0:T(8,128)(2,1)S(1)}, u32[]{:S(2)}, u32[]{:S(2)}) %collective-permute-start.29) | collective-permute-done | bytes 524320 | tf_op jit(solution)/shard_map/ppermute | solution.py:188
  136.7 2.8 %collective-permute-start.30 = (bf16[4,256,256]{2,1,0:T(8,128)(2,1)S(1)}, bf16[4,256,256]{2,1,0:T(8,128)(2,1)S(1)}, u32[]{:S(2)}, u32[]{:S(2)}) collective-permute-start(bf16[4,256,256]{2,1,0:T(8,128)(2,1)S(1)} %add_convert_fusion.2), channel_id=1, source_target_pairs={{0,4},{2,6},{4,8},{6,10},{1,5},{3,7},{5,9},{7,11},{16,20},{18,22},... | collective-permute-start | bytes 1572872 | tf_op jit(solution)/shard_map/ppermute | solution.py:188
  140.3 6.5 %collective-permute-done.23 = bf16[4,256,256]{2,1,0:T(8,128)(2,1)S(1)} collective-permute-done((bf16[4,256,256]{2,1,0:T(8,128)(2,1)S(1)}, bf16[4,256,256]{2,1,0:T(8,128)(2,1)S(1)}, u32[]{:S(2)}, u32[]{:S(2)}) %collective-permute-start.23) | collective-permute-done | bytes 524320 | tf_op jit(solution)/shard_map/ppermute | solution.py:188
  147.1 1.9 %collective-permute-start.24 = (bf16[4,256,256]{2,1,0:T(8,128)(2,1)S(1)}, bf16[4,256,256]{2,1,0:T(8,128)(2,1)S(1)}, u32[]{:S(2)}, u32[]{:S(2)}) collective-permute-start(bf16[4,256,256]{2,1,0:T(8,128)(2,1)S(1)} %add_convert_fusion.5), channel_id=1, source_target_pairs={{4,0},{6,2},{8,4},{10,6},{12,8},{14,10},{5,1},{7,3},{9,5},{11,7},{... | collective-permute-start | bytes 1572872 | tf_op jit(solution)/shard_map/ppermute | solution.py:188
  149.0 1.8 %collective-permute-done.30 = bf16[4,256,256]{2,1,0:T(8,128)(2,1)S(1)} collective-permute-done((bf16[4,256,256]{2,1,0:T(8,128)(2,1)S(1)}, bf16[4,256,256]{2,1,0:T(8,128)(2,1)S(1)}, u32[]{:S(2)}, u32[]{:S(2)}) %collective-permute-start.30) | collective-permute-done | bytes 524320 | tf_op jit(solution)/shard_map/ppermute | solution.py:188
  151.0 2.4 %collective-permute-start.31 = (bf16[4,256,256]{2,1,0:T(8,128)(2,1)S(1)}, bf16[4,256,256]{2,1,0:T(8,128)(2,1)S(1)}, u32[]{:S(2)}, u32[]{:S(2)}) collective-permute-start(bf16[4,256,256]{2,1,0:T(8,128)(2,1)S(1)} %add_convert_fusion.1), channel_id=1, source_target_pairs={{0,4},{2,6},{4,8},{6,10},{8,12},{10,14},{1,5},{3,7},{5,9},{7,11},{... | collective-permute-start | bytes 1572872 | tf_op jit(solution)/shard_map/ppermute | solution.py:188
  153.4 0.8 convert_element_type.169
  154.3 0.9 multiply_convert_fusion
  155.2 3.0 %collective-permute-done.24 = bf16[4,256,256]{2,1,0:T(8,128)(2,1)S(1)} collective-permute-done((bf16[4,256,256]{2,1,0:T(8,128)(2,1)S(1)}, bf16[4,256,256]{2,1,0:T(8,128)(2,1)S(1)}, u32[]{:S(2)}, u32[]{:S(2)}) %collective-permute-start.24) | collective-permute-done | bytes 524320 | tf_op jit(solution)/shard_map/ppermute | solution.py:188
  158.2 3.9 %collective-permute-done.31 = bf16[4,256,256]{2,1,0:T(8,128)(2,1)S(1)} collective-permute-done((bf16[4,256,256]{2,1,0:T(8,128)(2,1)S(1)}, bf16[4,256,256]{2,1,0:T(8,128)(2,1)S(1)}, u32[]{:S(2)}, u32[]{:S(2)}) %collective-permute-start.31) | collective-permute-done | bytes 524320 | tf_op jit(solution)/shard_map/ppermute | solution.py:188
  162.4 1.0 copy.15
  (84 shorter events, 14.1 us)
Async XLA Ops:
  0.6 1.3 copy-start.13
  2.0 0.7 copy-start.14
  2.0 1.0 copy-start.11
  2.0 1.2 copy-start.12
  3.2 8.7 %copy-start.15 = (s32[32,8]{0,1:T(8,128)S(1)}, s32[32,8]{0,1:T(8,128)}, u32[]{:S(2)}) copy-start(s32[32,8]{0,1:T(8,128)} %param.16) | copy-start | bytes 3076
  3.2 12.3 %copy-start = (bf16[1024,256]{1,0:T(8,128)(2,1)S(1)}, bf16[1024,256]{1,0:T(8,128)(2,1)}, u32[]{:S(2)}) copy-start(bf16[1024,256]{1,0:T(8,128)(2,1)} %param.10) | copy-start | bytes 1572868
  3.4 27.6 %collective-permute-start = (bf16[4,528,256]{2,1,0:T(8,128)(2,1)S(1)}, bf16[4,528,256]{2,1,0:T(8,128)(2,1)}, u32[]{:S(2)}, u32[]{:S(2)}) collective-permute-start(bf16[4,528,256]{2,1,0:T(8,128)(2,1)S(1)} %maximum_maximum_fusion.refs_0_), channel_id=1, source_target_pairs={{0,4},{2,6},{4,8},{6,10},{8,12},{10,14},{1,5},{3,7},{5,9},{7,11},{... | collective-permute-start | bytes 3244040 | tf_op jit(solution)/shard_map/ppermute | solution.py:188
  6.9 30.3 %collective-permute-start.2 = (bf16[4,528,256]{2,1,0:T(8,128)(2,1)S(1)}, bf16[4,528,256]{2,1,0:T(8,128)(2,1)}, u32[]{:S(2)}, u32[]{:S(2)}) collective-permute-start(bf16[4,528,256]{2,1,0:T(8,128)(2,1)S(1)} %maximum_maximum_fusion.refs_0_), channel_id=1, source_target_pairs={{4,0},{6,2},{8,4},{10,6},{12,8},{14,10},{5,1},{7,3},{9,5},{11,7},{... | collective-permute-start | bytes 3244040 | tf_op jit(solution)/shard_map/ppermute | solution.py:188
  10.3 32.3 %collective-permute-start.1 = (bf16[4,528,256]{2,1,0:T(8,128)(2,1)S(1)}, bf16[4,528,256]{2,1,0:T(8,128)(2,1)S(1)}, u32[]{:S(2)}, u32[]{:S(2)}) collective-permute-start(bf16[4,528,256]{2,1,0:T(8,128)(2,1)S(1)} %maximum_maximum_fusion.refs_0_), channel_id=1, source_target_pairs={{0,2},{2,0},{4,6},{6,4},{8,10},{10,8},{12,14},{14,12},{1,3},{3,1},... | collective-permute-start | bytes 3244040 | tf_op jit(solution)/shard_map/ppermute | solution.py:184
  15.5 1.0 copy-start.1
  16.5 0.7 copy-start.3
  17.2 0.7 copy-start.5
  17.8 26.4 %copy-start.4 = (s32[256]{0:T(256)S(1)}, s32[256]{0:T(256)}, u32[]{:S(2)}) copy-start(s32[256]{0:T(256)} %get-tuple-element.37.entry_ref) | copy-start | bytes 3076
  17.8 26.4 %copy-start.6 = (s32[8]{0:T(128)S(1)}, s32[8]{0:T(128)}, u32[]{:S(2)}) copy-start(s32[8]{0:T(128)} %get-tuple-element.36.count_ref) | copy-start | bytes 100
  23.1 1.0 copy-start.7
  24.2 1.0 copy-start.9
  31.0 26.0 %collective-permute-start.3 = (bf16[4,528,256]{2,1,0:T(8,128)(2,1)}, bf16[4,528,256]{2,1,0:T(8,128)(2,1)}, u32[]{:S(2)}, u32[]{:S(2)}) collective-permute-start(bf16[4,528,256]{2,1,0:T(8,128)(2,1)} %collective-permute-done.refs_1_), channel_id=1, source_target_pairs={{4,8},{6,10},{8,12},{10,14},{5,9},{7,11},{9,13},{11,15},{20,24},{2... | collective-permute-start | bytes 3244040 | tf_op jit(solution)/shard_map/ppermute | solution.py:188
  35.5 22.3 %collective-permute-start.5 = (bf16[4,528,256]{2,1,0:T(8,128)(2,1)}, bf16[4,528,256]{2,1,0:T(8,128)(2,1)}, u32[]{:S(2)}, u32[]{:S(2)}) collective-permute-start(bf16[4,528,256]{2,1,0:T(8,128)(2,1)} %collective-permute-done.refs_1_), channel_id=1, source_target_pairs={{8,10},{10,8},{12,14},{14,12},{9,11},{11,9},{13,15},{15,13},{24,26... | collective-permute-start | bytes 3244040 | tf_op jit(solution)/shard_map/ppermute | solution.py:184
  37.2 26.6 %collective-permute-start.4 = (bf16[4,528,256]{2,1,0:T(8,128)(2,1)}, bf16[4,528,256]{2,1,0:T(8,128)(2,1)}, u32[]{:S(2)}, u32[]{:S(2)}) collective-permute-start(bf16[4,528,256]{2,1,0:T(8,128)(2,1)} %collective-permute-done.2.refs_2_), channel_id=1, source_target_pairs={{4,0},{6,2},{8,4},{10,6},{5,1},{7,3},{9,5},{11,7},{20,16},{22,18},... | collective-permute-start | bytes 3244040 | tf_op jit(solution)/shard_map/ppermute | solution.py:188
  39.1 27.0 %collective-permute-start.6 = (bf16[4,528,256]{2,1,0:T(8,128)(2,1)}, bf16[4,528,256]{2,1,0:T(8,128)(2,1)}, u32[]{:S(2)}, u32[]{:S(2)}) collective-permute-start(bf16[4,528,256]{2,1,0:T(8,128)(2,1)} %collective-permute-done.2.refs_2_), channel_id=1, source_target_pairs={{0,2},{2,0},{4,6},{6,4},{1,3},{3,1},{5,7},{7,5},{16,18},{18,16},{2... | collective-permute-start | bytes 3244040 | tf_op jit(solution)/shard_map/ppermute | solution.py:184
  42.5 27.0 %collective-permute-start.7 = (bf16[4,528,256]{2,1,0:T(8,128)(2,1)S(1)}, bf16[4,528,256]{2,1,0:T(8,128)(2,1)}, u32[]{:S(2)}, u32[]{:S(2)}) collective-permute-start(bf16[4,528,256]{2,1,0:T(8,128)(2,1)S(1)} %collective-permute-done.1.refs_0_), channel_id=1, source_target_pairs={{0,4},{2,6},{12,8},{14,10},{1,5},{3,7},{13,9},{15,11},{16,20},{18,... | collective-permute-start | bytes 3244040 | tf_op jit(solution)/shard_map/ppermute | solution.py:225
  44.2 1.0 copy-start.2
  45.3 1.2 copy-start.8
  46.5 1.2 copy-start.10
  57.1 26.3 %collective-permute-start.11 = (bf16[4,528,256]{2,1,0:T(8,128)(2,1)}, bf16[4,528,256]{2,1,0:T(8,128)(2,1)S(1)}, u32[]{:S(2)}, u32[]{:S(2)}) collective-permute-start(bf16[4,528,256]{2,1,0:T(8,128)(2,1)} %collective-permute-done.3.refs_0_), channel_id=1, source_target_pairs={{8,12},{10,14},{9,13},{11,15},{24,28},{26,30},{25,29},{27,31}} | collective-permute-start | bytes 3244040 | tf_op jit(solution)/shard_map/ppermute | solution.py:188
  57.8 26.3 %collective-permute-start.13 = (bf16[4,528,256]{2,1,0:T(8,128)(2,1)}, bf16[4,528,256]{2,1,0:T(8,128)(2,1)S(1)}, u32[]{:S(2)}, u32[]{:S(2)}) collective-permute-start(bf16[4,528,256]{2,1,0:T(8,128)(2,1)} %collective-permute-done.3.refs_0_), channel_id=1, source_target_pairs={{8,10},{10,8},{12,14},{14,12},{9,11},{11,9},{13,15},{15,13},{24,26... | collective-permute-start | bytes 3244040 | tf_op jit(solution)/shard_map/ppermute | solution.py:184
  63.8 23.8 %collective-permute-start.12 = (bf16[4,528,256]{2,1,0:T(8,128)(2,1)}, bf16[4,528,256]{2,1,0:T(8,128)(2,1)S(1)}, u32[]{:S(2)}, u32[]{:S(2)}) collective-permute-start(bf16[4,528,256]{2,1,0:T(8,128)(2,1)} %collective-permute-done.4.refs_1_), channel_id=1, source_target_pairs={{4,0},{6,2},{5,1},{7,3},{20,16},{22,18},{21,17},{23,19}} | collective-permute-start | bytes 3244040 | tf_op jit(solution)/shard_map/ppermute | solution.py:188
  66.1 25.6 %collective-permute-start.14 = (bf16[4,528,256]{2,1,0:T(8,128)(2,1)}, bf16[4,528,256]{2,1,0:T(8,128)(2,1)S(1)}, u32[]{:S(2)}, u32[]{:S(2)}) collective-permute-start(bf16[4,528,256]{2,1,0:T(8,128)(2,1)} %collective-permute-done.4.refs_1_), channel_id=1, source_target_pairs={{0,2},{2,0},{4,6},{6,4},{1,3},{3,1},{5,7},{7,5},{16,18},{18,16},{2... | collective-permute-start | bytes 3244040 | tf_op jit(solution)/shard_map/ppermute | solution.py:184
  83.4 17.7 %collective-permute-start.15 = (bf16[2,528,256]{2,1,0:T(8,128)(2,1)S(1)}, bf16[2,528,256]{2,1,0:T(8,128)(2,1)S(1)}, u32[]{:S(2)}, u32[]{:S(2)}) collective-permute-start(bf16[2,528,256]{2,1,0:T(8,128)(2,1)S(1)} %slice.16), channel_id=1, source_target_pairs={{12,14},{14,12},{13,15},{15,13},{28,30},{30,28},{29,31},{31,29}} | collective-permute-start | bytes 1622024 | tf_op jit(solution)/shard_map/ppermute | solution.py:184
  84.2 17.0 %collective-permute-start.17 = (bf16[2,528,256]{2,1,0:T(8,128)(2,1)S(1)}, bf16[2,528,256]{2,1,0:T(8,128)(2,1)S(1)}, u32[]{:S(2)}, u32[]{:S(2)}) collective-permute-start(bf16[2,528,256]{2,1,0:T(8,128)(2,1)S(1)} %slice.18), channel_id=1, source_target_pairs={{8,12},{10,14},{9,13},{11,15},{24,28},{26,30},{25,29},{27,31}} | collective-permute-start | bytes 1622024 | tf_op jit(solution)/shard_map/ppermute | solution.py:188
  87.7 13.4 %collective-permute-start.16 = (bf16[2,528,256]{2,1,0:T(8,128)(2,1)S(1)}, bf16[2,528,256]{2,1,0:T(8,128)(2,1)S(1)}, u32[]{:S(2)}, u32[]{:S(2)}) collective-permute-start(bf16[2,528,256]{2,1,0:T(8,128)(2,1)S(1)} %slice.17), channel_id=1, source_target_pairs={{0,2},{2,0},{1,3},{3,1},{16,18},{18,16},{17,19},{19,17}} | collective-permute-start | bytes 1622024 | tf_op jit(solution)/shard_map/ppermute | solution.py:184
  91.8 12.2 %collective-permute-start.18 = (bf16[2,528,256]{2,1,0:T(8,128)(2,1)S(1)}, bf16[2,528,256]{2,1,0:T(8,128)(2,1)S(1)}, u32[]{:S(2)}, u32[]{:S(2)}) collective-permute-start(bf16[2,528,256]{2,1,0:T(8,128)(2,1)S(1)} %slice.19), channel_id=1, source_target_pairs={{4,0},{6,2},{5,1},{7,3},{20,16},{22,18},{21,17},{23,19}} | collective-permute-start | bytes 1622024 | tf_op jit(solution)/shard_map/ppermute | solution.py:188
  105.9 3.4 %collective-permute-start.19 = (bf16[2,256,256]{2,1,0:T(8,128)(2,1)S(1)}, bf16[2,256,256]{2,1,0:T(8,128)(2,1)S(1)}, u32[]{:S(2)}, u32[]{:S(2)}) collective-permute-start(bf16[2,256,256]{2,1,0:T(8,128)(2,1)S(1)} %get-tuple-element.57), channel_id=1, source_target_pairs={{12,8},{14,10},{13,9},{15,11},{28,24},{30,26},{29,25},{31,27}} | collective-permute-start | bytes 786440 | tf_op jit(solution)/shard_map/ppermute | solution.py:188
  106.6 3.5 %collective-permute-start.21 = (bf16[2,256,256]{2,1,0:T(8,128)(2,1)S(1)}, bf16[2,256,256]{2,1,0:T(8,128)(2,1)S(1)}, u32[]{:S(2)}, u32[]{:S(2)}) collective-permute-start(bf16[2,256,256]{2,1,0:T(8,128)(2,1)S(1)} %get-tuple-element.59), channel_id=1, source_target_pairs={{12,14},{14,12},{13,15},{15,13},{28,30},{30,28},{29,31},{31,29}} | collective-permute-start | bytes 786440 | tf_op jit(solution)/shard_map/ppermute | solution.py:184
  107.3 11.7 %collective-permute-start.26 = (bf16[2,256,256]{2,1,0:T(8,128)(2,1)S(1)}, bf16[2,256,256]{2,1,0:T(8,128)(2,1)S(1)}, u32[]{:S(2)}, u32[]{:S(2)}) collective-permute-start(bf16[2,256,256]{2,1,0:T(8,128)(2,1)S(1)} %get-tuple-element.64), channel_id=1, source_target_pairs={{0,4},{2,6},{1,5},{3,7},{16,20},{18,22},{17,21},{19,23}} | collective-permute-start | bytes 786440 | tf_op jit(solution)/shard_map/ppermute | solution.py:188
  108.6 12.4 %collective-permute-start.28 = (bf16[2,256,256]{2,1,0:T(8,128)(2,1)S(1)}, bf16[2,256,256]{2,1,0:T(8,128)(2,1)S(1)}, u32[]{:S(2)}, u32[]{:S(2)}) collective-permute-start(bf16[2,256,256]{2,1,0:T(8,128)(2,1)S(1)} %get-tuple-element.66), channel_id=1, source_target_pairs={{0,2},{2,0},{1,3},{3,1},{16,18},{18,16},{17,19},{19,17}} | collective-permute-start | bytes 786440 | tf_op jit(solution)/shard_map/ppermute | solution.py:184
  109.4 19.8 %collective-permute-start.20 = (bf16[4,256,256]{2,1,0:T(8,128)(2,1)S(1)}, bf16[4,256,256]{2,1,0:T(8,128)(2,1)S(1)}, u32[]{:S(2)}, u32[]{:S(2)}) collective-permute-start(bf16[4,256,256]{2,1,0:T(8,128)(2,1)S(1)} %add_convert_fusion.8), channel_id=1, source_target_pairs={{8,10},{10,8},{12,14},{14,12},{9,11},{11,9},{13,15},{15,13},{24,26... | collective-permute-start | bytes 1572872 | tf_op jit(solution)/shard_map/ppermute | solution.py:184
  110.1 19.7 %collective-permute-start.22 = (bf16[4,256,256]{2,1,0:T(8,128)(2,1)S(1)}, bf16[4,256,256]{2,1,0:T(8,128)(2,1)S(1)}, u32[]{:S(2)}, u32[]{:S(2)}) collective-permute-start(bf16[4,256,256]{2,1,0:T(8,128)(2,1)S(1)} %add_convert_fusion.7), channel_id=1, source_target_pairs={{12,8},{14,10},{13,9},{15,11},{28,24},{30,26},{29,25},{31,27}} | collective-permute-start | bytes 1572872 | tf_op jit(solution)/shard_map/ppermute | solution.py:188
  119.0 14.5 %collective-permute-start.27 = (bf16[4,256,256]{2,1,0:T(8,128)(2,1)S(1)}, bf16[4,256,256]{2,1,0:T(8,128)(2,1)S(1)}, u32[]{:S(2)}, u32[]{:S(2)}) collective-permute-start(bf16[4,256,256]{2,1,0:T(8,128)(2,1)S(1)} %add_convert_fusion.4), channel_id=1, source_target_pairs={{0,2},{2,0},{4,6},{6,4},{1,3},{3,1},{5,7},{7,5},{16,18},{18,16},{2... | collective-permute-start | bytes 1572872 | tf_op jit(solution)/shard_map/ppermute | solution.py:184
  121.0 15.5 %collective-permute-start.29 = (bf16[4,256,256]{2,1,0:T(8,128)(2,1)S(1)}, bf16[4,256,256]{2,1,0:T(8,128)(2,1)S(1)}, u32[]{:S(2)}, u32[]{:S(2)}) collective-permute-start(bf16[4,256,256]{2,1,0:T(8,128)(2,1)S(1)} %add_convert_fusion.3), channel_id=1, source_target_pairs={{0,4},{2,6},{1,5},{3,7},{16,20},{18,22},{17,21},{19,23}} | collective-permute-start | bytes 1572872 | tf_op jit(solution)/shard_map/ppermute | solution.py:188
  122.3 17.2 %collective-permute-start.8 = (bf16[4,256,256]{2,1,0:T(8,128)(2,1)S(1)}, bf16[4,256,256]{2,1,0:T(8,128)(2,1)S(1)}, u32[]{:S(2)}, u32[]{:S(2)}) collective-permute-start(bf16[4,256,256]{2,1,0:T(8,128)(2,1)S(1)} %get-tuple-element.48), channel_id=1, source_target_pairs={{4,0},{6,2},{8,12},{10,14},{5,1},{7,3},{9,13},{11,15},{20,16},{22,... | collective-permute-start | bytes 1572872 | tf_op jit(solution)/shard_map/ppermute | solution.py:270
  129.1 11.2 %collective-permute-start.10 = (bf16[4,256,256]{2,1,0:T(8,128)(2,1)S(1)}, bf16[4,256,256]{2,1,0:T(8,128)(2,1)S(1)}, u32[]{:S(2)}, u32[]{:S(2)}) collective-permute-start(bf16[4,256,256]{2,1,0:T(8,128)(2,1)S(1)} %get-tuple-element.50), channel_id=1, source_target_pairs={{8,10},{10,8},{12,14},{14,12},{9,11},{11,9},{13,15},{15,13},{24,26... | collective-permute-start | bytes 1572872 | tf_op jit(solution)/shard_map/ppermute | solution.py:184
  129.9 19.2 %collective-permute-start.25 = (bf16[4,256,256]{2,1,0:T(8,128)(2,1)S(1)}, bf16[4,256,256]{2,1,0:T(8,128)(2,1)S(1)}, u32[]{:S(2)}, u32[]{:S(2)}) collective-permute-start(bf16[4,256,256]{2,1,0:T(8,128)(2,1)S(1)} %get-tuple-element.61), channel_id=1, source_target_pairs={{0,2},{2,0},{4,6},{6,4},{1,3},{3,1},{5,7},{7,5},{16,18},{18,16},{2... | collective-permute-start | bytes 1572872 | tf_op jit(solution)/shard_map/ppermute | solution.py:184
  133.5 13.4 %collective-permute-start.23 = (bf16[4,256,256]{2,1,0:T(8,128)(2,1)S(1)}, bf16[4,256,256]{2,1,0:T(8,128)(2,1)S(1)}, u32[]{:S(2)}, u32[]{:S(2)}) collective-permute-start(bf16[4,256,256]{2,1,0:T(8,128)(2,1)S(1)} %add_convert_fusion.6), channel_id=1, source_target_pairs={{8,4},{10,6},{12,8},{14,10},{9,5},{11,7},{13,9},{15,11},{24,20},{2... | collective-permute-start | bytes 1572872 | tf_op jit(solution)/shard_map/ppermute | solution.py:188
  136.7 14.1 %collective-permute-start.30 = (bf16[4,256,256]{2,1,0:T(8,128)(2,1)S(1)}, bf16[4,256,256]{2,1,0:T(8,128)(2,1)S(1)}, u32[]{:S(2)}, u32[]{:S(2)}) collective-permute-start(bf16[4,256,256]{2,1,0:T(8,128)(2,1)S(1)} %add_convert_fusion.2), channel_id=1, source_target_pairs={{0,4},{2,6},{4,8},{6,10},{1,5},{3,7},{5,9},{7,11},{16,20},{18,22},... | collective-permute-start | bytes 1572872 | tf_op jit(solution)/shard_map/ppermute | solution.py:188
  139.7 15.4 %collective-permute-start.9 = (bf16[4,256,256]{2,1,0:T(8,128)(2,1)S(1)}, bf16[4,256,256]{2,1,0:T(8,128)(2,1)S(1)}, u32[]{:S(2)}, u32[]{:S(2)}) collective-permute-start(bf16[4,256,256]{2,1,0:T(8,128)(2,1)S(1)} %add_convert_fusion.9), channel_id=1, source_target_pairs={{0,2},{2,0},{4,6},{6,4},{8,10},{10,8},{12,14},{14,12},{1,3},{3,1},... | collective-permute-start | bytes 1572872 | tf_op jit(solution)/shard_map/ppermute | solution.py:184
  147.1 11.1 %collective-permute-start.24 = (bf16[4,256,256]{2,1,0:T(8,128)(2,1)S(1)}, bf16[4,256,256]{2,1,0:T(8,128)(2,1)S(1)}, u32[]{:S(2)}, u32[]{:S(2)}) collective-permute-start(bf16[4,256,256]{2,1,0:T(8,128)(2,1)S(1)} %add_convert_fusion.5), channel_id=1, source_target_pairs={{4,0},{6,2},{8,4},{10,6},{12,8},{14,10},{5,1},{7,3},{9,5},{11,7},{... | collective-permute-start | bytes 1572872 | tf_op jit(solution)/shard_map/ppermute | solution.py:188
  151.0 11.1 %collective-permute-start.31 = (bf16[4,256,256]{2,1,0:T(8,128)(2,1)S(1)}, bf16[4,256,256]{2,1,0:T(8,128)(2,1)S(1)}, u32[]{:S(2)}, u32[]{:S(2)}) collective-permute-start(bf16[4,256,256]{2,1,0:T(8,128)(2,1)S(1)} %add_convert_fusion.1), channel_id=1, source_target_pairs={{0,4},{2,6},{4,8},{6,10},{8,12},{10,14},{1,5},{3,7},{5,9},{7,11},{... | collective-permute-start | bytes 1572872 | tf_op jit(solution)/shard_map/ppermute | solution.py:188
